TPU v7x, 512 devices: a whole 4x4x16 slice. The times are simulated.
512 devices in a mesh: rows: 16 (over y, z_hi), lat: 32 (over x, z_lo, core).
Axes of the slice: x: 4, y: 4, z: 16 (z_hi: 4, z_lo: 4; z = z_hi * 4 + z_lo), core: 2. Of those that a mesh axis runs over, the one named last changes fastest.
Arguments:
- activations: bfloat16 [65536, 3584], P(('rows', 'lat')), may hold values from -6 to 6
- block_ids: int32 [65536, 2], P(('rows', 'lat')), may hold values from 0 to 31, all different within a row; in each aligned block of 128 rows (0 to 127, 128 to 255, ...) at most 12 rows name the same one
- enc_weight: bfloat16 [3584, 4096], P(None, 'lat'), may hold values from -0.09375 to 0.09375
- enc_bias: float32 [4096], P('lat'), may hold values from -3 to 3
- dec_weight: bfloat16 [4096, 3584], P('lat'), may hold values from -0.375 to 0.375
- dec_bias: float32 [3584], replicated, may hold values from -3 to 3
Outputs:
- enc_grad: float32 [3584, 4096], P('rows', 'lat')
- dec_grad: float32 [4096, 3584], P('lat', 'rows')
- bias_grad: float32 [4096], P(('lat', 'rows'))
Inputs may be any that keep to these rules, and one draw needn't show every extreme that they name: `block_ids`: each row names 2 different latent blocks. Among the 128 rows of one device (aligned blocks of 128 rows) no latent block is named by more than 12 rows, and on some device one block is named by exactly 12 rows.
All inputs are finite; a program needn't handle non-finite values.
Results may differ from a plain program's by a relative error of at most 0.0033.
Values may be sent and summed in bfloat16 or wider, within the bound.
No kernel may reach another device: no remote copies, remote signals or barrier semaphores. Data moves between devices by JAX's collectives and lax.ppermute only.
A program may use at most 64 MiB of HBM per device.

v0:
```python
import jax
import jax.numpy as jnp
from jax import lax
from jax.sharding import PartitionSpec as P


def contract_rows(left, right):
    return lax.dot_general(
        left, right, (((0,), (0,)), ((), ())), preferred_element_type=jnp.float32
    )


def swish_grad(grad_in, pre_act):
    gate_sig = jax.nn.sigmoid(pre_act)
    return grad_in * gate_sig * (1.0 + pre_act * (1.0 - gate_sig))


def local(activations, block_ids, enc_weight, enc_bias, dec_weight, dec_bias):
    lat_count = lax.axis_size("lat")
    rows_dev, active = block_ids.shape
    width = activations.shape[1]
    latents = enc_weight.shape[1]
    capacity = 3 * active * rows_dev // (2 * lat_count)
    slots = lat_count * capacity
    flat_ids = block_ids.reshape(-1)
    one_hot = (flat_ids[:, None] == jnp.arange(lat_count, dtype=jnp.int32)[None, :]).astype(
        jnp.int32
    )
    earlier = jnp.cumsum(one_hot, axis=0) - one_hot
    position = jnp.sum(earlier * one_hot, axis=1)
    slot_ids = flat_ids * capacity + position
    pair_row = jnp.arange(rows_dev * active, dtype=jnp.int32) // active
    sources = jnp.full((slots,), rows_dev, jnp.int32).at[slot_ids].set(pair_row)
    padded = jnp.concatenate([activations, jnp.zeros((1, width), activations.dtype)], axis=0)
    outgoing = padded[sources].reshape(lat_count, capacity, width)
    received = lax.all_to_all(outgoing, "lat", split_axis=0, concat_axis=0, tiled=True)
    pre_act = (
        jnp.einsum("scd,dl->scl", received, enc_weight, preferred_element_type=jnp.float32)
        + enc_bias
    )
    latent_codes = (pre_act * jax.nn.sigmoid(pre_act)).astype(jnp.bfloat16)
    decoded = jnp.einsum(
        "scl,ld->scd", latent_codes, dec_weight, preferred_element_type=jnp.float32
    ).astype(jnp.bfloat16)
    returned = lax.all_to_all(decoded, "lat", split_axis=0, concat_axis=0, tiled=True)
    returned, kept_rows, pre_act, latent_codes = (returned, received, pre_act, latent_codes)
    back_rows = returned.reshape(slots, width)
    own_parts = back_rows[slot_ids].reshape(rows_dev, active, width).astype(jnp.float32)
    rebuilt = dec_bias + jnp.sum(own_parts, axis=1)
    errors = ((rebuilt - activations.astype(jnp.float32)) / 64.0).astype(jnp.bfloat16)
    err_pad = jnp.concatenate([errors, jnp.zeros((1, width), errors.dtype)], axis=0)
    err_out = err_pad[sources].reshape(lat_count, capacity, width)
    err_in = lax.all_to_all(err_out, "lat", split_axis=0, concat_axis=0, tiled=True)
    slot_rows = kept_rows.reshape(slots, width)
    slot_errs = err_in.reshape(slots, width)
    code_rows = latent_codes.reshape(slots, latents)
    pre_rows = pre_act.reshape(slots, latents)
    dec_part = contract_rows(slot_errs, code_rows)
    code_grad = lax.dot_general(
        slot_errs, dec_weight, (((1,), (1,)), ((), ())), preferred_element_type=jnp.float32
    )
    grad_rows = swish_grad(code_grad, pre_rows).astype(jnp.bfloat16)
    enc_part = contract_rows(slot_rows, grad_rows)
    bias_part = jnp.sum(grad_rows.astype(jnp.float32), axis=0)
    enc_grad, dec_summed, bias_grad = (
        lax.psum_scatter(enc_part, "rows", scatter_dimension=0, tiled=True),
        lax.psum_scatter(dec_part, "rows", scatter_dimension=0, tiled=True),
        lax.psum_scatter(bias_part, "rows", scatter_dimension=0, tiled=True),
    )
    dec_grad = dec_summed.T
    return (enc_grad, dec_grad, bias_grad)


def solution(mesh):
    in_specs = (
        P(("rows", "lat"), None),
        P(("rows", "lat"), None),
        P(None, "lat"),
        P("lat"),
        P("lat", None),
        P(),
    )
    out_specs = (P("rows", "lat"), P("lat", "rows"), P(("lat", "rows")))
    return jax.shard_map(local, mesh=mesh, in_specs=in_specs, out_specs=out_specs, check_vma=False)
```

profile of v0, /device:TPU:1, one launch (start us, length us, event | category | flops | bytes accessed | tf_op | source)
XLA Modules:
  0.0 592.4 jit_solution(8226857079439162562)
XLA Ops:
  12.9 3.9 gather_fusion
  16.8 5.3 reshape.77
  22.1 95.1 %all_to_all.15 = bf16[32,12,3584]{2,1,0:T(8,128)(2,1)S(1)} all-to-all(bf16[32,12,3584]{2,1,0:T(8,128)(2,1)} %reshape.77), channel_id=1, replica_groups=mesh['rows'=16,'lat'=32] {'lat'}, dimensions={0} | all-to-all | bytes 5505024 | tf_op jit(solution)/shard_map/all_to_all | solution.py:36
  117.2 1.8 copy-done.2
  119.0 1.9 fusion.3
  121.8 3.5 copy.24
  125.2 4.8 all-to-all-start.1
  130.1 83.1 %all-to-all-done.1 = bf16[32,12,3584]{2,1,0:T(8,128)(2,1)} async-done(((bf16[32,12,3584]{2,1,0:T(8,128)(2,1)}), bf16[32,12,3584]{2,1,0:T(8,128)(2,1)}, u32[]{:S(2)}, u32[]{:S(2)}) %all-to-all-start.1) | async-done | bytes 2752544 | tf_op jit(solution)/shard_map/all_to_all | solution.py:45
  213.1 5.4 reshape.79
  218.5 5.7 gather_fusion.1
  224.2 3.6 reshape.83
  227.8 6.4 %reduce_sum.31 = f32[128,3584]{1,0:T(8,128)S(1)} reduce(f32[128,2,3584]{2,1,0:T(2,128)} %reshape.83, f32[]{:T(128)} %constant.39.clone.1), dimensions={1}, to_apply=%region_4.5 | reduce | flops 458752 | bytes 5505028 | tf_op jit(solution)/shard_map/reduce_sum | solution.py:49
  235.7 3.9 gather_fusion.2
  239.6 5.4 reshape.80
  245.0 5.7 all-to-all-start.2
  251.0 5.4 reshape.78
  256.4 77.5 %all-to-all-done.2 = bf16[32,12,3584]{2,1,0:T(8,128)(2,1)} async-done(((bf16[32,12,3584]{2,1,0:T(8,128)(2,1)}), bf16[32,12,3584]{2,1,0:T(8,128)(2,1)}, u32[]{:S(2)}, u32[]{:S(2)}) %all-to-all-start.2) | async-done | bytes 2752544 | tf_op jit(solution)/shard_map/all_to_all | solution.py:53
  334.0 5.3 reshape.81
  339.3 2.8 convert_reduce_fusion
  342.1 2.2 fusion.16
  344.4 5.1 convolution_bitcast_fusion
  351.4 49.6 %all-reduce.2 = f32[128]{0:T(128)S(1)} all-reduce(f32[128]{0:T(128)S(1)} %get-tuple-element.3), channel_id=4, replica_groups=mesh['rows'=16,'lat'=32] {'rows'}, use_global_device_ids=true, to_apply=%region_8.9.clone | all-reduce | flops 128 | bytes 1024
  401.6 65.9 %reduce-scatter.3.cloned.1.call-done = f32[224,128]{1,0:T(8,128)} async-done(((f32[3584,128]{1,0:T(8,128)}), f32[224,128]{1,0:T(8,128)}) %reduce-scatter.3.cloned.1.call-update) | async-done | bytes 114704 | tf_op jit(solution)/shard_map/reduce_scatter | solution.py:66
  467.5 118.1 %reduce-scatter.5.cloned.1.call-done = f32[224,128]{1,0:T(8,128)} async-done(((f32[3584,128]{1,0:T(8,128)}), f32[224,128]{1,0:T(8,128)}) %reduce-scatter.5.cloned.1.call-update) | async-done | bytes 114704 | tf_op jit(solution)/shard_map/reduce_scatter | solution.py:67
  (41 shorter events, 10.4 us)
Async XLA Ops:
  7.2 113.7 %copy-start = (bf16[128,3584]{1,0:T(8,128)(2,1)S(1)}, bf16[128,3584]{1,0:T(8,128)(2,1)}, u32[]{:S(2)}) copy-start(bf16[128,3584]{1,0:T(8,128)(2,1)} %param.10) | copy-start | bytes 2752516
  22.1 96.9 %copy-start.4 = (bf16[3584,128]{1,0:T(8,128)(2,1)S(1)}, bf16[3584,128]{1,0:T(8,128)(2,1)}, u32[]{:S(2)}) copy-start(bf16[3584,128]{1,0:T(8,128)(2,1)} %param.8) | copy-start | bytes 2752516
  22.1 96.9 %copy-start.5 = (f32[128]{0:T(128)S(1)}, f32[128]{0:T(128)}, u32[]{:S(2)}) copy-start(f32[128]{0:T(128)} %param.9) | copy-start | bytes 1540
  117.2 1.8 copy-start.2
  125.2 87.9 %all-to-all-start.1 = ((bf16[32,12,3584]{2,1,0:T(8,128)(2,1)}), bf16[32,12,3584]{2,1,0:T(8,128)(2,1)}, u32[]{:S(2)}, u32[]{:S(2)}) async-start(bf16[32,12,3584]{2,1,0:T(8,128)(2,1)} %copy.24), calls=%async_computation.1 | async-start | bytes 7340032 | tf_op jit(solution)/shard_map/all_to_all | solution.py:45
  227.8 6.4 %copy-start.3 = (f32[3584]{0:T(1024)S(1)}, f32[3584]{0:T(1024)}, u32[]{:S(2)}) copy-start(f32[3584]{0:T(1024)} %param.11) | copy-start | bytes 43012
  245.0 89.0 %all-to-all-start.2 = ((bf16[32,12,3584]{2,1,0:T(8,128)(2,1)}), bf16[32,12,3584]{2,1,0:T(8,128)(2,1)}, u32[]{:S(2)}, u32[]{:S(2)}) async-start(bf16[32,12,3584]{2,1,0:T(8,128)(2,1)} %reshape.80), calls=%async_computation.2 | async-start | bytes 7340032 | tf_op jit(solution)/shard_map/all_to_all | solution.py:53
  250.6 216.8 %reduce-scatter.3.cloned.1.call-start = ((), (), s32[]{:S(2)}) async-start(), calls=%async_computation.5 | async-start | bytes 1949696 | tf_op jit(solution)/shard_map/reduce_scatter | solution.py:66
  339.3 2.8 copy-start.1
  344.4 241.2 %reduce-scatter.5.cloned.1.call-start = ((), (), s32[]{:S(2)}) async-start(), calls=%async_computation.6 | async-start | bytes 1949696 | tf_op jit(solution)/shard_map/reduce_scatter | solution.py:67
Sparse Core Ops, SparseCore 0:
  344.5 122.9 reduce-scatter.2
  472.1 113.3 reduce-scatter.4
where the time goes:
time: 594 us; the launch traced here: 592 us
  waiting for transfers between devices  345 us (58%)
  blocking collectives  145 us (24%)
  local copies, waits for them, and re-layouts  55.3 us (9%)
  between operations  14.9 us (3%)
  matrix products  12.9 us (2%)
  starting transfers between devices  10.8 us (2%)
  other arithmetic  9.38 us (2%)
    reduce_scatter x1, waiting for transfers between devices, local(): lax.psum_scatter(dec_part, 'rows', scatter_dimension=0, tiled=True)  118 us
    all_to_all x1, blocking collectives, local(): lax.all_to_all(outgoing, 'lat', split_axis=0, concat_axis=0, tiled=True)  95.1 us
    all_to_all x1, waiting for transfers between devices, local(): lax.all_to_all(decoded, 'lat', split_axis=0, concat_axis=0, tiled=True)  83.1 us
    all_to_all x1, waiting for transfers between devices, local(): lax.all_to_all(err_out, 'lat', split_axis=0, concat_axis=0, tiled=True)  77.5 us
    reduce_scatter x1, waiting for transfers between devices, local(): lax.psum_scatter(enc_part, 'rows', scatter_dimension=0, tiled=True)  65.9 us
    unnamed x1, blocking collectives  49.6 us
  transfers between devices with their start and end apart: 4, of which 4 were waited for; matrix products, arithmetic and copies ran while one was open for 2% of the time, Pallas kernels for 0%

commit v1 on v0

v1 whole, which is shorter than its diff:
```python
import functools

import jax
import jax.numpy as jnp
from jax import lax
from jax.experimental import pallas as pl
from jax.experimental.pallas import tpu as pltpu
from jax.sharding import PartitionSpec as P

CAP = 12
PAIR = 2 * CAP
BF = jnp.bfloat16
F32 = jnp.float32
VMEM = 56 * 1024 * 1024


def place_of(rows, first):
    row = lax.broadcasted_iota(jnp.int32, (rows, 1), 0) + first
    block = lax.shift_right_logical(row * 2731, 16)
    return block, row - block * PAIR


def left_rows(rows):
    _, place = place_of(rows, 0)
    return place < CAP


def dot(a, b):
    return lax.dot_general(a, b, (((1,), (0,)), ((), ())), preferred_element_type=F32)


def dot_t(a, b):
    return lax.dot_general(a, b, (((0,), (0,)), ((), ())), preferred_element_type=F32)


def dot_nt(a, b):
    return lax.dot_general(a, b, (((1,), (1,)), ((), ())), preferred_element_type=F32)


def split_halves(x, left):
    zero = jnp.zeros_like(x)
    return jnp.concatenate([jnp.where(left, x, zero), jnp.where(left, zero, x)], axis=1)


def join_halves(y, left):
    rows, n = y.shape[0], y.shape[1] // 2
    yl, yr = y[:, :n], y[:, n:]
    after = pltpu.roll(yr, rows - CAP, 0)
    before = pltpu.roll(yl, CAP, 0)
    return jnp.where(left, yl + after, yr + before)


def one_hot_slots(ids, blocks, first, rows):
    n = ids.shape[1]
    number = lax.broadcasted_iota(jnp.int32, (blocks, n), 0)
    member = (number == ids[0:1, :]) | (number == ids[1:2, :])
    earlier = (
        lax.broadcasted_iota(jnp.int32, (n, n), 0) < lax.broadcasted_iota(jnp.int32, (n, n), 1)
    )
    position = dot(member.astype(F32).astype(BF), earlier.astype(F32).astype(BF))
    code = jnp.where(member, position, 200.0).astype(BF)
    block, place = place_of(rows, first)
    left = place < CAP
    slot = (place - jnp.where(left, 0, CAP)).astype(F32)
    expand = lax.broadcasted_iota(jnp.int32, (rows, blocks), 1) == block
    spread = dot(expand.astype(F32).astype(BF), code)
    hit = (spread == slot).astype(F32)
    return split_halves(hit, left).astype(BF)


def pack_kernel(blocks, step, ids_ref, act_ref, out_ref, act2):
    rows = out_ref.shape[0]
    half = act_ref.shape[1] // 2
    n = act_ref.shape[0]

    @pl.when(pl.program_id(0) == 0)
    def _():
        act2[:n, :] = act_ref[:, :half]
        act2[n:, :] = act_ref[:, half:]

    sel = one_hot_slots(ids_ref[...], blocks, pl.program_id(0) * rows, rows)
    for c in range(0, half, step):
        out_ref[:, c : c + step] = dot(sel, act2[:, c : c + step]).astype(BF)


def pack(ids, act, blocks):
    n, width = act.shape
    half = width // 2
    total = blocks * PAIR
    rows = total // 4
    return pl.pallas_call(
        functools.partial(pack_kernel, blocks, 256),
        grid=(total // rows,),
        in_specs=[
            pl.BlockSpec(ids.shape, lambda i: (0, 0)),
            pl.BlockSpec(act.shape, lambda i: (0, 0)),
        ],
        out_specs=pl.BlockSpec((rows, half), lambda i: (i, 0)),
        out_shape=jax.ShapeDtypeStruct((total, half), BF),
        scratch_shapes=[pltpu.VMEM((2 * n, half), BF)],
        compiler_params=pltpu.CompilerParams(vmem_limit_bytes=VMEM),
        name="pack_rows",
    )(ids, act)


def code_kernel(step, x_ref, enc_ref, bias_ref, dec_ref, out_ref, pre_ref, enc2, dec2):
    rows, half = x_ref.shape
    n = enc_ref.shape[1]

    @pl.when(pl.program_id(0) == 0)
    def _():
        enc2[:, :n] = enc_ref[:half, :]
        enc2[:, n:] = enc_ref[half:, :]
        dec2[:n, :] = dec_ref[:, :half]
        dec2[n:, :] = dec_ref[:, half:]

    left = left_rows(rows)
    pre = join_halves(dot(x_ref[...], enc2[...]), left) + bias_ref[...]
    pre_ref[...] = pre
    codes = split_halves(pre * jax.nn.sigmoid(pre), left).astype(BF)
    for c in range(0, half, step):
        out_ref[:, c : c + step] = dot(codes, dec2[:, c : c + step]).astype(BF)


def encode_decode(x, enc, bias, dec):
    total, half = x.shape
    n = enc.shape[1]
    rows = total // 4
    return pl.pallas_call(
        functools.partial(code_kernel, 256),
        grid=(total // rows,),
        in_specs=[
            pl.BlockSpec((rows, half), lambda i: (i, 0)),
            pl.BlockSpec(enc.shape, lambda i: (0, 0)),
            pl.BlockSpec((1, n), lambda i: (0, 0)),
            pl.BlockSpec(dec.shape, lambda i: (0, 0)),
        ],
        out_specs=[
            pl.BlockSpec((rows, half), lambda i: (i, 0)),
            pl.BlockSpec((rows, n), lambda i: (i, 0)),
        ],
        out_shape=[
            jax.ShapeDtypeStruct((total, half), BF),
            jax.ShapeDtypeStruct((total, n), F32),
        ],
        scratch_shapes=[pltpu.VMEM((half, 2 * n), BF), pltpu.VMEM((2 * n, half), BF)],
        compiler_params=pltpu.CompilerParams(vmem_limit_bytes=VMEM),
        name="encode_decode",
    )(x, enc, bias, dec)


def error_kernel(blocks, ids_ref, parts_ref, al_ref, ar_ref, bl_ref, br_ref, out_ref, sel):
    total = parts_ref.shape[0]
    n = al_ref.shape[0]

    @pl.when(pl.program_id(0) == 0)
    def _():
        sel[...] = one_hot_slots(ids_ref[...], blocks, 0, total)

    sums = dot_t(sel[...], parts_ref[...])
    err_l = (sums[:n] + bl_ref[...] - al_ref[...].astype(F32)) * (1.0 / 64.0)
    err_r = (sums[n:] + br_ref[...] - ar_ref[...].astype(F32)) * (1.0 / 64.0)
    errors = jnp.concatenate([err_l.astype(BF), err_r.astype(BF)], axis=0)
    out_ref[...] = dot(sel[...], errors).astype(BF)


def error_rows(ids, parts, act, bias, blocks):
    total, half = parts.shape
    n = act.shape[0]
    step = 256
    steps = half // step
    return pl.pallas_call(
        functools.partial(error_kernel, blocks),
        grid=(steps,),
        in_specs=[
            pl.BlockSpec(ids.shape, lambda i: (0, 0)),
            pl.BlockSpec((total, step), lambda i: (0, i)),
            pl.BlockSpec((n, step), lambda i: (0, i)),
            pl.BlockSpec((n, step), lambda i: (0, i + steps)),
            pl.BlockSpec((1, step), lambda i: (0, i)),
            pl.BlockSpec((1, step), lambda i: (0, i + steps)),
        ],
        out_specs=pl.BlockSpec((total, step), lambda i: (0, i)),
        out_shape=jax.ShapeDtypeStruct((total, half), BF),
        scratch_shapes=[pltpu.VMEM((total, 2 * n), BF)],
        compiler_params=pltpu.CompilerParams(vmem_limit_bytes=VMEM),
        name="error_rows",
    )(ids, parts, act, act, bias, bias)


def hi_lo(x):
    hi = x.astype(BF).astype(F32)
    row = lax.broadcasted_iota(jnp.int32, (16, x.shape[1]), 0)
    return jnp.where(row == 0, hi, jnp.where(row == 1, x - hi, 0.0)).astype(BF)


def grad_kernel(x_ref, e_ref, pre_ref, dec_ref, out_ref, dec2):
    rows, half = x_ref.shape
    n = pre_ref.shape[1]
    groups, _, quarter = out_ref.shape
    dec2[:n, :] = dec_ref[:, :half]
    dec2[n:, :] = dec_ref[:, half:]
    left = left_rows(rows)
    pre = pre_ref[...]
    sig = jax.nn.sigmoid(pre)
    codes = split_halves(pre * sig, left).astype(BF)
    code_grad = join_halves(dot_nt(e_ref[...], dec2[...]), left)
    grad = (code_grad * sig * (1.0 + pre * (1.0 - sig))).astype(BF).astype(F32)
    grads = split_halves(grad, left)
    bias = jnp.sum(grads[:, :n], axis=0, keepdims=True)
    grads = grads.astype(BF)
    for g in range(0, groups // 2):
        cols = pl.ds(g * quarter, quarter)
        enc = dot_t(grads, x_ref[:, cols]).astype(BF)
        dec = dot_t(codes, e_ref[:, cols]).astype(BF)
        for s in range(2):
            out_ref[g + s * (groups // 2), :n, :] = enc[s * n : s * n + n]
            out_ref[g + s * (groups // 2), n : 2 * n, :] = dec[s * n : s * n + n]
    for g in range(groups):
        shifted = pltpu.roll(bias, (n - g * (n // groups)) % n, 1)
        out_ref[g, 2 * n :, :] = jnp.zeros((16, quarter), BF)
        out_ref[g, 2 * n :, :n] = hi_lo(shifted)


def gradients(x, err, pre, dec, groups):
    n, width = dec.shape
    return pl.pallas_call(
        grad_kernel,
        out_shape=jax.ShapeDtypeStruct((groups, 2 * n + 16, width // groups), BF),
        scratch_shapes=[pltpu.VMEM((2 * n, width // 2), BF)],
        compiler_params=pltpu.CompilerParams(vmem_limit_bytes=VMEM),
        name="gradients",
    )(x, err, pre, dec)


def first_sum_kernel(parts_ref, out_ref):
    groups, rows, quarter = parts_ref.shape
    n = (rows - 16) // 2
    chunks, out_rows, _ = out_ref.shape
    piece = out_rows - 16
    total = parts_ref[0, : 2 * n, :].astype(F32)
    bias = parts_ref[0, 2 * n :, :n].astype(F32)
    for g in range(1, groups):
        total = total + parts_ref[g, : 2 * n, :].astype(F32)
        bias = bias + parts_ref[g, 2 * n :, :n].astype(F32)
    turned = total.T.astype(BF)
    bias = jnp.sum(bias, axis=0, keepdims=True)
    for c in range(chunks):
        out_ref[c, :piece, :] = turned[c * piece : (c + 1) * piece]
        shifted = pltpu.roll(bias, (n - c * (n // 16)) % n, 1)
        out_ref[c, piece:, :n] = hi_lo(shifted)
        out_ref[c, piece:, n:] = jnp.zeros((16, n), BF)


def first_sum(parts, chunks):
    groups, rows, quarter = parts.shape
    return pl.pallas_call(
        first_sum_kernel,
        out_shape=jax.ShapeDtypeStruct((chunks, quarter // chunks + 16, rows - 16), BF),
        compiler_params=pltpu.CompilerParams(vmem_limit_bytes=VMEM),
        name="sum_over_y",
    )(parts)


def last_sum_kernel(parts_ref, enc_ref, dec_ref, bias_ref):
    groups, rows, cols = parts_ref.shape
    piece, n = rows - 16, cols // 2
    total = parts_ref[0].astype(F32)
    for g in range(1, groups):
        total = total + parts_ref[g].astype(F32)
    enc_ref[...] = total[:piece, :n]
    dec_ref[...] = total[:piece, n:]
    bias = jnp.sum(total[piece:, :n], axis=0, keepdims=True)
    bias_ref[...] = bias[:, : bias_ref.shape[1]]


def last_sum(parts, own):
    groups, rows, cols = parts.shape
    piece, n = rows - 16, cols // 2
    return pl.pallas_call(
        last_sum_kernel,
        out_shape=[
            jax.ShapeDtypeStruct((piece, n), F32),
            jax.ShapeDtypeStruct((piece, n), F32),
            jax.ShapeDtypeStruct((1, own), F32),
        ],
        compiler_params=pltpu.CompilerParams(vmem_limit_bytes=VMEM),
        name="sum_over_z",
    )(parts)


def exchange(x, blocks):
    shape = x.shape
    out = lax.all_to_all(
        x.reshape(blocks, shape[0] // blocks, shape[1]), "lat", split_axis=0, concat_axis=0, tiled=True
    )
    return out.reshape(shape)


def local(activations, block_ids, enc_weight, enc_bias, dec_weight, dec_bias):
    blocks = lax.axis_size("lat")
    parts_rows = lax.axis_size("rows")
    side = 4
    along_z = [[y * side + z for z in range(side)] for y in range(side)]
    along_y = [[y * side + z for y in range(side)] for z in range(side)]
    n = enc_weight.shape[1]
    ids = block_ids.T
    x = exchange(pack(ids, activations, blocks), blocks)
    decoded, pre = encode_decode(x, enc_weight, enc_bias[None, :], dec_weight)
    back = exchange(decoded, blocks)
    err = exchange(error_rows(ids, back, activations, dec_bias[None, :], blocks), blocks)
    terms = gradients(x, err, pre, dec_weight, side)
    terms = lax.all_to_all(
        terms, "rows", split_axis=0, concat_axis=0, axis_index_groups=along_y, tiled=True
    )
    terms = first_sum(terms, side)
    terms = lax.all_to_all(
        terms, "rows", split_axis=0, concat_axis=0, axis_index_groups=along_z, tiled=True
    )
    enc_grad, dec_turned, bias_grad = last_sum(terms, n // parts_rows)
    return enc_grad, dec_turned.T, bias_grad.reshape(-1)


def solution(mesh):
    in_specs = (
        P(("rows", "lat"), None),
        P(("rows", "lat"), None),
        P(None, "lat"),
        P("lat"),
        P("lat", None),
        P(),
    )
    out_specs = (P("rows", "lat"), P("lat", "rows"), P(("lat", "rows")))
    return jax.shard_map(local, mesh=mesh, in_specs=in_specs, out_specs=out_specs, check_vma=False)
```

time: 594 us -> 318 us (0.54)
  waiting for transfers between devices: 345 us -> 63 us
  blocking collectives: 145 us -> 214 us
  local copies, waits for them, and re-layouts: 55.3 us -> 2.19 us
  Pallas kernels: 0 us -> 33.4 us
  between operations: 14.9 us -> 0.65 us
  matrix products: 12.9 us -> 0 us
  other arithmetic: 9.38 us -> 0 us
  starting transfers between devices: 10.8 us -> 4.04 us
    reduce_scatter x2 -> x0, waiting for transfers between devices: 184 us -> none  [the longest x1 118 us: local(): lax.psum_scatter(dec_part, 'rows', scatter_dimension=0, tiled=True)]
    all_to_all x1 -> x4, blocking collectives: 95.1 us -> 214 us  [the longest x2 146 us: exchange(): lax.all_to_all(x.reshape(blocks, shape[0] // blocks, shape[1]), 'lat', sp...]
    all_to_all x2 -> x1, waiting for transfers between devices: 161 us -> 63 us  [exchange(): lax.all_to_all(x.reshape(blocks, shape[0] // blocks, shape[1]), 'lat', sp...]
    unnamed x1 -> x0, blocking collectives: 49.6 us -> none
    pallas_call x0 -> x6, Pallas kernels: none -> 33.4 us  [the longest x1 8.66 us: error_rows(): pl.pallas_call(functools.partial(error_kernel, blocks), grid=(steps,), in...]
    reshape x6 -> x0, local copies, waits for them, and re-layouts: 26.8 us -> none  [the longest x1 5.39 us: local(): back_rows = returned.reshape(slots, width)]
    gather x3 -> x0, local copies, waits for them, and re-layouts: 13.4 us -> none  [the longest x1 5.66 us: local(): back_rows[slot_ids].reshape(rows_dev, active, width).astype(jnp.float32)]
    dot_general x5 -> x0, matrix products: 12.9 us -> none  [the longest x2 7.29 us: contract_rows(): lax.dot_general(left, right, (((0,), (0,)), ((), ())), preferred_element_...]
  transfers between devices with their start and end apart: 4 -> 1, of which waited for: 4 -> 1; matrix products, arithmetic and copies ran while one was open for 2% -> 0% of each run, Pallas kernels for 0% -> 0%
where the time goes in v1:
time: 318 us; the launch traced here: 317 us
  blocking collectives  214 us (67%)
  waiting for transfers between devices  63 us (20%)
  Pallas kernels  33.4 us (11%)
  starting transfers between devices  4.04 us (1%)
    all_to_all x2, blocking collectives, exchange(): lax.all_to_all(x.reshape(blocks, shape[0] // blocks, shape[1]), 'lat', sp...  146 us
    all_to_all x2, blocking collectives, local(): lax.all_to_all(terms, 'rows', split_axis=0, concat_axis=0, axis_index_gro...  67.9 us
    all_to_all x1, waiting for transfers between devices, exchange(): lax.all_to_all(x.reshape(blocks, shape[0] // blocks, shape[1]), 'lat', sp...  63 us
    pallas_call x1, Pallas kernels, error_rows(): pl.pallas_call(functools.partial(error_kernel, blocks), grid=(steps,), in...  8.66 us
    pallas_call x1, Pallas kernels, gradients(): pl.pallas_call(grad_kernel, out_shape=jax.ShapeDtypeStruct((groups, 2 * n...  8.43 us
    pallas_call x1, Pallas kernels, encode_decode(): pl.pallas_call(functools.partial(code_kernel, 256), grid=(total // rows,)...  7.19 us
  transfers between devices with their start and end apart: 1, of which 1 were waited for; matrix products, arithmetic and copies ran while one was open for 0% of the time, Pallas kernels for 0%

profile of v1, /device:TPU:1, one launch (start us, length us, event | category | flops | bytes accessed | tf_op | source)
XLA Modules:
  0.0 317.4 jit_solution(5791846305005510941)
XLA Ops:
  0.6 4.8 %pack_rows.1 = bf16[768,1792]{1,0:T(8,128)(2,1)} custom-call(s32[2,128]{1,0:T(2,128)} %bitcast.17, bf16[128,3584]{1,0:T(8,128)(2,1)} %ar_ref.1), custom_call_target="tpu_custom_call" | custom-call | tf_op jit(solution)/shard_map/pack_rows/pallas_call | solution.py:91
  5.4 75.9 %all_to_all.25 = bf16[32,24,1792]{2,1,0:T(8,128)(2,1)} all-to-all(bf16[32,24,1792]{2,1,0:T(8,128)(2,1)} %bitcast.15), channel_id=1, replica_groups=mesh['rows'=16,'lat'=32] {'lat'}, dimensions={0} | all-to-all | bytes 5505024 | tf_op jit(solution)/shard_map/all_to_all | solution.py:294
  81.4 7.2 %encode_decode.1 = (bf16[768,1792]{1,0:T(8,128)(2,1)}, f32[768,128]{1,0:T(8,128)}) custom-call(bf16[768,1792]{1,0:T(8,128)(2,1)} %bitcast.10, bf16[3584,128]{1,0:T(8,128)(2,1)} %enc_ref.1, f32[1,128]{1,0:T(1,128)} %bitcast.19, bf16[128,3584]{1,0:T(8,128)(2,1)} %dec_ref.3), custom_call_target="tpu_custom_call" | custom-call | tf_op jit(solution)/shard_map/encode_decode/pallas_call | solution.py:129
  88.5 0.0 copy-start.1
  88.6 4.0 %all-to-all-start.1 = ((bf16[32,24,1792]{2,1,0:T(8,128)(2,1)}), bf16[32,24,1792]{2,1,0:T(8,128)(2,1)S(1)}, u32[]{:S(2)}, u32[]{:S(2)}) async-start(bf16[32,24,1792]{2,1,0:T(8,128)(2,1)} %bitcast.16), calls=%async_computation.1 | async-start | bytes 5505024 | tf_op jit(solution)/shard_map/all_to_all | solution.py:294
  92.6 0.0 copy-done.1
  92.6 0.6 broadcast_in_dim.7.bl_ref.br_ref
  93.2 63.0 %all-to-all-done.1 = bf16[32,24,1792]{2,1,0:T(8,128)(2,1)S(1)} async-done(((bf16[32,24,1792]{2,1,0:T(8,128)(2,1)}), bf16[32,24,1792]{2,1,0:T(8,128)(2,1)S(1)}, u32[]{:S(2)}, u32[]{:S(2)}) %all-to-all-start.1) | async-done | bytes 2752544 | tf_op jit(solution)/shard_map/all_to_all | solution.py:294
  156.2 0.0 copy-start
  156.2 1.6 copy-done
  157.8 8.7 %error_rows.1 = bf16[768,1792]{1,0:T(8,128)(2,1)} custom-call(s32[2,128]{1,0:T(2,128)} %bitcast.18, bf16[768,1792]{1,0:T(8,128)(2,1)} %bitcast.12, bf16[128,3584]{1,0:T(8,128)(2,1)} %ar_ref.1, bf16[128,3584]{1,0:T(8,128)(2,1)} %ar_ref.1, f32[1,3584]{1,0:T(1,128)} %broadcast_in_dim.7.bl_ref.br_ref, f32[1,3584]{1,0:T(1,128)} %broadcast_in_dim.7.bl_ref.br_ref), custom_call_target="tpu_custom_call" | custom-call | tf_op jit(solution)/shard_map/error_rows/pallas_call | solution.py:172
  166.5 70.3 %all_to_all.26 = bf16[32,24,1792]{2,1,0:T(8,128)(2,1)} all-to-all(bf16[32,24,1792]{2,1,0:T(8,128)(2,1)} %bitcast.14), channel_id=1, replica_groups=mesh['rows'=16,'lat'=32] {'lat'}, dimensions={0} | all-to-all | bytes 5505024 | tf_op jit(solution)/shard_map/all_to_all | solution.py:294
  236.7 8.4 %gradients.1 = bf16[4,272,896]{2,1,0:T(8,128)(2,1)} custom-call(bf16[768,1792]{1,0:T(8,128)(2,1)} %bitcast.11, bf16[768,1792]{1,0:T(8,128)(2,1)} %bitcast.13, f32[768,128]{1,0:T(8,128)} %get-tuple-element.9.pre_ref, bf16[128,3584]{1,0:T(8,128)(2,1)} %dec_ref.3), custom_call_target="tpu_custom_call" | custom-call | tf_op jit(solution)/shard_map/gradients/pallas_call | solution.py:227
  245.2 29.1 %all_to_all.27.parts_ref = bf16[4,272,896]{2,1,0:T(8,128)(2,1)} all-to-all(bf16[4,272,896]{2,1,0:T(8,128)(2,1)} %gradients.1), channel_id=1, replica_groups={{0,128,256,384},{32,160,288,416},{64,192,320,448},{96,224,352,480},{1,1..., dimensions={0} | all-to-all | bytes 3899392 | tf_op jit(solution)/shard_map/all_to_all | solution.py:313
  274.3 2.6 sum_over_y.1
  276.9 38.8 %all_to_all.28.parts_ref = bf16[4,240,256]{2,1,0:T(8,128)(2,1)} all-to-all(bf16[4,240,256]{2,1,0:T(8,128)(2,1)} %sum_over_y.1), channel_id=1, replica_groups={{0,32,64,96},{128,160,192,224},{256,288,320,352},{384,416,448,480},{1,3..., dimensions={0} | all-to-all | bytes 983040 | tf_op jit(solution)/shard_map/all_to_all | solution.py:317
  315.7 1.7 sum_over_z.1
Async XLA Ops:
  88.5 4.0 %copy-start.1 = (f32[3584]{0:T(1024)S(1)}, f32[3584]{0:T(1024)}, u32[]{:S(2)}) copy-start(f32[3584]{0:T(1024)} %param.11) | copy-start | bytes 43012
  88.6 67.7 %all-to-all-start.1 = ((bf16[32,24,1792]{2,1,0:T(8,128)(2,1)}), bf16[32,24,1792]{2,1,0:T(8,128)(2,1)S(1)}, u32[]{:S(2)}, u32[]{:S(2)}) async-start(bf16[32,24,1792]{2,1,0:T(8,128)(2,1)} %bitcast.16), calls=%async_computation.1 | async-start | bytes 5505024 | tf_op jit(solution)/shard_map/all_to_all | solution.py:294
  156.2 1.6 copy-start

commit v2 on v1

--- a/solution.py
+++ b/solution.py
@@ -12,6 +12,7 @@
 BF = jnp.bfloat16
 F32 = jnp.float32
 VMEM = 56 * 1024 * 1024
+SIDE = 4
 
 
 def place_of(rows, first):
@@ -194,10 +195,12 @@
     return jnp.where(row == 0, hi, jnp.where(row == 1, x - hi, 0.0)).astype(BF)
 
 
-def grad_kernel(x_ref, e_ref, pre_ref, dec_ref, out_ref, dec2):
+def grad_kernel(x_ref, e_ref, pre_ref, dec_ref, *refs):
+    outs, (dec2, pieces, sems) = refs[:-3], refs[-3:]
     rows, half = x_ref.shape
     n = pre_ref.shape[1]
-    groups, _, quarter = out_ref.shape
+    groups, _, quarter = pieces.shape
+    me = lax.axis_index("rows") // SIDE
     dec2[:n, :] = dec_ref[:, :half]
     dec2[n:, :] = dec_ref[:, half:]
     left = left_rows(rows)
@@ -214,60 +217,83 @@
         enc = dot_t(grads, x_ref[:, cols]).astype(BF)
         dec = dot_t(codes, e_ref[:, cols]).astype(BF)
         for s in range(2):
-            out_ref[g + s * (groups // 2), :n, :] = enc[s * n : s * n + n]
-            out_ref[g + s * (groups // 2), n : 2 * n, :] = dec[s * n : s * n + n]
+            pieces[g + s * (groups // 2), :n, :] = enc[s * n : s * n + n]
+            pieces[g + s * (groups // 2), n : 2 * n, :] = dec[s * n : s * n + n]
     for g in range(groups):
         shifted = pltpu.roll(bias, (n - g * (n // groups)) % n, 1)
-        out_ref[g, 2 * n :, :] = jnp.zeros((16, quarter), BF)
-        out_ref[g, 2 * n :, :n] = hi_lo(shifted)
-
-
-def gradients(x, err, pre, dec, groups):
+        pieces[g, 2 * n :, :] = jnp.zeros((16, quarter), BF)
+        pieces[g, 2 * n :, :n] = hi_lo(shifted)
+    hand_out(pieces, outs, me, sems)
+
+
+def hand_out(pieces, outs, me, sems):
+    copies = [
+        pltpu.make_async_copy(pieces.at[lax.rem(me + k, SIDE)], out, sems.at[k])
+        for k, out in enumerate(outs)
+    ]
+    for copy in copies:
+        copy.start()
+    for copy in copies:
+        copy.wait()
+
+
+def gradients(x, err, pre, dec):
     n, width = dec.shape
+    piece = (2 * n + 16, width // SIDE)
     return pl.pallas_call(
         grad_kernel,
-        out_shape=jax.ShapeDtypeStruct((groups, 2 * n + 16, width // groups), BF),
-        scratch_shapes=[pltpu.VMEM((2 * n, width // 2), BF)],
+        out_shape=[jax.ShapeDtypeStruct(piece, BF)] * SIDE,
+        out_specs=[pl.BlockSpec(memory_space=pl.ANY)] * SIDE,
+        scratch_shapes=[
+            pltpu.VMEM((2 * n, width // 2), BF),
+            pltpu.VMEM((SIDE,) + piece, BF),
+            pltpu.SemaphoreType.DMA((SIDE,)),
+        ],
         compiler_params=pltpu.CompilerParams(vmem_limit_bytes=VMEM),
         name="gradients",
     )(x, err, pre, dec)
 
 
-def first_sum_kernel(parts_ref, out_ref):
-    groups, rows, quarter = parts_ref.shape
+def first_sum_kernel(*refs):
+    ins, outs, (pieces, sems) = refs[:SIDE], refs[SIDE : 2 * SIDE], refs[2 * SIDE :]
+    rows, quarter = ins[0].shape
     n = (rows - 16) // 2
-    chunks, out_rows, _ = out_ref.shape
-    piece = out_rows - 16
-    total = parts_ref[0, : 2 * n, :].astype(F32)
-    bias = parts_ref[0, 2 * n :, :n].astype(F32)
-    for g in range(1, groups):
-        total = total + parts_ref[g, : 2 * n, :].astype(F32)
-        bias = bias + parts_ref[g, 2 * n :, :n].astype(F32)
+    piece = pieces.shape[1] - 16
+    total = ins[0][: 2 * n, :].astype(F32)
+    bias = ins[0][2 * n :, :n].astype(F32)
+    for part in ins[1:]:
+        total = total + part[: 2 * n, :].astype(F32)
+        bias = bias + part[2 * n :, :n].astype(F32)
     turned = total.T.astype(BF)
     bias = jnp.sum(bias, axis=0, keepdims=True)
-    for c in range(chunks):
-        out_ref[c, :piece, :] = turned[c * piece : (c + 1) * piece]
-        shifted = pltpu.roll(bias, (n - c * (n // 16)) % n, 1)
-        out_ref[c, piece:, :n] = hi_lo(shifted)
-        out_ref[c, piece:, n:] = jnp.zeros((16, n), BF)
-
-
-def first_sum(parts, chunks):
-    groups, rows, quarter = parts.shape
+    for c in range(SIDE):
+        pieces[c, :piece, :] = turned[c * piece : (c + 1) * piece]
+        shifted = pltpu.roll(bias, (n - c * (n // (SIDE * SIDE))) % n, 1)
+        pieces[c, piece:, :n] = hi_lo(shifted)
+        pieces[c, piece:, n:] = jnp.zeros((16, n), BF)
+    hand_out(pieces, outs, lax.rem(lax.axis_index("rows"), SIDE), sems)
+
+
+def first_sum(parts):
+    rows, quarter = parts[0].shape
+    piece = (quarter // SIDE + 16, rows - 16)
     return pl.pallas_call(
         first_sum_kernel,
-        out_shape=jax.ShapeDtypeStruct((chunks, quarter // chunks + 16, rows - 16), BF),
+        out_shape=[jax.ShapeDtypeStruct(piece, BF)] * SIDE,
+        out_specs=[pl.BlockSpec(memory_space=pl.ANY)] * SIDE,
+        scratch_shapes=[pltpu.VMEM((SIDE,) + piece, BF), pltpu.SemaphoreType.DMA((SIDE,))],
         compiler_params=pltpu.CompilerParams(vmem_limit_bytes=VMEM),
         name="sum_over_y",
-    )(parts)
-
-
-def last_sum_kernel(parts_ref, enc_ref, dec_ref, bias_ref):
-    groups, rows, cols = parts_ref.shape
+    )(*parts)
+
+
+def last_sum_kernel(*refs):
+    ins, (enc_ref, dec_ref, bias_ref) = refs[:SIDE], refs[SIDE:]
+    rows, cols = ins[0].shape
     piece, n = rows - 16, cols // 2
-    total = parts_ref[0].astype(F32)
-    for g in range(1, groups):
-        total = total + parts_ref[g].astype(F32)
+    total = ins[0][...].astype(F32)
+    for part in ins[1:]:
+        total = total + part[...].astype(F32)
     enc_ref[...] = total[:piece, :n]
     dec_ref[...] = total[:piece, n:]
     bias = jnp.sum(total[piece:, :n], axis=0, keepdims=True)
@@ -275,7 +301,7 @@
 
 
 def last_sum(parts, own):
-    groups, rows, cols = parts.shape
+    rows, cols = parts[0].shape
     piece, n = rows - 16, cols // 2
     return pl.pallas_call(
         last_sum_kernel,
@@ -286,7 +312,19 @@
         ],
         compiler_params=pltpu.CompilerParams(vmem_limit_bytes=VMEM),
         name="sum_over_z",
-    )(parts)
+    )(*parts)
+
+
+def swap_pieces(pieces, along_y):
+    got = [pieces[0]]
+    for k in (1, 3, 2):
+        pairs = []
+        for i in range(SIDE * SIDE):
+            y, z = divmod(i, SIDE)
+            to = ((y + k) % SIDE, z) if along_y else (y, (z + k) % SIDE)
+            pairs.append((i, to[0] * SIDE + to[1]))
+        got.append(lax.ppermute(pieces[k], "rows", pairs))
+    return got
 
 
 def exchange(x, blocks):
@@ -300,23 +338,14 @@
 def local(activations, block_ids, enc_weight, enc_bias, dec_weight, dec_bias):
     blocks = lax.axis_size("lat")
     parts_rows = lax.axis_size("rows")
-    side = 4
-    along_z = [[y * side + z for z in range(side)] for y in range(side)]
-    along_y = [[y * side + z for y in range(side)] for z in range(side)]
     n = enc_weight.shape[1]
     ids = block_ids.T
     x = exchange(pack(ids, activations, blocks), blocks)
     decoded, pre = encode_decode(x, enc_weight, enc_bias[None, :], dec_weight)
     back = exchange(decoded, blocks)
     err = exchange(error_rows(ids, back, activations, dec_bias[None, :], blocks), blocks)
-    terms = gradients(x, err, pre, dec_weight, side)
-    terms = lax.all_to_all(
-        terms, "rows", split_axis=0, concat_axis=0, axis_index_groups=along_y, tiled=True
-    )
-    terms = first_sum(terms, side)
-    terms = lax.all_to_all(
-        terms, "rows", split_axis=0, concat_axis=0, axis_index_groups=along_z, tiled=True
-    )
+    terms = swap_pieces(gradients(x, err, pre, dec_weight), True)
+    terms = swap_pieces(first_sum(terms), False)
     enc_grad, dec_turned, bias_grad = last_sum(terms, n // parts_rows)
     return enc_grad, dec_turned.T, bias_grad.reshape(-1)
 

time: 318 us -> 318 us (level)
  the two profiles are of different devices: /device:TPU:1 before, /device:TPU:42 now
where the time goes in v2:
time: 318 us; the launch traced here: 317 us
  blocking collectives  141 us (44%)
  waiting for transfers between devices  97.9 us (31%)
  starting transfers between devices  39.6 us (12%)
  Pallas kernels  33.5 us (11%)
  local copies, waits for them, and re-layouts  3.64 us (1%)
    all_to_all x2, blocking collectives, exchange(): lax.all_to_all(x.reshape(blocks, shape[0] // blocks, shape[1]), 'lat', sp...  141 us
    all_to_all x1, waiting for transfers between devices, exchange(): lax.all_to_all(x.reshape(blocks, shape[0] // blocks, shape[1]), 'lat', sp...  59.7 us
    ppermute x6, waiting for transfers between devices, swap_pieces(): got.append(lax.ppermute(pieces[k], 'rows', pairs))  38.2 us
    ppermute x6, starting transfers between devices, swap_pieces(): got.append(lax.ppermute(pieces[k], 'rows', pairs))  32.8 us
    pallas_call x1, Pallas kernels, error_rows(): pl.pallas_call(functools.partial(error_kernel, blocks), grid=(steps,), in...  8.67 us
    pallas_call x1, Pallas kernels, gradients(): pl.pallas_call(grad_kernel, out_shape=[jax.ShapeDtypeStruct(piece, BF)] *...  8.45 us
    pallas_call x1, Pallas kernels, encode_decode(): pl.pallas_call(functools.partial(code_kernel, 256), grid=(total // rows,)...  7.21 us
    all_to_all x1, starting transfers between devices, exchange(): lax.all_to_all(x.reshape(blocks, shape[0] // blocks, shape[1]), 'lat', sp...  6.85 us
  transfers between devices with their start and end apart: 7, of which 5 were waited for; matrix products, arithmetic and copies ran while one was open for 0% of the time, Pallas kernels for 0%

profile of v2, /device:TPU:42, one launch (start us, length us, event | category | flops | bytes accessed | tf_op | source)
XLA Modules:
  0.0 316.7 jit_solution(10646829221233597508)
XLA Ops:
  0.6 4.8 %pack_rows.1 = bf16[768,1792]{1,0:T(8,128)(2,1)} custom-call(s32[2,128]{1,0:T(2,128)} %bitcast.17, bf16[128,3584]{1,0:T(8,128)(2,1)} %ar_ref.1), custom_call_target="tpu_custom_call" | custom-call | tf_op jit(solution)/shard_map/pack_rows/pallas_call | solution.py:92
  5.4 70.5 %all_to_all.15 = bf16[32,24,1792]{2,1,0:T(8,128)(2,1)} all-to-all(bf16[32,24,1792]{2,1,0:T(8,128)(2,1)} %bitcast.15), channel_id=1, replica_groups=mesh['rows'=16,'lat'=32] {'lat'}, dimensions={0} | all-to-all | bytes 5505024 | tf_op jit(solution)/shard_map/all_to_all | solution.py:332
  75.9 7.2 %encode_decode.1 = (bf16[768,1792]{1,0:T(8,128)(2,1)}, f32[768,128]{1,0:T(8,128)}) custom-call(bf16[768,1792]{1,0:T(8,128)(2,1)} %bitcast.10, bf16[3584,128]{1,0:T(8,128)(2,1)} %enc_ref.1, f32[1,128]{1,0:T(1,128)} %bitcast.19, bf16[128,3584]{1,0:T(8,128)(2,1)} %dec_ref.3), custom_call_target="tpu_custom_call" | custom-call | tf_op jit(solution)/shard_map/encode_decode/pallas_call | solution.py:130
  83.1 6.8 %all-to-all-start.1 = ((bf16[32,24,1792]{2,1,0:T(8,128)(2,1)}), bf16[32,24,1792]{2,1,0:T(8,128)(2,1)S(1)}, u32[]{:S(2)}, u32[]{:S(2)}) async-start(bf16[32,24,1792]{2,1,0:T(8,128)(2,1)} %bitcast.16), calls=%async_computation.1 | async-start | bytes 5505024 | tf_op jit(solution)/shard_map/all_to_all | solution.py:332
  90.0 0.6 broadcast_in_dim.7.bl_ref.br_ref
  90.6 59.7 %all-to-all-done.1 = bf16[32,24,1792]{2,1,0:T(8,128)(2,1)S(1)} async-done(((bf16[32,24,1792]{2,1,0:T(8,128)(2,1)}), bf16[32,24,1792]{2,1,0:T(8,128)(2,1)S(1)}, u32[]{:S(2)}, u32[]{:S(2)}) %all-to-all-start.1) | async-done | bytes 2752544 | tf_op jit(solution)/shard_map/all_to_all | solution.py:332
  150.3 1.6 copy-done
  151.9 8.7 %error_rows.1 = bf16[768,1792]{1,0:T(8,128)(2,1)} custom-call(s32[2,128]{1,0:T(2,128)} %bitcast.18, bf16[768,1792]{1,0:T(8,128)(2,1)} %bitcast.12, bf16[128,3584]{1,0:T(8,128)(2,1)} %ar_ref.1, bf16[128,3584]{1,0:T(8,128)(2,1)} %ar_ref.1, f32[1,3584]{1,0:T(1,128)} %broadcast_in_dim.7.bl_ref.br_ref, f32[1,3584]{1,0:T(1,128)} %broadcast_in_dim.7.bl_ref.br_ref), custom_call_target="tpu_custom_call" | custom-call | tf_op jit(solution)/shard_map/error_rows/pallas_call | solution.py:173
  160.6 70.8 %all_to_all.16 = bf16[32,24,1792]{2,1,0:T(8,128)(2,1)} all-to-all(bf16[32,24,1792]{2,1,0:T(8,128)(2,1)} %bitcast.14), channel_id=1, replica_groups=mesh['rows'=16,'lat'=32] {'lat'}, dimensions={0} | all-to-all | bytes 5505024 | tf_op jit(solution)/shard_map/all_to_all | solution.py:332
  231.3 8.5 %gradients.1 = (bf16[272,896]{1,0:T(8,128)(2,1)}, bf16[272,896]{1,0:T(8,128)(2,1)}, bf16[272,896]{1,0:T(8,128)(2,1)}, bf16[272,896]{1,0:T(8,128)(2,1)}) custom-call(bf16[768,1792]{1,0:T(8,128)(2,1)} %bitcast.11, bf16[768,1792]{1,0:T(8,128)(2,1)} %bitcast.13, f32[768,128]{1,0:T(8,128)} %get-tuple-element.17.pre_ref, bf16[128,3584]{1,0:T(8,128)(2,1)} %dec_ref.3), custom_call_target="tpu_custom_call" | custom-call | tf_op jit(solution)/shard_map/gradients/pallas_call | solution.py:243
  239.8 3.5 %collective-permute-start = (bf16[272,896]{1,0:T(8,128)(2,1)}, bf16[272,896]{1,0:T(8,128)(2,1)S(1)}, u32[]{:S(2)}, u32[]{:S(2)}) collective-permute-start(bf16[272,896]{1,0:T(8,128)(2,1)} %get-tuple-element.19), channel_id=1, source_target_pairs={{0,128},{32,160},{64,192},{96,224},{128,256},{160,288},{192,320},{... | collective-permute-start | bytes 1462280 | tf_op jit(solution)/shard_map/ppermute | solution.py:326
  243.3 2.4 collective-permute-start.1
  245.7 4.2 %collective-permute-start.2 = (bf16[272,896]{1,0:T(8,128)(2,1)}, bf16[272,896]{1,0:T(8,128)(2,1)S(1)}, u32[]{:S(2)}, u32[]{:S(2)}) collective-permute-start(bf16[272,896]{1,0:T(8,128)(2,1)} %get-tuple-element.21), channel_id=1, source_target_pairs={{0,256},{32,288},{64,320},{96,352},{128,384},{160,416},{192,448},{... | collective-permute-start | bytes 1462280 | tf_op jit(solution)/shard_map/ppermute | solution.py:326
  249.9 6.1 %collective-permute-done.refs_1_ = bf16[272,896]{1,0:T(8,128)(2,1)S(1)} collective-permute-done((bf16[272,896]{1,0:T(8,128)(2,1)}, bf16[272,896]{1,0:T(8,128)(2,1)S(1)}, u32[]{:S(2)}, u32[]{:S(2)}) %collective-permute-start) | collective-permute-done | bytes 487456 | tf_op jit(solution)/shard_map/ppermute | solution.py:326
  256.0 2.8 collective-permute-done.1.refs_2_
  258.7 10.1 %collective-permute-done.2.refs_3_ = bf16[272,896]{1,0:T(8,128)(2,1)S(1)} collective-permute-done((bf16[272,896]{1,0:T(8,128)(2,1)}, bf16[272,896]{1,0:T(8,128)(2,1)S(1)}, u32[]{:S(2)}, u32[]{:S(2)}) %collective-permute-start.2) | collective-permute-done | bytes 487456 | tf_op jit(solution)/shard_map/ppermute | solution.py:326
  268.9 0.8 copy-done.3
  269.6 2.6 sum_over_y.1
  272.2 9.1 %collective-permute-start.3 = (bf16[240,256]{1,0:T(8,128)(2,1)}, bf16[240,256]{1,0:T(8,128)(2,1)S(1)}, u32[]{:S(2)}, u32[]{:S(2)}) collective-permute-start(bf16[240,256]{1,0:T(8,128)(2,1)} %get-tuple-element.23), channel_id=1, source_target_pairs={{0,32},{32,64},{64,96},{96,0},{128,160},{160,192},{192,224},{224,1... | collective-permute-start | bytes 368648 | tf_op jit(solution)/shard_map/ppermute | solution.py:326
  281.3 2.9 collective-permute-start.4
  284.2 10.8 %collective-permute-start.5 = (bf16[240,256]{1,0:T(8,128)(2,1)}, bf16[240,256]{1,0:T(8,128)(2,1)S(1)}, u32[]{:S(2)}, u32[]{:S(2)}) collective-permute-start(bf16[240,256]{1,0:T(8,128)(2,1)} %get-tuple-element.25), channel_id=1, source_target_pairs={{0,64},{32,96},{64,0},{96,32},{128,192},{160,224},{192,128},{224,1... | collective-permute-start | bytes 368648 | tf_op jit(solution)/shard_map/ppermute | solution.py:326
  295.1 19.2 %collective-permute-done.5.refs_3_ = bf16[240,256]{1,0:T(8,128)(2,1)S(1)} collective-permute-done((bf16[240,256]{1,0:T(8,128)(2,1)}, bf16[240,256]{1,0:T(8,128)(2,1)S(1)}, u32[]{:S(2)}, u32[]{:S(2)}) %collective-permute-start.5) | collective-permute-done | bytes 122912 | tf_op jit(solution)/shard_map/ppermute | solution.py:326
  314.3 0.6 copy-done.6
  314.9 1.8 sum_over_z.1
  (15 shorter events, 0.0 us)
Async XLA Ops:
  83.1 6.9 %copy-start.7 = (f32[3584]{0:T(1024)S(1)}, f32[3584]{0:T(1024)}, u32[]{:S(2)}) copy-start(f32[3584]{0:T(1024)} %param.11) | copy-start | bytes 43012
  83.1 67.2 %all-to-all-start.1 = ((bf16[32,24,1792]{2,1,0:T(8,128)(2,1)}), bf16[32,24,1792]{2,1,0:T(8,128)(2,1)S(1)}, u32[]{:S(2)}, u32[]{:S(2)}) async-start(bf16[32,24,1792]{2,1,0:T(8,128)(2,1)} %bitcast.16), calls=%async_computation.1 | async-start | bytes 5505024 | tf_op jit(solution)/shard_map/all_to_all | solution.py:332
  150.3 1.6 copy-start
  239.8 16.2 %collective-permute-start = (bf16[272,896]{1,0:T(8,128)(2,1)}, bf16[272,896]{1,0:T(8,128)(2,1)S(1)}, u32[]{:S(2)}, u32[]{:S(2)}) collective-permute-start(bf16[272,896]{1,0:T(8,128)(2,1)} %get-tuple-element.19), channel_id=1, source_target_pairs={{0,128},{32,160},{64,192},{96,224},{128,256},{160,288},{192,320},{... | collective-permute-start | bytes 1462280 | tf_op jit(solution)/shard_map/ppermute | solution.py:326
  243.3 15.5 %collective-permute-start.1 = (bf16[272,896]{1,0:T(8,128)(2,1)}, bf16[272,896]{1,0:T(8,128)(2,1)S(1)}, u32[]{:S(2)}, u32[]{:S(2)}) collective-permute-start(bf16[272,896]{1,0:T(8,128)(2,1)} %get-tuple-element.20), channel_id=1, source_target_pairs={{0,384},{32,416},{64,448},{96,480},{128,0},{160,32},{192,64},{224,... | collective-permute-start | bytes 1462280 | tf_op jit(solution)/shard_map/ppermute | solution.py:326
  245.7 23.2 %collective-permute-start.2 = (bf16[272,896]{1,0:T(8,128)(2,1)}, bf16[272,896]{1,0:T(8,128)(2,1)S(1)}, u32[]{:S(2)}, u32[]{:S(2)}) collective-permute-start(bf16[272,896]{1,0:T(8,128)(2,1)} %get-tuple-element.21), channel_id=1, source_target_pairs={{0,256},{32,288},{64,320},{96,352},{128,384},{160,416},{192,448},{... | collective-permute-start | bytes 1462280 | tf_op jit(solution)/shard_map/ppermute | solution.py:326
  256.0 12.9 %copy-start.1 = (bf16[272,896]{1,0:T(8,128)(2,1)}, bf16[272,896]{1,0:T(8,128)(2,1)S(1)}, u32[]{:S(2)}) copy-start(bf16[272,896]{1,0:T(8,128)(2,1)S(1)} %collective-permute-done.refs_1_) | copy-start | bytes 1462276
  258.7 10.1 %copy-start.2 = (bf16[272,896]{1,0:T(8,128)(2,1)}, bf16[272,896]{1,0:T(8,128)(2,1)S(1)}, u32[]{:S(2)}) copy-start(bf16[272,896]{1,0:T(8,128)(2,1)S(1)} %collective-permute-done.1.refs_2_) | copy-start | bytes 1462276
  268.8 0.8 copy-start.3
  272.2 22.8 %collective-permute-start.3 = (bf16[240,256]{1,0:T(8,128)(2,1)}, bf16[240,256]{1,0:T(8,128)(2,1)S(1)}, u32[]{:S(2)}, u32[]{:S(2)}) collective-permute-start(bf16[240,256]{1,0:T(8,128)(2,1)} %get-tuple-element.23), channel_id=1, source_target_pairs={{0,32},{32,64},{64,96},{96,0},{128,160},{160,192},{192,224},{224,1... | collective-permute-start | bytes 368648 | tf_op jit(solution)/shard_map/ppermute | solution.py:326
  281.3 13.7 %collective-permute-start.4 = (bf16[240,256]{1,0:T(8,128)(2,1)}, bf16[240,256]{1,0:T(8,128)(2,1)S(1)}, u32[]{:S(2)}, u32[]{:S(2)}) collective-permute-start(bf16[240,256]{1,0:T(8,128)(2,1)} %get-tuple-element.24), channel_id=1, source_target_pairs={{0,96},{32,0},{64,32},{96,64},{128,224},{160,128},{192,160},{224,1... | collective-permute-start | bytes 368648 | tf_op jit(solution)/shard_map/ppermute | solution.py:326
  284.2 30.0 %collective-permute-start.5 = (bf16[240,256]{1,0:T(8,128)(2,1)}, bf16[240,256]{1,0:T(8,128)(2,1)S(1)}, u32[]{:S(2)}, u32[]{:S(2)}) collective-permute-start(bf16[240,256]{1,0:T(8,128)(2,1)} %get-tuple-element.25), channel_id=1, source_target_pairs={{0,64},{32,96},{64,0},{96,32},{128,192},{160,224},{192,128},{224,1... | collective-permute-start | bytes 368648 | tf_op jit(solution)/shard_map/ppermute | solution.py:326
  295.0 19.2 %copy-start.4 = (bf16[240,256]{1,0:T(8,128)(2,1)}, bf16[240,256]{1,0:T(8,128)(2,1)S(1)}, u32[]{:S(2)}) copy-start(bf16[240,256]{1,0:T(8,128)(2,1)S(1)} %collective-permute-done.3.refs_1_) | copy-start | bytes 368644
  295.1 19.2 %copy-start.5 = (bf16[240,256]{1,0:T(8,128)(2,1)}, bf16[240,256]{1,0:T(8,128)(2,1)S(1)}, u32[]{:S(2)}) copy-start(bf16[240,256]{1,0:T(8,128)(2,1)S(1)} %collective-permute-done.4.refs_2_) | copy-start | bytes 368644
  314.3 0.6 copy-start.6

commit v3 on v2

v3 whole, which is shorter than its diff:
```python
import functools

import jax
import jax.numpy as jnp
from jax import lax
from jax.experimental import pallas as pl
from jax.experimental.pallas import tpu as pltpu
from jax.sharding import PartitionSpec as P

SLOTS = 6
PAIR = 2 * SLOTS
SIDE = 4
STEPS = (0, 1, 2, -2, -1)
BF = jnp.bfloat16
F32 = jnp.float32
VMEM = 56 * 1024 * 1024
PARAMS = pltpu.CompilerParams(vmem_limit_bytes=VMEM)
ANY = pl.BlockSpec(memory_space=pl.ANY)


def by_twelve(row):
    return lax.shift_right_logical(row * 5462, 16)


def dot(a, b):
    return lax.dot_general(a, b, (((1,), (0,)), ((), ())), preferred_element_type=F32)


def dot_t(a, b):
    return lax.dot_general(a, b, (((0,), (0,)), ((), ())), preferred_element_type=F32)


def dot_nt(a, b):
    return lax.dot_general(a, b, (((1,), (1,)), ((), ())), preferred_element_type=F32)


def left_rows(rows):
    row = lax.broadcasted_iota(jnp.int32, (rows, 1), 0)
    return row - by_twelve(row) * PAIR < SLOTS


def split_halves(x, left):
    zero = jnp.zeros_like(x)
    return jnp.concatenate([jnp.where(left, x, zero), jnp.where(left, zero, x)], axis=1)


def join_halves(y, left):
    rows, n = y.shape[0], y.shape[1] // 2
    yl, yr = y[:, :n], y[:, n:]
    after = pltpu.roll(yr, rows - SLOTS, 0)
    before = pltpu.roll(yl, SLOTS, 0)
    return jnp.where(left, yl + after, yr + before)


def one_hot_slots(ids, blocks):
    n = ids.shape[1]
    rows = 2 * blocks * PAIR
    number = lax.broadcasted_iota(jnp.int32, (blocks, n), 0)
    member = (number == ids[0:1, :]) | (number == ids[1:2, :])
    earlier = (
        lax.broadcasted_iota(jnp.int32, (n, n), 0) < lax.broadcasted_iota(jnp.int32, (n, n), 1)
    )
    position = dot(member.astype(F32).astype(BF), earlier.astype(F32).astype(BF))
    code = jnp.where(member, position, 200.0).astype(BF)
    zl = lax.rem(lax.axis_index("lat") // 2, SIDE)
    row = lax.broadcasted_iota(jnp.int32, (rows, 1), 0)
    piece = by_twelve(row)
    place = row - piece * PAIR
    first = piece < blocks
    in_a, in_b = piece, piece - blocks
    xc = jnp.where(first, in_a & 7, lax.shift_right_logical(in_b, 2))
    k = jnp.where(first, lax.shift_right_logical(in_a, 3), in_b & 3)
    block = lax.shift_right_logical(xc, 1) * (2 * SIDE) + ((zl + k) & 3) * 2 + (xc & 1)
    left = place < SLOTS
    slot = place - jnp.where(left, 0, SLOTS) + jnp.where(first, 0, SLOTS)
    expand = lax.broadcasted_iota(jnp.int32, (rows, blocks), 1) == block
    spread = dot(expand.astype(F32).astype(BF), code)
    hit = (spread == slot.astype(F32)).astype(F32)
    return split_halves(hit, left).astype(BF)


def start(pairs, sems, first=0):
    copies = [pltpu.make_async_copy(a, b, sems.at[first + i]) for i, (a, b) in enumerate(pairs)]
    for copy in copies:
        copy.start()
    return copies


def wait(copies):
    for copy in copies:
        copy.wait()


def five_moves(refs, k, first, rows, other):
    if k != 2:
        return [(refs[k if k < 2 else 4].at[first : first + rows], other)]
    part = refs[2].shape[0]
    return [
        (refs[2 + h], other.at[h * part - first : (h + 1) * part - first])
        for h in range(2)
        if first <= h * part < first + rows
    ]


def flip(pairs):
    return [(b, a) for a, b in pairs]


def send_slots(sel, rows2, pieces, outs, sems):
    part = pieces.shape[1]
    copies = []
    for i in range(2 * SIDE):
        pieces[i] = dot(sel[i * part : (i + 1) * part, :], rows2[...]).astype(BF)
        if i < SIDE:
            pairs = flip(five_moves(outs, i, 0, part, pieces.at[i]))
        else:
            pairs = [(pieces.at[i], outs[5].at[(i - SIDE) * part : (i - SIDE + 1) * part])]
        copies += start(pairs, sems, 2 * i)
    wait(copies)


def five_shapes(total, half):
    part = total // SIDE
    rows = [part, part, part // 2, part // 2, part]
    return [jax.ShapeDtypeStruct((r, half), BF) for r in rows]


def slot_shapes(blocks, half):
    total = blocks * PAIR
    return five_shapes(total, half) + [jax.ShapeDtypeStruct((total, half), BF)]


def pack_kernel(blocks, ids_ref, act_ref, *refs):
    outs, (act2, sel, pieces, in_sems, sems) = refs[:6], refs[6:]
    n, width = act_ref.shape
    half = width // 2
    copies = start(
        [(act_ref.at[:, s * half : (s + 1) * half], act2.at[s * n : (s + 1) * n]) for s in range(2)],
        in_sems,
    )
    sel[...] = one_hot_slots(ids_ref[...], blocks)
    wait(copies)
    send_slots(sel, act2, pieces, outs, sems)


def pack(ids, act, blocks):
    n, width = act.shape
    half = width // 2
    part = blocks * PAIR // SIDE
    return pl.pallas_call(
        functools.partial(pack_kernel, blocks),
        in_specs=[pl.BlockSpec(memory_space=pltpu.VMEM), ANY],
        out_specs=[ANY] * 6,
        out_shape=slot_shapes(blocks, half),
        scratch_shapes=[
            pltpu.VMEM((2 * n, half), BF),
            pltpu.VMEM((2 * SIDE * part, 2 * n), BF),
            pltpu.VMEM((2 * SIDE, part, half), BF),
            pltpu.SemaphoreType.DMA((2,)),
            pltpu.SemaphoreType.DMA((4 * SIDE,)),
        ],
        compiler_params=PARAMS,
        name="pack_rows",
    )(ids, act)


def swap_kernel(merge, *refs):
    if merge:
        ins, out_ref, (pieces, done, in_sems, sems) = refs[:5], refs[5], refs[6:]
    else:
        in_ref, outs, (pieces, done, in_sems, sems) = refs[0], refs[1:6], refs[6:]
    rows = pieces.shape[1]
    part = rows // SIDE
    halves = range(2)

    def by_step(arrays, buffer, h):
        pairs = []
        for k in range(SIDE):
            pairs += five_moves(arrays, k, h * part, part, buffer.at[h, k * part : (k + 1) * part])
        return pairs

    if merge:
        moves = [by_step(ins, pieces, h) for h in halves]
    else:
        moves = [[(in_ref.at[h * rows : (h + 1) * rows], pieces.at[h])] for h in halves]
    copies = [start(moves[h], in_sems, h * SIDE) for h in halves]
    row = lax.broadcasted_iota(jnp.int32, (rows, 1), 0)
    piece = by_twelve(row)
    source = (piece & 3) * part + lax.shift_right_logical(piece, 2) * PAIR + row - piece * PAIR
    turn = (lax.broadcasted_iota(jnp.int32, (rows, rows), 1) == source).astype(F32).astype(BF)
    sent = []
    for h in halves:
        wait(copies[h])
        done[h] = dot(turn, pieces[h]).astype(BF)
        if merge:
            sent += start([(done.at[h], out_ref.at[h * rows : (h + 1) * rows])], sems, h * SIDE)
        else:
            sent += start(flip(by_step(outs, done, h)), sems, h * SIDE)
    wait(sent)


def swap_pieces(arrays, merge):
    total = sum(a.shape[0] for a in arrays)
    half = arrays[0].shape[1]
    return pl.pallas_call(
        functools.partial(swap_kernel, merge),
        in_specs=[ANY] * len(arrays),
        out_specs=ANY if merge else [ANY] * 5,
        out_shape=jax.ShapeDtypeStruct((total, half), BF) if merge else five_shapes(total, half),
        scratch_shapes=[
            pltpu.VMEM((2, total // 2, half), BF),
            pltpu.VMEM((2, total // 2, half), BF),
            pltpu.SemaphoreType.DMA((4 * SIDE,)),
            pltpu.SemaphoreType.DMA((4 * SIDE,)),
        ],
        compiler_params=PARAMS,
        name="merge_pieces" if merge else "split_pieces",
    )(*arrays)


def code_kernel(parts, *refs):
    ins, (enc_ref, bias_ref, dec_ref) = refs[:parts], refs[parts : parts + 3]
    outs, pre_ref = refs[parts + 3 : 2 * parts + 3], refs[2 * parts + 3]
    enc2, dec2, x, done, w_sems, in_sems, sems = refs[2 * parts + 4 :]
    half, n = enc2.shape[0], enc2.shape[1] // 2
    rows = x.shape[1]

    def piece(refs, i, buffer):
        if parts == 1:
            return [(refs[0].at[i * rows : (i + 1) * rows], buffer.at[i])]
        return five_moves(refs, i, 0, rows, buffer.at[i])

    enc_copies = start(
        [(enc_ref.at[s * half : (s + 1) * half], enc2.at[:, s * n : (s + 1) * n]) for s in range(2)],
        w_sems,
    )
    in_copies = [start(piece(ins, i, x), in_sems, 2 * i) for i in range(SIDE)]
    dec_copies = start(
        [(dec_ref.at[:, s * half : (s + 1) * half], dec2.at[s * n : (s + 1) * n]) for s in range(2)],
        w_sems,
        2,
    )
    left = left_rows(rows)
    wait(enc_copies)
    sent = []
    for i in range(SIDE):
        wait(in_copies[i])
        pre = join_halves(dot(x[i], enc2[...]), left) + bias_ref[...]
        pre_ref[i * rows : (i + 1) * rows, :] = pre
        codes = split_halves(pre * jax.nn.sigmoid(pre), left).astype(BF)
        if i == 0:
            wait(dec_copies)
        done[i] = dot(codes, dec2[...]).astype(BF)
        sent += start(flip(piece(outs, i, done)), sems, 2 * i)
    wait(sent)


def encode_decode(x, enc, bias, dec):
    width, n = enc.shape
    half = width // 2
    parts = len(x)
    total = sum(a.shape[0] for a in x)
    rows = total // SIDE
    return pl.pallas_call(
        functools.partial(code_kernel, parts),
        in_specs=[ANY] * (parts + 1) + [pl.BlockSpec(memory_space=pltpu.VMEM), ANY],
        out_specs=[ANY] * parts + [pl.BlockSpec(memory_space=pltpu.VMEM)],
        out_shape=[jax.ShapeDtypeStruct(a.shape, BF) for a in x]
        + [jax.ShapeDtypeStruct((total, n), F32)],
        scratch_shapes=[
            pltpu.VMEM((half, 2 * n), BF),
            pltpu.VMEM((2 * n, half), BF),
            pltpu.VMEM((SIDE, rows, half), BF),
            pltpu.VMEM((SIDE, rows, half), BF),
            pltpu.SemaphoreType.DMA((4,)),
            pltpu.SemaphoreType.DMA((2 * SIDE,)),
            pltpu.SemaphoreType.DMA((2 * SIDE,)),
        ],
        compiler_params=PARAMS,
        name="encode_decode",
    )(*x, enc, bias, dec)


def slot_moves(refs, buffer):
    part = refs[0].shape[0]
    pairs = []
    for k in range(SIDE):
        pairs += five_moves(refs, k, 0, part, buffer.at[k * part : (k + 1) * part])
    return pairs + [(refs[5], buffer.at[SIDE * part :])]


def error_kernel(blocks, ids_ref, bias_ref, act_ref, *refs):
    ins, outs = refs[:6], refs[6:12]
    act2, back, sel, err2, pieces, act_sems, in_sems, sems = refs[12:]
    n, width = act_ref.shape
    half = width // 2
    copies = start(slot_moves(ins, back), in_sems)
    copies += start(
        [(act_ref.at[:, s * half : (s + 1) * half], act2.at[s * n : (s + 1) * n]) for s in range(2)],
        act_sems,
    )
    sel[...] = one_hot_slots(ids_ref[...], blocks)
    wait(copies)
    step = 256
    for c in range(0, half, step):
        sums = dot_t(sel[...], back[:, c : c + step])
        for s in range(2):
            rows = slice(s * n, (s + 1) * n)
            bias = bias_ref[:, s * half + c : s * half + c + step]
            wanted = act2[rows, c : c + step].astype(F32)
            err2[rows, c : c + step] = ((sums[rows] + bias - wanted) * (1.0 / 64.0)).astype(BF)
    send_slots(sel, err2, pieces, outs, sems)


def error_rows(ids, back, act, bias, blocks):
    n, width = act.shape
    half = width // 2
    total = 2 * blocks * PAIR
    part = total // (2 * SIDE)
    in_vmem = pl.BlockSpec(memory_space=pltpu.VMEM)
    return pl.pallas_call(
        functools.partial(error_kernel, blocks),
        in_specs=[in_vmem, in_vmem] + [ANY] * 7,
        out_specs=[ANY] * 6,
        out_shape=slot_shapes(blocks, half),
        scratch_shapes=[
            pltpu.VMEM((2 * n, half), BF),
            pltpu.VMEM((total, half), BF),
            pltpu.VMEM((total, 2 * n), BF),
            pltpu.VMEM((2 * n, half), BF),
            pltpu.VMEM((2 * SIDE, part, half), BF),
            pltpu.SemaphoreType.DMA((2,)),
            pltpu.SemaphoreType.DMA((6,)),
            pltpu.SemaphoreType.DMA((4 * SIDE,)),
        ],
        compiler_params=PARAMS,
        name="error_rows",
    )(ids, bias, act, *back)


def hi_lo(x):
    hi = x.astype(BF).astype(F32)
    row = lax.broadcasted_iota(jnp.int32, (16, x.shape[1]), 0)
    return jnp.where(row == 0, hi, jnp.where(row == 1, x - hi, 0.0)).astype(BF)


def grad_kernel(pre_a, pre_b, dec_ref, *refs):
    x_refs, e_refs, outs = refs[:6], refs[6:12], refs[12:16]
    dec2, x, e, pieces, w_sems, x_sems, e_sems, sems = refs[16:]
    rows, half = x.shape
    n = pre_a.shape[1]
    groups, _, quarter = pieces.shape
    dec_copies = start(
        [(dec_ref.at[:, s * half : (s + 1) * half], dec2.at[s * n : (s + 1) * n]) for s in range(2)],
        w_sems,
    )
    e_copies = start(slot_moves(e_refs, e), e_sems)
    x_copies = start(slot_moves(x_refs, x), x_sems)
    me = lax.axis_index("rows") // SIDE
    left = left_rows(rows)
    pre = jnp.concatenate([pre_b[...], pre_a[...]], axis=0)
    sig = jax.nn.sigmoid(pre)
    codes = split_halves(pre * sig, left).astype(BF)
    wait(dec_copies)
    wait(e_copies)
    code_grad = join_halves(dot_nt(e[...], dec2[...]), left)
    grad = (code_grad * sig * (1.0 + pre * (1.0 - sig))).astype(BF).astype(F32)
    grads = split_halves(grad, left)
    bias = jnp.sum(grads[:, :n], axis=0, keepdims=True)
    grads = grads.astype(BF)
    wait(x_copies)
    for g in range(0, groups // 2):
        cols = pl.ds(g * quarter, quarter)
        enc = dot_t(grads, x[:, cols]).astype(BF)
        dec = dot_t(codes, e[:, cols]).astype(BF)
        for s in range(2):
            pieces[g + s * (groups // 2), :n, :] = enc[s * n : s * n + n]
            pieces[g + s * (groups // 2), n : 2 * n, :] = dec[s * n : s * n + n]
    for g in range(groups):
        shifted = pltpu.roll(bias, (n - g * (n // groups)) % n, 1)
        pieces[g, 2 * n :, :] = jnp.zeros((16, quarter), BF)
        pieces[g, 2 * n :, :n] = hi_lo(shifted)
    hand_out(pieces, outs, me, sems)


def hand_out(pieces, outs, me, sems):
    wait(start([(pieces.at[lax.rem(me + k, SIDE)], out) for k, out in enumerate(outs)], sems))


def gradients(x, err, pre_a, pre_b, dec):
    n, width = dec.shape
    piece = (2 * n + 16, width // SIDE)
    rows = 2 * pre_a.shape[0]
    in_vmem = pl.BlockSpec(memory_space=pltpu.VMEM)
    return pl.pallas_call(
        grad_kernel,
        in_specs=[in_vmem, in_vmem] + [ANY] * 13,
        out_shape=[jax.ShapeDtypeStruct(piece, BF)] * SIDE,
        out_specs=[ANY] * SIDE,
        scratch_shapes=[
            pltpu.VMEM((2 * n, width // 2), BF),
            pltpu.VMEM((rows, width // 2), BF),
            pltpu.VMEM((rows, width // 2), BF),
            pltpu.VMEM((SIDE,) + piece, BF),
            pltpu.SemaphoreType.DMA((2,)),
            pltpu.SemaphoreType.DMA((6,)),
            pltpu.SemaphoreType.DMA((6,)),
            pltpu.SemaphoreType.DMA((SIDE,)),
        ],
        compiler_params=PARAMS,
        name="gradients",
    )(pre_a, pre_b, dec, *x, *err)


def first_sum_kernel(*refs):
    ins, outs, (pieces, sems) = refs[:SIDE], refs[SIDE : 2 * SIDE], refs[2 * SIDE :]
    rows, quarter = ins[0].shape
    n = (rows - 16) // 2
    piece = pieces.shape[1] - 16
    total = ins[0][: 2 * n, :].astype(F32)
    bias = ins[0][2 * n :, :n].astype(F32)
    for part in ins[1:]:
        total = total + part[: 2 * n, :].astype(F32)
        bias = bias + part[2 * n :, :n].astype(F32)
    turned = total.T.astype(BF)
    bias = jnp.sum(bias, axis=0, keepdims=True)
    for c in range(SIDE):
        pieces[c, :piece, :] = turned[c * piece : (c + 1) * piece]
        shifted = pltpu.roll(bias, (n - c * (n // (SIDE * SIDE))) % n, 1)
        pieces[c, piece:, :n] = hi_lo(shifted)
        pieces[c, piece:, n:] = jnp.zeros((16, n), BF)
    hand_out(pieces, outs, lax.rem(lax.axis_index("rows"), SIDE), sems)


def first_sum(parts):
    rows, quarter = parts[0].shape
    piece = (quarter // SIDE + 16, rows - 16)
    return pl.pallas_call(
        first_sum_kernel,
        out_shape=[jax.ShapeDtypeStruct(piece, BF)] * SIDE,
        out_specs=[pl.BlockSpec(memory_space=pl.ANY)] * SIDE,
        scratch_shapes=[pltpu.VMEM((SIDE,) + piece, BF), pltpu.SemaphoreType.DMA((SIDE,))],
        compiler_params=PARAMS,
        name="sum_over_y",
    )(*parts)


def last_sum_kernel(*refs):
    ins, (enc_ref, dec_ref, bias_ref) = refs[:SIDE], refs[SIDE:]
    rows, cols = ins[0].shape
    piece, n = rows - 16, cols // 2
    total = ins[0][...].astype(F32)
    for part in ins[1:]:
        total = total + part[...].astype(F32)
    enc_ref[...] = total[:piece, :n]
    dec_ref[...] = total[:piece, n:]
    bias = jnp.sum(total[piece:, :n], axis=0, keepdims=True)
    bias_ref[...] = bias[:, : bias_ref.shape[1]]


def last_sum(parts, own):
    rows, cols = parts[0].shape
    piece, n = rows - 16, cols // 2
    return pl.pallas_call(
        last_sum_kernel,
        out_shape=[
            jax.ShapeDtypeStruct((piece, n), F32),
            jax.ShapeDtypeStruct((piece, n), F32),
            jax.ShapeDtypeStruct((1, own), F32),
        ],
        compiler_params=PARAMS,
        name="sum_over_z",
    )(*parts)


def share_pieces(pieces, along_y):
    got = [pieces[0]]
    for k in (1, 3, 2):
        pairs = []
        for i in range(SIDE * SIDE):
            y, z = divmod(i, SIDE)
            to = ((y + k) % SIDE, z) if along_y else (y, (z + k) % SIDE)
            pairs.append((i, to[0] * SIDE + to[1]))
        got.append(lax.ppermute(pieces[k], "rows", pairs))
    return got


def along_z(x, step):
    if step == 0:
        return x
    pairs = []
    for i in range(512):
        rows, lat = divmod(i, 32)
        y, z_hi = divmod(rows, SIDE)
        x_place, rest = divmod(lat, 2 * SIDE)
        z_lo, core = divmod(rest, 2)
        z = (z_hi * SIDE + z_lo + step) % (SIDE * SIDE)
        to_rows = y * SIDE + z // SIDE
        pairs.append((i, to_rows * 32 + x_place * 2 * SIDE + z % SIDE * 2 + core))
    return lax.ppermute(x, ("rows", "lat"), pairs)


def over_x(x):
    groups = [
        [xp * 2 * SIDE + z * 2 + core for xp in range(SIDE) for core in range(2)]
        for z in range(SIDE)
    ]
    members = 2 * SIDE
    shape = x.shape
    out = lax.all_to_all(
        x.reshape(members, shape[0] // members, shape[1]),
        "lat",
        split_axis=0,
        concat_axis=0,
        axis_index_groups=groups,
        tiled=True,
    )
    return out.reshape(shape)


def to_owners(slots):
    moved = [along_z(a, step) for a, step in zip(slots[:5], STEPS)]
    crossed, merged = lax.optimization_barrier((over_x(slots[5]), swap_pieces(moved, True)))
    stream_a = over_x(merged)
    stream_b = [along_z(a, step) for a, step in zip(swap_pieces([crossed], False), STEPS)]
    return stream_a, stream_b


def to_homes(stream_a, stream_b):
    moved = [along_z(a, -step) for a, step in zip(stream_b, STEPS)]
    crossed, merged = lax.optimization_barrier((over_x(stream_a), swap_pieces(moved, True)))
    home_b = over_x(merged)
    home_a = [along_z(a, -step) for a, step in zip(swap_pieces([crossed], False), STEPS)]
    return [*home_a, home_b]


def local(activations, block_ids, enc_weight, enc_bias, dec_weight, dec_bias):
    blocks = lax.axis_size("lat")
    parts_rows = lax.axis_size("rows")
    n = enc_weight.shape[1]
    ids = block_ids.T
    bias = enc_bias[None, :]
    x_a, x_b = to_owners(pack(ids, activations, blocks))
    dec_a, pre_a = encode_decode([x_a], enc_weight, bias, dec_weight)
    x_b, dec_a = lax.optimization_barrier((x_b, dec_a))
    *dec_b, pre_b = encode_decode(x_b, enc_weight, bias, dec_weight)
    back = to_homes(dec_a, dec_b)
    e_a, e_b = to_owners(error_rows(ids, back, activations, dec_bias[None, :], blocks))
    terms = gradients([*x_b, x_a], [*e_b, e_a], pre_a, pre_b, dec_weight)
    terms = share_pieces(terms, True)
    terms = share_pieces(first_sum(terms), False)
    enc_grad, dec_turned, bias_grad = last_sum(terms, n // parts_rows)
    return enc_grad, dec_turned.T, bias_grad.reshape(-1)


def solution(mesh):
    in_specs = (
        P(("rows", "lat"), None),
        P(("rows", "lat"), None),
        P(None, "lat"),
        P("lat"),
        P("lat", None),
        P(),
    )
    out_specs = (P("rows", "lat"), P("lat", "rows"), P(("lat", "rows")))
    return jax.shard_map(local, mesh=mesh, in_specs=in_specs, out_specs=out_specs, check_vma=False)
```

time: 318 us -> 298 us (0.937)
  the two profiles are of different devices: /device:TPU:42 before, /device:TPU:56 now
where the time goes in v3:
time: 298 us; the launch traced here: 296 us
  starting transfers between devices  142 us (48%)
  waiting for transfers between devices  84.7 us (28%)
  Pallas kernels  54.6 us (18%)
  local copies, waits for them, and re-layouts  12.8 us (4%)
    ppermute x24, starting transfers between devices, along_z(): return lax.ppermute(x, ('rows', 'lat'), pairs)  89.4 us
    ppermute x24, waiting for transfers between devices, along_z(): return lax.ppermute(x, ('rows', 'lat'), pairs)  46.1 us
    ppermute x6, waiting for transfers between devices, share_pieces(): got.append(lax.ppermute(pieces[k], 'rows', pairs))  36.1 us
    ppermute x6, starting transfers between devices, share_pieces(): got.append(lax.ppermute(pieces[k], 'rows', pairs))  26.9 us
    all_to_all x6, starting transfers between devices, over_x(): lax.all_to_all(x.reshape(members, shape[0] // members, shape[1]), 'lat',...  26.1 us
    pallas_call x6, Pallas kernels, swap_pieces(): pl.pallas_call(functools.partial(swap_kernel, merge), in_specs=[ANY] * le...  18 us
    pallas_call x2, Pallas kernels, encode_decode(): pl.pallas_call(functools.partial(code_kernel, parts), in_specs=[ANY] * (p...  13.4 us
    unnamed x90, local copies, waits for them, and re-layouts  12.2 us
  transfers between devices with their start and end apart: 36, of which 13 were waited for; matrix products, arithmetic and copies ran while one was open for 0% of the time, Pallas kernels for 11%

profile of v3, /device:TPU:56, one launch (start us, length us, event | category | flops | bytes accessed | tf_op | source)
XLA Modules:
  0.0 295.9 jit_solution(14578469508500094333)
XLA Ops:
  14.9 6.3 %collective-permute-start.1 = (bf16[48,1792]{1,0:T(8,128)(2,1)S(1)}, bf16[48,1792]{1,0:T(8,128)(2,1)S(1)}, u32[]{:S(2)}, u32[]{:S(2)}) collective-permute-start(bf16[48,1792]{1,0:T(8,128)(2,1)S(1)} %copy-done.44), channel_id=1, source_target_pairs={{0,4},{1,5},{2,6},{3,7},{4,32},{5,33},{6,34},{7,35},{8,12},{9,13},... | collective-permute-start | bytes 516104 | tf_op jit(solution)/shard_map/ppermute | solution.py:500
  21.2 6.6 %collective-permute-start.2 = (bf16[48,1792]{1,0:T(8,128)(2,1)S(1)}, bf16[48,1792]{1,0:T(8,128)(2,1)S(1)}, u32[]{:S(2)}, u32[]{:S(2)}) collective-permute-start(bf16[48,1792]{1,0:T(8,128)(2,1)S(1)} %copy-done.43), channel_id=1, source_target_pairs={{0,100},{1,101},{2,102},{3,103},{4,0},{5,1},{6,2},{7,3},{8,108},{9... | collective-permute-start | bytes 516104 | tf_op jit(solution)/shard_map/ppermute | solution.py:500
  27.8 8.3 %collective-permute-done.1.refs_2_ = bf16[48,1792]{1,0:T(8,128)(2,1)S(1)} collective-permute-done((bf16[48,1792]{1,0:T(8,128)(2,1)S(1)}, bf16[48,1792]{1,0:T(8,128)(2,1)S(1)}, u32[]{:S(2)}, u32[]{:S(2)}) %collective-permute-start.1) | collective-permute-done | bytes 172064 | tf_op jit(solution)/shard_map/ppermute | solution.py:500
  54.4 5.8 %collective-permute-start.5 = (bf16[48,1792]{1,0:T(8,128)(2,1)}, bf16[48,1792]{1,0:T(8,128)(2,1)S(1)}, u32[]{:S(2)}, u32[]{:S(2)}) collective-permute-start(bf16[48,1792]{1,0:T(8,128)(2,1)} %get-tuple-element.72), channel_id=1, source_target_pairs={{0,4},{1,5},{2,6},{3,7},{4,32},{5,33},{6,34},{7,35},{8,12},{9,13},... | collective-permute-start | bytes 516104 | tf_op jit(solution)/shard_map/ppermute | solution.py:500
  66.2 6.7 %encode_decode.2 = (bf16[384,1792]{1,0:T(8,128)(2,1)}, f32[384,128]{1,0:T(8,128)}) custom-call(bf16[384,1792]{1,0:T(8,128)(2,1)} %bitcast.16, bf16[3584,128]{1,0:T(8,128)(2,1)} %refs_5_.1, f32[1,128]{1,0:T(1,128)} %bitcast.31, bf16[128,3584]{1,0:T(8,128)(2,1)} %dec_ref.1), custom_call_target="tpu_custom_call" | custom-call | tf_op jit(solution)/shard_map/encode_decode/pallas_call | solution.py:264
  77.5 6.7 %encode_decode.3 = (bf16[96,1792]{1,0:T(8,128)(2,1)}, bf16[96,1792]{1,0:T(8,128)(2,1)}, bf16[48,1792]{1,0:T(8,128)(2,1)}, bf16[48,1792]{1,0:T(8,128)(2,1)}, bf16...) custom-call(bf16[96,1792]{1,0:T(8,128)(2,1)} %get-tuple-element.76.refs_0_, bf16[96,1792]{1,0:T(8,128)(2,1)} %copy-done.6, ...), custom_call_target="tpu_custom_call" | custom-call | tf_op jit(solution)/shard_map/encode_decode/pallas_call | solution.py:264
  84.1 4.7 %collective-permute-start.8 = (bf16[96,1792]{1,0:T(8,128)(2,1)}, bf16[96,1792]{1,0:T(8,128)(2,1)S(1)}, u32[]{:S(2)}, u32[]{:S(2)}) collective-permute-start(bf16[96,1792]{1,0:T(8,128)(2,1)} %get-tuple-element.84), channel_id=1, source_target_pairs={{0,102},{1,103},{2,0},{3,1},{4,2},{5,3},{6,4},{7,5},{8,110},{9,111... | collective-permute-start | bytes 1032200 | tf_op jit(solution)/shard_map/ppermute | solution.py:500
  99.9 8.8 %collective-permute-done.9.refs_2_ = bf16[48,1792]{1,0:T(8,128)(2,1)S(1)} collective-permute-done((bf16[48,1792]{1,0:T(8,128)(2,1)}, bf16[48,1792]{1,0:T(8,128)(2,1)S(1)}, u32[]{:S(2)}, u32[]{:S(2)}) %collective-permute-start.9) | collective-permute-done | bytes 172064 | tf_op jit(solution)/shard_map/ppermute | solution.py:500
  136.4 5.7 %collective-permute-done.13.refs_2_ = bf16[48,1792]{1,0:T(8,128)(2,1)S(1)} collective-permute-done((bf16[48,1792]{1,0:T(8,128)(2,1)}, bf16[48,1792]{1,0:T(8,128)(2,1)S(1)}, u32[]{:S(2)}, u32[]{:S(2)}) %collective-permute-start.13) | collective-permute-done | bytes 172064 | tf_op jit(solution)/shard_map/ppermute | solution.py:500
  142.1 4.9 %collective-permute-done.14.refs_3_ = bf16[48,1792]{1,0:T(8,128)(2,1)S(1)} collective-permute-done((bf16[48,1792]{1,0:T(8,128)(2,1)}, bf16[48,1792]{1,0:T(8,128)(2,1)S(1)}, u32[]{:S(2)}, u32[]{:S(2)}) %collective-permute-start.14) | collective-permute-done | bytes 172064 | tf_op jit(solution)/shard_map/ppermute | solution.py:500
  148.3 5.7 %error_rows.1 = (bf16[96,1792]{1,0:T(8,128)(2,1)}, bf16[96,1792]{1,0:T(8,128)(2,1)}, bf16[48,1792]{1,0:T(8,128)(2,1)}, bf16[48,1792]{1,0:T(8,128)(2,1)}, bf16[96...) custom-call(s32[2,128]{1,0:T(2,128)} %bitcast.30, f32[1,3584]{1,0:T(1,128)} %broadcast_in_dim.7.bias_ref, ...), custom_call_target="tpu_custom_call" | custom-call | tf_op jit(solution)/shard_map/error_rows/pallas_call | solution.py:321
  154.0 4.6 %all-to-all-start.4 = ((bf16[8,48,1792]{2,1,0:T(8,128)(2,1)}), bf16[8,48,1792]{2,1,0:T(8,128)(2,1)S(1)}, u32[]{:S(2)}, u32[]{:S(2)}) async-start(bf16[8,48,1792]{2,1,0:T(8,128)(2,1)} %bitcast.27), calls=%async_computation.4 | async-start | bytes 2752512 | tf_op jit(solution)/shard_map/all_to_all | solution.py:510
  166.7 5.8 %collective-permute-start.18 = (bf16[48,1792]{1,0:T(8,128)(2,1)S(1)}, bf16[48,1792]{1,0:T(8,128)(2,1)S(1)}, u32[]{:S(2)}, u32[]{:S(2)}) collective-permute-start(bf16[48,1792]{1,0:T(8,128)(2,1)S(1)} %copy-done.41), channel_id=1, source_target_pairs={{0,100},{1,101},{2,102},{3,103},{4,0},{5,1},{6,2},{7,3},{8,108},{9... | collective-permute-start | bytes 516104 | tf_op jit(solution)/shard_map/ppermute | solution.py:500
  172.5 4.9 %collective-permute-done.17.refs_2_ = bf16[48,1792]{1,0:T(8,128)(2,1)S(1)} collective-permute-done((bf16[48,1792]{1,0:T(8,128)(2,1)S(1)}, bf16[48,1792]{1,0:T(8,128)(2,1)S(1)}, u32[]{:S(2)}, u32[]{:S(2)}) %collective-permute-start.17) | collective-permute-done | bytes 172064 | tf_op jit(solution)/shard_map/ppermute | solution.py:500
  185.6 4.6 %all-to-all-start.5 = ((bf16[8,48,1792]{2,1,0:T(8,128)(2,1)}), bf16[8,48,1792]{2,1,0:T(8,128)(2,1)S(1)}, u32[]{:S(2)}, u32[]{:S(2)}) async-start(bf16[8,48,1792]{2,1,0:T(8,128)(2,1)} %bitcast.24), calls=%async_computation.5 | async-start | bytes 2752512 | tf_op jit(solution)/shard_map/all_to_all | solution.py:510
  199.1 5.9 %collective-permute-start.21 = (bf16[48,1792]{1,0:T(8,128)(2,1)}, bf16[48,1792]{1,0:T(8,128)(2,1)S(1)}, u32[]{:S(2)}, u32[]{:S(2)}) collective-permute-start(bf16[48,1792]{1,0:T(8,128)(2,1)} %get-tuple-element.104), channel_id=1, source_target_pairs={{0,4},{1,5},{2,6},{3,7},{4,32},{5,33},{6,34},{7,35},{8,12},{9,13},... | collective-permute-start | bytes 516104 | tf_op jit(solution)/shard_map/ppermute | solution.py:500
  207.0 7.8 %collective-permute-done.21.refs_8_ = bf16[48,1792]{1,0:T(8,128)(2,1)S(1)} collective-permute-done((bf16[48,1792]{1,0:T(8,128)(2,1)}, bf16[48,1792]{1,0:T(8,128)(2,1)S(1)}, u32[]{:S(2)}, u32[]{:S(2)}) %collective-permute-start.21) | collective-permute-done | bytes 172064 | tf_op jit(solution)/shard_map/ppermute | solution.py:500
  217.5 9.3 %gradients.1 = (bf16[272,896]{1,0:T(8,128)(2,1)}, bf16[272,896]{1,0:T(8,128)(2,1)}, bf16[272,896]{1,0:T(8,128)(2,1)}, bf16[272,896]{1,0:T(8,128)(2,1)}) custom-call(f32[384,128]{1,0:T(8,128)} %get-tuple-element.68.pre_a, f32[384,128]{1,0:T(8,128)} %get-tuple-element.81.pre_b, bf16[128,3584]{1,0:T(8,128)(2,1)} %dec_ref.1, ...), custom_call_target="tpu_custom_call" | custom-call | tf_op jit(solution)/shard_map/gradients/pallas_call | solution.py:395
  235.9 7.2 %collective-permute-done.24.refs_1_ = bf16[272,896]{1,0:T(8,128)(2,1)S(1)} collective-permute-done((bf16[272,896]{1,0:T(8,128)(2,1)}, bf16[272,896]{1,0:T(8,128)(2,1)S(1)}, u32[]{:S(2)}, u32[]{:S(2)}) %collective-permute-start.24) | collective-permute-done | bytes 487456 | tf_op jit(solution)/shard_map/ppermute | solution.py:484
  243.0 11.9 %collective-permute-done.25.refs_2_ = bf16[272,896]{1,0:T(8,128)(2,1)S(1)} collective-permute-done((bf16[272,896]{1,0:T(8,128)(2,1)}, bf16[272,896]{1,0:T(8,128)(2,1)S(1)}, u32[]{:S(2)}, u32[]{:S(2)}) %collective-permute-start.25) | collective-permute-done | bytes 487456 | tf_op jit(solution)/shard_map/ppermute | solution.py:484
  258.5 4.9 %collective-permute-start.27 = (bf16[240,256]{1,0:T(8,128)(2,1)}, bf16[240,256]{1,0:T(8,128)(2,1)S(1)}, u32[]{:S(2)}, u32[]{:S(2)}) collective-permute-start(bf16[240,256]{1,0:T(8,128)(2,1)} %get-tuple-element.113), channel_id=1, source_target_pairs={{0,32},{32,64},{64,96},{96,0},{128,160},{160,192},{192,224},{224,1... | collective-permute-start | bytes 368648 | tf_op jit(solution)/shard_map/ppermute | solution.py:484
  263.4 4.8 %collective-permute-start.28 = (bf16[240,256]{1,0:T(8,128)(2,1)}, bf16[240,256]{1,0:T(8,128)(2,1)S(1)}, u32[]{:S(2)}, u32[]{:S(2)}) collective-permute-start(bf16[240,256]{1,0:T(8,128)(2,1)} %get-tuple-element.114), channel_id=1, source_target_pairs={{0,96},{32,0},{64,32},{96,64},{128,224},{160,128},{192,160},{224,1... | collective-permute-start | bytes 368648 | tf_op jit(solution)/shard_map/ppermute | solution.py:484
  268.2 8.1 %collective-permute-start.29 = (bf16[240,256]{1,0:T(8,128)(2,1)}, bf16[240,256]{1,0:T(8,128)(2,1)S(1)}, u32[]{:S(2)}, u32[]{:S(2)}) collective-permute-start(bf16[240,256]{1,0:T(8,128)(2,1)} %get-tuple-element.115), channel_id=1, source_target_pairs={{0,64},{32,96},{64,0},{96,32},{128,192},{160,224},{192,128},{224,1... | collective-permute-start | bytes 368648 | tf_op jit(solution)/shard_map/ppermute | solution.py:484
  276.4 17.0 %collective-permute-done.29.refs_3_ = bf16[240,256]{1,0:T(8,128)(2,1)S(1)} collective-permute-done((bf16[240,256]{1,0:T(8,128)(2,1)}, bf16[240,256]{1,0:T(8,128)(2,1)S(1)}, u32[]{:S(2)}, u32[]{:S(2)}) %collective-permute-start.29) | collective-permute-done | bytes 122912 | tf_op jit(solution)/shard_map/ppermute | solution.py:484
  (152 shorter events, 127.7 us)
Async XLA Ops:
  4.6 35.5 %all-to-all-start = ((bf16[8,48,1792]{2,1,0:T(8,128)(2,1)}), bf16[8,48,1792]{2,1,0:T(8,128)(2,1)S(1)}, u32[]{:S(2)}, u32[]{:S(2)}) async-start(bf16[8,48,1792]{2,1,0:T(8,128)(2,1)} %bitcast.28), calls=%async_computation | async-start | bytes 2752512 | tf_op jit(solution)/shard_map/all_to_all | solution.py:510
  9.0 27.0 %collective-permute-start = (bf16[96,1792]{1,0:T(8,128)(2,1)S(1)}, bf16[96,1792]{1,0:T(8,128)(2,1)S(1)}, u32[]{:S(2)}, u32[]{:S(2)}) collective-permute-start(bf16[96,1792]{1,0:T(8,128)(2,1)S(1)} %copy-done.40), channel_id=1, source_target_pairs={{0,2},{1,3},{2,4},{3,5},{4,6},{5,7},{6,32},{7,33},{8,10},{9,11},{1... | collective-permute-start | bytes 1032200 | tf_op jit(solution)/shard_map/ppermute | solution.py:500
  12.8 23.2 %collective-permute-start.3 = (bf16[96,1792]{1,0:T(8,128)(2,1)S(1)}, bf16[96,1792]{1,0:T(8,128)(2,1)S(1)}, u32[]{:S(2)}, u32[]{:S(2)}) collective-permute-start(bf16[96,1792]{1,0:T(8,128)(2,1)S(1)} %copy-done.39), channel_id=1, source_target_pairs={{0,102},{1,103},{2,0},{3,1},{4,2},{5,3},{6,4},{7,5},{8,110},{9,111... | collective-permute-start | bytes 1032200 | tf_op jit(solution)/shard_map/ppermute | solution.py:500
  14.9 21.2 %collective-permute-start.1 = (bf16[48,1792]{1,0:T(8,128)(2,1)S(1)}, bf16[48,1792]{1,0:T(8,128)(2,1)S(1)}, u32[]{:S(2)}, u32[]{:S(2)}) collective-permute-start(bf16[48,1792]{1,0:T(8,128)(2,1)S(1)} %copy-done.44), channel_id=1, source_target_pairs={{0,4},{1,5},{2,6},{3,7},{4,32},{5,33},{6,34},{7,35},{8,12},{9,13},... | collective-permute-start | bytes 516104 | tf_op jit(solution)/shard_map/ppermute | solution.py:500
  41.2 23.9 %all-to-all-start.1 = ((bf16[8,48,1792]{2,1,0:T(8,128)(2,1)}), bf16[8,48,1792]{2,1,0:T(8,128)(2,1)S(1)}, u32[]{:S(2)}, u32[]{:S(2)}) async-start(bf16[8,48,1792]{2,1,0:T(8,128)(2,1)} %bitcast.25), calls=%async_computation.1 | async-start | bytes 2752512 | tf_op jit(solution)/shard_map/all_to_all | solution.py:510
  48.6 24.3 %collective-permute-start.4 = (bf16[96,1792]{1,0:T(8,128)(2,1)}, bf16[96,1792]{1,0:T(8,128)(2,1)S(1)}, u32[]{:S(2)}, u32[]{:S(2)}) collective-permute-start(bf16[96,1792]{1,0:T(8,128)(2,1)} %get-tuple-element.71), channel_id=1, source_target_pairs={{0,2},{1,3},{2,4},{3,5},{4,6},{5,7},{6,32},{7,33},{8,10},{9,11},{1... | collective-permute-start | bytes 1032200 | tf_op jit(solution)/shard_map/ppermute | solution.py:500
  52.4 20.5 %collective-permute-start.7 = (bf16[96,1792]{1,0:T(8,128)(2,1)}, bf16[96,1792]{1,0:T(8,128)(2,1)S(1)}, u32[]{:S(2)}, u32[]{:S(2)}) collective-permute-start(bf16[96,1792]{1,0:T(8,128)(2,1)} %get-tuple-element.74), channel_id=1, source_target_pairs={{0,102},{1,103},{2,0},{3,1},{4,2},{5,3},{6,4},{7,5},{8,110},{9,111... | collective-permute-start | bytes 1032200 | tf_op jit(solution)/shard_map/ppermute | solution.py:500
  54.4 18.4 %collective-permute-start.5 = (bf16[48,1792]{1,0:T(8,128)(2,1)}, bf16[48,1792]{1,0:T(8,128)(2,1)S(1)}, u32[]{:S(2)}, u32[]{:S(2)}) collective-permute-start(bf16[48,1792]{1,0:T(8,128)(2,1)} %get-tuple-element.72), channel_id=1, source_target_pairs={{0,4},{1,5},{2,6},{3,7},{4,32},{5,33},{6,34},{7,35},{8,12},{9,13},... | collective-permute-start | bytes 516104 | tf_op jit(solution)/shard_map/ppermute | solution.py:500
  73.9 40.0 %all-to-all-start.2 = ((bf16[8,48,1792]{2,1,0:T(8,128)(2,1)}), bf16[8,48,1792]{2,1,0:T(8,128)(2,1)S(1)}, u32[]{:S(2)}, u32[]{:S(2)}) async-start(bf16[8,48,1792]{2,1,0:T(8,128)(2,1)} %bitcast.26), calls=%async_computation.2 | async-start | bytes 2752512 | tf_op jit(solution)/shard_map/all_to_all | solution.py:510
  84.1 25.8 %collective-permute-start.8 = (bf16[96,1792]{1,0:T(8,128)(2,1)}, bf16[96,1792]{1,0:T(8,128)(2,1)S(1)}, u32[]{:S(2)}, u32[]{:S(2)}) collective-permute-start(bf16[96,1792]{1,0:T(8,128)(2,1)} %get-tuple-element.84), channel_id=1, source_target_pairs={{0,102},{1,103},{2,0},{3,1},{4,2},{5,3},{6,4},{7,5},{8,110},{9,111... | collective-permute-start | bytes 1032200 | tf_op jit(solution)/shard_map/ppermute | solution.py:500
  88.9 21.1 %collective-permute-start.11 = (bf16[96,1792]{1,0:T(8,128)(2,1)}, bf16[96,1792]{1,0:T(8,128)(2,1)S(1)}, u32[]{:S(2)}, u32[]{:S(2)}) collective-permute-start(bf16[96,1792]{1,0:T(8,128)(2,1)} %get-tuple-element.87), channel_id=1, source_target_pairs={{0,2},{1,3},{2,4},{3,5},{4,6},{5,7},{6,32},{7,33},{8,10},{9,11},{1... | collective-permute-start | bytes 1032200 | tf_op jit(solution)/shard_map/ppermute | solution.py:500
  115.0 32.0 %all-to-all-start.3 = ((bf16[8,48,1792]{2,1,0:T(8,128)(2,1)}), bf16[8,48,1792]{2,1,0:T(8,128)(2,1)S(1)}, u32[]{:S(2)}, u32[]{:S(2)}) async-start(bf16[8,48,1792]{2,1,0:T(8,128)(2,1)} %bitcast.23), calls=%async_computation.3 | async-start | bytes 2752512 | tf_op jit(solution)/shard_map/all_to_all | solution.py:510
  122.4 24.6 %collective-permute-start.12 = (bf16[96,1792]{1,0:T(8,128)(2,1)}, bf16[96,1792]{1,0:T(8,128)(2,1)S(1)}, u32[]{:S(2)}, u32[]{:S(2)}) collective-permute-start(bf16[96,1792]{1,0:T(8,128)(2,1)} %get-tuple-element.90), channel_id=1, source_target_pairs={{0,102},{1,103},{2,0},{3,1},{4,2},{5,3},{6,4},{7,5},{8,110},{9,111... | collective-permute-start | bytes 1032200 | tf_op jit(solution)/shard_map/ppermute | solution.py:500
  126.3 20.6 %collective-permute-start.15 = (bf16[96,1792]{1,0:T(8,128)(2,1)}, bf16[96,1792]{1,0:T(8,128)(2,1)S(1)}, u32[]{:S(2)}, u32[]{:S(2)}) collective-permute-start(bf16[96,1792]{1,0:T(8,128)(2,1)} %get-tuple-element.93), channel_id=1, source_target_pairs={{0,2},{1,3},{2,4},{3,5},{4,6},{5,7},{6,32},{7,33},{8,10},{9,11},{1... | collective-permute-start | bytes 1032200 | tf_op jit(solution)/shard_map/ppermute | solution.py:500
  154.0 30.5 %all-to-all-start.4 = ((bf16[8,48,1792]{2,1,0:T(8,128)(2,1)}), bf16[8,48,1792]{2,1,0:T(8,128)(2,1)S(1)}, u32[]{:S(2)}, u32[]{:S(2)}) async-start(bf16[8,48,1792]{2,1,0:T(8,128)(2,1)} %bitcast.27), calls=%async_computation.4 | async-start | bytes 2752512 | tf_op jit(solution)/shard_map/all_to_all | solution.py:510
  158.6 22.0 %collective-permute-start.16 = (bf16[96,1792]{1,0:T(8,128)(2,1)S(1)}, bf16[96,1792]{1,0:T(8,128)(2,1)S(1)}, u32[]{:S(2)}, u32[]{:S(2)}) collective-permute-start(bf16[96,1792]{1,0:T(8,128)(2,1)S(1)} %copy-done.38), channel_id=1, source_target_pairs={{0,2},{1,3},{2,4},{3,5},{4,6},{5,7},{6,32},{7,33},{8,10},{9,11},{1... | collective-permute-start | bytes 1032200 | tf_op jit(solution)/shard_map/ppermute | solution.py:500
  160.6 20.0 %collective-permute-start.19 = (bf16[96,1792]{1,0:T(8,128)(2,1)S(1)}, bf16[96,1792]{1,0:T(8,128)(2,1)S(1)}, u32[]{:S(2)}, u32[]{:S(2)}) collective-permute-start(bf16[96,1792]{1,0:T(8,128)(2,1)S(1)} %copy-done.37), channel_id=1, source_target_pairs={{0,102},{1,103},{2,0},{3,1},{4,2},{5,3},{6,4},{7,5},{8,110},{9,111... | collective-permute-start | bytes 1032200 | tf_op jit(solution)/shard_map/ppermute | solution.py:500
  185.6 30.6 %all-to-all-start.5 = ((bf16[8,48,1792]{2,1,0:T(8,128)(2,1)}), bf16[8,48,1792]{2,1,0:T(8,128)(2,1)S(1)}, u32[]{:S(2)}, u32[]{:S(2)}) async-start(bf16[8,48,1792]{2,1,0:T(8,128)(2,1)} %bitcast.24), calls=%async_computation.5 | async-start | bytes 2752512 | tf_op jit(solution)/shard_map/all_to_all | solution.py:510
  193.2 23.0 %collective-permute-start.20 = (bf16[96,1792]{1,0:T(8,128)(2,1)}, bf16[96,1792]{1,0:T(8,128)(2,1)S(1)}, u32[]{:S(2)}, u32[]{:S(2)}) collective-permute-start(bf16[96,1792]{1,0:T(8,128)(2,1)} %get-tuple-element.103), channel_id=1, source_target_pairs={{0,2},{1,3},{2,4},{3,5},{4,6},{5,7},{6,32},{7,33},{8,10},{9,11},{1... | collective-permute-start | bytes 1032200 | tf_op jit(solution)/shard_map/ppermute | solution.py:500
  196.5 19.7 %collective-permute-start.23 = (bf16[96,1792]{1,0:T(8,128)(2,1)}, bf16[96,1792]{1,0:T(8,128)(2,1)S(1)}, u32[]{:S(2)}, u32[]{:S(2)}) collective-permute-start(bf16[96,1792]{1,0:T(8,128)(2,1)} %get-tuple-element.106), channel_id=1, source_target_pairs={{0,102},{1,103},{2,0},{3,1},{4,2},{5,3},{6,4},{7,5},{8,110},{9,111... | collective-permute-start | bytes 1032200 | tf_op jit(solution)/shard_map/ppermute | solution.py:500
  229.0 25.9 %collective-permute-start.25 = (bf16[272,896]{1,0:T(8,128)(2,1)}, bf16[272,896]{1,0:T(8,128)(2,1)S(1)}, u32[]{:S(2)}, u32[]{:S(2)}) collective-permute-start(bf16[272,896]{1,0:T(8,128)(2,1)} %get-tuple-element.110), channel_id=1, source_target_pairs={{0,384},{32,416},{64,448},{96,480},{128,0},{160,32},{192,64},{224,... | collective-permute-start | bytes 1462280 | tf_op jit(solution)/shard_map/ppermute | solution.py:484
  232.7 22.2 %collective-permute-start.26 = (bf16[272,896]{1,0:T(8,128)(2,1)}, bf16[272,896]{1,0:T(8,128)(2,1)S(1)}, u32[]{:S(2)}, u32[]{:S(2)}) collective-permute-start(bf16[272,896]{1,0:T(8,128)(2,1)} %get-tuple-element.111), channel_id=1, source_target_pairs={{0,256},{32,288},{64,320},{96,352},{128,384},{160,416},{192,448},{... | collective-permute-start | bytes 1462280 | tf_op jit(solution)/shard_map/ppermute | solution.py:484
  258.5 17.9 %collective-permute-start.27 = (bf16[240,256]{1,0:T(8,128)(2,1)}, bf16[240,256]{1,0:T(8,128)(2,1)S(1)}, u32[]{:S(2)}, u32[]{:S(2)}) collective-permute-start(bf16[240,256]{1,0:T(8,128)(2,1)} %get-tuple-element.113), channel_id=1, source_target_pairs={{0,32},{32,64},{64,96},{96,0},{128,160},{160,192},{192,224},{224,1... | collective-permute-start | bytes 368648 | tf_op jit(solution)/shard_map/ppermute | solution.py:484
  268.2 25.2 %collective-permute-start.29 = (bf16[240,256]{1,0:T(8,128)(2,1)}, bf16[240,256]{1,0:T(8,128)(2,1)S(1)}, u32[]{:S(2)}, u32[]{:S(2)}) collective-permute-start(bf16[240,256]{1,0:T(8,128)(2,1)} %get-tuple-element.115), channel_id=1, source_target_pairs={{0,64},{32,96},{64,0},{96,32},{128,192},{160,224},{192,128},{224,1... | collective-permute-start | bytes 368648 | tf_op jit(solution)/shard_map/ppermute | solution.py:484
  (57 other events, 339.4 us)

commit v4 on v3

--- a/solution.py
+++ b/solution.py
@@ -10,10 +10,11 @@
 SLOTS = 6
 PAIR = 2 * SLOTS
 SIDE = 4
-STEPS = (0, 1, 2, -2, -1)
+STEPS = ((0, 0), (1, 1), (2, -2), (-1, -1))
 BF = jnp.bfloat16
 F32 = jnp.float32
 VMEM = 56 * 1024 * 1024
+COLS = 256
 PARAMS = pltpu.CompilerParams(vmem_limit_bytes=VMEM)
 ANY = pl.BlockSpec(memory_space=pl.ANY)
 
@@ -91,47 +92,34 @@
         copy.wait()
 
 
-def five_moves(refs, k, first, rows, other):
-    if k != 2:
-        return [(refs[k if k < 2 else 4].at[first : first + rows], other)]
-    part = refs[2].shape[0]
-    return [
-        (refs[2 + h], other.at[h * part - first : (h + 1) * part - first])
-        for h in range(2)
-        if first <= h * part < first + rows
-    ]
-
-
-def flip(pairs):
-    return [(b, a) for a, b in pairs]
-
-
-def send_slots(sel, rows2, pieces, outs, sems):
-    part = pieces.shape[1]
+def send_slots(sel, rows2, slots, outs, sems):
+    total, half = slots.shape
+    rows = total // 2
+    part = rows // SIDE
     copies = []
-    for i in range(2 * SIDE):
-        pieces[i] = dot(sel[i * part : (i + 1) * part, :], rows2[...]).astype(BF)
-        if i < SIDE:
-            pairs = flip(five_moves(outs, i, 0, part, pieces.at[i]))
+    for i in range(2):
+        own = slice(i * rows, (i + 1) * rows)
+        chosen = sel[own, :]
+        for c in range(0, half, COLS):
+            slots[own, c : c + COLS] = dot(chosen, rows2[:, c : c + COLS]).astype(BF)
+        if i == 0:
+            copies += start(
+                [(slots.at[k * part : (k + 1) * part], outs[k]) for k in range(SIDE)], sems
+            )
         else:
-            pairs = [(pieces.at[i], outs[5].at[(i - SIDE) * part : (i - SIDE + 1) * part])]
-        copies += start(pairs, sems, 2 * i)
+            copies += start([(slots.at[rows:], outs[SIDE])], sems, SIDE)
     wait(copies)
-
-
-def five_shapes(total, half):
-    part = total // SIDE
-    rows = [part, part, part // 2, part // 2, part]
-    return [jax.ShapeDtypeStruct((r, half), BF) for r in rows]
 
 
 def slot_shapes(blocks, half):
     total = blocks * PAIR
-    return five_shapes(total, half) + [jax.ShapeDtypeStruct((total, half), BF)]
+    part = total // SIDE
+    shapes = [jax.ShapeDtypeStruct((part, half), BF)] * SIDE
+    return shapes + [jax.ShapeDtypeStruct((total, half), BF)]
 
 
 def pack_kernel(blocks, ids_ref, act_ref, *refs):
-    outs, (act2, sel, pieces, in_sems, sems) = refs[:6], refs[6:]
+    outs, (act2, sel, pieces, in_sems, sems) = refs[: SIDE + 1], refs[SIDE + 1 :]
     n, width = act_ref.shape
     half = width // 2
     copies = start(
@@ -150,14 +138,14 @@
     return pl.pallas_call(
         functools.partial(pack_kernel, blocks),
         in_specs=[pl.BlockSpec(memory_space=pltpu.VMEM), ANY],
-        out_specs=[ANY] * 6,
+        out_specs=[ANY] * (SIDE + 1),
         out_shape=slot_shapes(blocks, half),
         scratch_shapes=[
             pltpu.VMEM((2 * n, half), BF),
             pltpu.VMEM((2 * SIDE * part, 2 * n), BF),
-            pltpu.VMEM((2 * SIDE, part, half), BF),
+            pltpu.VMEM((2 * SIDE * part, half), BF),
             pltpu.SemaphoreType.DMA((2,)),
-            pltpu.SemaphoreType.DMA((4 * SIDE,)),
+            pltpu.SemaphoreType.DMA((SIDE + 1,)),
         ],
         compiler_params=PARAMS,
         name="pack_rows",
@@ -166,21 +154,20 @@
 
 def swap_kernel(merge, *refs):
     if merge:
-        ins, out_ref, (pieces, done, in_sems, sems) = refs[:5], refs[5], refs[6:]
+        ins, out_ref, (pieces, done, in_sems, sems) = refs[:SIDE], refs[SIDE], refs[SIDE + 1 :]
     else:
-        in_ref, outs, (pieces, done, in_sems, sems) = refs[0], refs[1:6], refs[6:]
+        in_ref, outs, (pieces, done, in_sems, sems) = refs[0], refs[1 : SIDE + 1], refs[SIDE + 1 :]
     rows = pieces.shape[1]
     part = rows // SIDE
     halves = range(2)
-
-    def by_step(arrays, buffer, h):
-        pairs = []
-        for k in range(SIDE):
-            pairs += five_moves(arrays, k, h * part, part, buffer.at[h, k * part : (k + 1) * part])
-        return pairs
-
     if merge:
-        moves = [by_step(ins, pieces, h) for h in halves]
+        moves = [
+            [
+                (ins[k].at[h * part : (h + 1) * part], pieces.at[h, k * part : (k + 1) * part])
+                for k in range(SIDE)
+            ]
+            for h in halves
+        ]
     else:
         moves = [[(in_ref.at[h * rows : (h + 1) * rows], pieces.at[h])] for h in halves]
     copies = [start(moves[h], in_sems, h * SIDE) for h in halves]
@@ -195,23 +182,32 @@
         if merge:
             sent += start([(done.at[h], out_ref.at[h * rows : (h + 1) * rows])], sems, h * SIDE)
         else:
-            sent += start(flip(by_step(outs, done, h)), sems, h * SIDE)
+            sent += start(
+                [
+                    (done.at[h, k * part : (k + 1) * part], outs[k].at[h * part : (h + 1) * part])
+                    for k in range(SIDE)
+                ],
+                sems,
+                h * SIDE,
+            )
     wait(sent)
 
 
 def swap_pieces(arrays, merge):
-    total = sum(a.shape[0] for a in arrays)
+    total = arrays[0].shape[0] * (SIDE if merge else 1)
     half = arrays[0].shape[1]
+    shape = jax.ShapeDtypeStruct((total, half), BF)
+    shapes = [jax.ShapeDtypeStruct((total // SIDE, half), BF)] * SIDE
     return pl.pallas_call(
         functools.partial(swap_kernel, merge),
         in_specs=[ANY] * len(arrays),
-        out_specs=ANY if merge else [ANY] * 5,
-        out_shape=jax.ShapeDtypeStruct((total, half), BF) if merge else five_shapes(total, half),
+        out_specs=ANY if merge else [ANY] * SIDE,
+        out_shape=shape if merge else shapes,
         scratch_shapes=[
             pltpu.VMEM((2, total // 2, half), BF),
             pltpu.VMEM((2, total // 2, half), BF),
-            pltpu.SemaphoreType.DMA((4 * SIDE,)),
-            pltpu.SemaphoreType.DMA((4 * SIDE,)),
+            pltpu.SemaphoreType.DMA((2 * SIDE,)),
+            pltpu.SemaphoreType.DMA((2 * SIDE,)),
         ],
         compiler_params=PARAMS,
         name="merge_pieces" if merge else "split_pieces",
@@ -223,36 +219,32 @@
     outs, pre_ref = refs[parts + 3 : 2 * parts + 3], refs[2 * parts + 3]
     enc2, dec2, x, done, w_sems, in_sems, sems = refs[2 * parts + 4 :]
     half, n = enc2.shape[0], enc2.shape[1] // 2
-    rows = x.shape[1]
-
-    def piece(refs, i, buffer):
-        if parts == 1:
-            return [(refs[0].at[i * rows : (i + 1) * rows], buffer.at[i])]
-        return five_moves(refs, i, 0, rows, buffer.at[i])
+    total = x.shape[0]
+    rows = total // parts
+
+    def moves(refs, buffer):
+        return [(refs[i], buffer.at[i * rows : (i + 1) * rows]) for i in range(parts)]
 
     enc_copies = start(
         [(enc_ref.at[s * half : (s + 1) * half], enc2.at[:, s * n : (s + 1) * n]) for s in range(2)],
         w_sems,
     )
-    in_copies = [start(piece(ins, i, x), in_sems, 2 * i) for i in range(SIDE)]
+    in_copies = start(moves(ins, x), in_sems)
     dec_copies = start(
         [(dec_ref.at[:, s * half : (s + 1) * half], dec2.at[s * n : (s + 1) * n]) for s in range(2)],
         w_sems,
         2,
     )
-    left = left_rows(rows)
+    left = left_rows(total)
     wait(enc_copies)
-    sent = []
-    for i in range(SIDE):
-        wait(in_copies[i])
-        pre = join_halves(dot(x[i], enc2[...]), left) + bias_ref[...]
-        pre_ref[i * rows : (i + 1) * rows, :] = pre
-        codes = split_halves(pre * jax.nn.sigmoid(pre), left).astype(BF)
-        if i == 0:
-            wait(dec_copies)
-        done[i] = dot(codes, dec2[...]).astype(BF)
-        sent += start(flip(piece(outs, i, done)), sems, 2 * i)
-    wait(sent)
+    wait(in_copies)
+    pre = join_halves(dot(x[...], enc2[...]), left) + bias_ref[...]
+    pre_ref[...] = pre
+    codes = split_halves(pre * jax.nn.sigmoid(pre), left).astype(BF)
+    wait(dec_copies)
+    for c in range(0, half, COLS):
+        done[:, c : c + COLS] = dot(codes, dec2[:, c : c + COLS]).astype(BF)
+    wait(start([(b, a) for a, b in moves(outs, done)], sems))
 
 
 def encode_decode(x, enc, bias, dec):
@@ -260,7 +252,6 @@
     half = width // 2
     parts = len(x)
     total = sum(a.shape[0] for a in x)
-    rows = total // SIDE
     return pl.pallas_call(
         functools.partial(code_kernel, parts),
         in_specs=[ANY] * (parts + 1) + [pl.BlockSpec(memory_space=pltpu.VMEM), ANY],
@@ -270,11 +261,11 @@
         scratch_shapes=[
             pltpu.VMEM((half, 2 * n), BF),
             pltpu.VMEM((2 * n, half), BF),
-            pltpu.VMEM((SIDE, rows, half), BF),
-            pltpu.VMEM((SIDE, rows, half), BF),
+            pltpu.VMEM((total, half), BF),
+            pltpu.VMEM((total, half), BF),
             pltpu.SemaphoreType.DMA((4,)),
-            pltpu.SemaphoreType.DMA((2 * SIDE,)),
-            pltpu.SemaphoreType.DMA((2 * SIDE,)),
+            pltpu.SemaphoreType.DMA((SIDE,)),
+            pltpu.SemaphoreType.DMA((SIDE,)),
         ],
         compiler_params=PARAMS,
         name="encode_decode",
@@ -283,15 +274,13 @@
 
 def slot_moves(refs, buffer):
     part = refs[0].shape[0]
-    pairs = []
-    for k in range(SIDE):
-        pairs += five_moves(refs, k, 0, part, buffer.at[k * part : (k + 1) * part])
-    return pairs + [(refs[5], buffer.at[SIDE * part :])]
+    pairs = [(refs[k], buffer.at[k * part : (k + 1) * part]) for k in range(SIDE)]
+    return pairs + [(refs[SIDE], buffer.at[SIDE * part :])]
 
 
 def error_kernel(blocks, ids_ref, bias_ref, act_ref, *refs):
-    ins, outs = refs[:6], refs[6:12]
-    act2, back, sel, err2, pieces, act_sems, in_sems, sems = refs[12:]
+    ins, outs = refs[: SIDE + 1], refs[SIDE + 1 : 2 * SIDE + 2]
+    act2, back, sel, err2, pieces, act_sems, in_sems, sems = refs[2 * SIDE + 2 :]
     n, width = act_ref.shape
     half = width // 2
     copies = start(slot_moves(ins, back), in_sems)
@@ -301,7 +290,7 @@
     )
     sel[...] = one_hot_slots(ids_ref[...], blocks)
     wait(copies)
-    step = 256
+    step = COLS
     for c in range(0, half, step):
         sums = dot_t(sel[...], back[:, c : c + step])
         for s in range(2):
@@ -316,22 +305,21 @@
     n, width = act.shape
     half = width // 2
     total = 2 * blocks * PAIR
-    part = total // (2 * SIDE)
     in_vmem = pl.BlockSpec(memory_space=pltpu.VMEM)
     return pl.pallas_call(
         functools.partial(error_kernel, blocks),
-        in_specs=[in_vmem, in_vmem] + [ANY] * 7,
-        out_specs=[ANY] * 6,
+        in_specs=[in_vmem, in_vmem] + [ANY] * (SIDE + 2),
+        out_specs=[ANY] * (SIDE + 1),
         out_shape=slot_shapes(blocks, half),
         scratch_shapes=[
             pltpu.VMEM((2 * n, half), BF),
             pltpu.VMEM((total, half), BF),
             pltpu.VMEM((total, 2 * n), BF),
             pltpu.VMEM((2 * n, half), BF),
-            pltpu.VMEM((2 * SIDE, part, half), BF),
+            pltpu.VMEM((total, half), BF),
             pltpu.SemaphoreType.DMA((2,)),
-            pltpu.SemaphoreType.DMA((6,)),
-            pltpu.SemaphoreType.DMA((4 * SIDE,)),
+            pltpu.SemaphoreType.DMA((SIDE + 1,)),
+            pltpu.SemaphoreType.DMA((SIDE + 1,)),
         ],
         compiler_params=PARAMS,
         name="error_rows",
@@ -345,8 +333,8 @@
 
 
 def grad_kernel(pre_a, pre_b, dec_ref, *refs):
-    x_refs, e_refs, outs = refs[:6], refs[6:12], refs[12:16]
-    dec2, x, e, pieces, w_sems, x_sems, e_sems, sems = refs[16:]
+    x_refs, e_refs, outs = refs[: SIDE + 1], refs[SIDE + 1 : 2 * SIDE + 2], refs[2 * SIDE + 2 : 3 * SIDE + 2]
+    dec2, x, e, pieces, w_sems, x_sems, e_sems, sems = refs[3 * SIDE + 2 :]
     rows, half = x.shape
     n = pre_a.shape[1]
     groups, _, quarter = pieces.shape
@@ -394,7 +382,7 @@
     in_vmem = pl.BlockSpec(memory_space=pltpu.VMEM)
     return pl.pallas_call(
         grad_kernel,
-        in_specs=[in_vmem, in_vmem] + [ANY] * 13,
+        in_specs=[in_vmem, in_vmem] + [ANY] * (2 * SIDE + 3),
         out_shape=[jax.ShapeDtypeStruct(piece, BF)] * SIDE,
         out_specs=[ANY] * SIDE,
         scratch_shapes=[
@@ -403,8 +391,8 @@
             pltpu.VMEM((rows, width // 2), BF),
             pltpu.VMEM((SIDE,) + piece, BF),
             pltpu.SemaphoreType.DMA((2,)),
-            pltpu.SemaphoreType.DMA((6,)),
-            pltpu.SemaphoreType.DMA((6,)),
+            pltpu.SemaphoreType.DMA((SIDE + 1,)),
+            pltpu.SemaphoreType.DMA((SIDE + 1,)),
             pltpu.SemaphoreType.DMA((SIDE,)),
         ],
         compiler_params=PARAMS,
@@ -485,8 +473,8 @@
     return got
 
 
-def along_z(x, step):
-    if step == 0:
+def along_z(x, steps, back=False):
+    if steps[0] == 0:
         return x
     pairs = []
     for i in range(512):
@@ -494,6 +482,7 @@
         y, z_hi = divmod(rows, SIDE)
         x_place, rest = divmod(lat, 2 * SIDE)
         z_lo, core = divmod(rest, 2)
+        step = -steps[core] if back else steps[core]
         z = (z_hi * SIDE + z_lo + step) % (SIDE * SIDE)
         to_rows = y * SIDE + z // SIDE
         pairs.append((i, to_rows * 32 + x_place * 2 * SIDE + z % SIDE * 2 + core))
@@ -519,18 +508,18 @@
 
 
 def to_owners(slots):
-    moved = [along_z(a, step) for a, step in zip(slots[:5], STEPS)]
-    crossed, merged = lax.optimization_barrier((over_x(slots[5]), swap_pieces(moved, True)))
+    moved = [along_z(a, steps) for a, steps in zip(slots[:SIDE], STEPS)]
+    crossed, merged = lax.optimization_barrier((over_x(slots[SIDE]), swap_pieces(moved, True)))
     stream_a = over_x(merged)
-    stream_b = [along_z(a, step) for a, step in zip(swap_pieces([crossed], False), STEPS)]
+    stream_b = [along_z(a, steps) for a, steps in zip(swap_pieces([crossed], False), STEPS)]
     return stream_a, stream_b
 
 
 def to_homes(stream_a, stream_b):
-    moved = [along_z(a, -step) for a, step in zip(stream_b, STEPS)]
+    moved = [along_z(a, steps, True) for a, steps in zip(stream_b, STEPS)]
     crossed, merged = lax.optimization_barrier((over_x(stream_a), swap_pieces(moved, True)))
     home_b = over_x(merged)
-    home_a = [along_z(a, -step) for a, step in zip(swap_pieces([crossed], False), STEPS)]
+    home_a = [along_z(a, steps, True) for a, steps in zip(swap_pieces([crossed], False), STEPS)]
     return [*home_a, home_b]
 
 

time: 298 us -> 299 us (level)
  the two profiles are of different devices: /device:TPU:56 before, /device:TPU:1 now
where the time goes in v4:
time: 299 us; the launch traced here: 294 us
  starting transfers between devices  117 us (39%)
  waiting for transfers between devices  111 us (37%)
  Pallas kernels  52.8 us (18%)
  local copies, waits for them, and re-layouts  12.3 us (4%)
    ppermute x18, waiting for transfers between devices, along_z(): return lax.ppermute(x, ('rows', 'lat'), pairs)  72.1 us
    ppermute x18, starting transfers between devices, along_z(): return lax.ppermute(x, ('rows', 'lat'), pairs)  55.8 us
    all_to_all x6, starting transfers between devices, over_x(): lax.all_to_all(x.reshape(members, shape[0] // members, shape[1]), 'lat',...  33.9 us
    ppermute x6, waiting for transfers between devices, share_pieces(): got.append(lax.ppermute(pieces[k], 'rows', pairs))  33.3 us
    ppermute x6, starting transfers between devices, share_pieces(): got.append(lax.ppermute(pieces[k], 'rows', pairs))  26.8 us
    pallas_call x6, Pallas kernels, swap_pieces(): pl.pallas_call(functools.partial(swap_kernel, merge), in_specs=[ANY] * le...  17.2 us
    pallas_call x2, Pallas kernels, encode_decode(): pl.pallas_call(functools.partial(code_kernel, parts), in_specs=[ANY] * (p...  12 us
    unnamed x74, local copies, waits for them, and re-layouts  11.6 us
  transfers between devices with their start and end apart: 30, of which 21 were waited for; matrix products, arithmetic and copies ran while one was open for 0% of the time, Pallas kernels for 10%

profile of v4, /device:TPU:1, one launch (start us, length us, event | category | flops | bytes accessed | tf_op | source)
XLA Modules:
  0.0 293.8 jit_solution(5207486881744089896)
XLA Ops:
  4.7 10.5 %all-to-all-start = ((bf16[8,48,1792]{2,1,0:T(8,128)(2,1)}), bf16[8,48,1792]{2,1,0:T(8,128)(2,1)S(1)}, u32[]{:S(2)}, u32[]{:S(2)}) async-start(bf16[8,48,1792]{2,1,0:T(8,128)(2,1)} %bitcast.28), calls=%async_computation | async-start | bytes 2752512 | tf_op jit(solution)/shard_map/all_to_all | solution.py:499
  17.1 7.7 %collective-permute-start.1 = (bf16[96,1792]{1,0:T(8,128)(2,1)S(1)}, bf16[96,1792]{1,0:T(8,128)(2,1)S(1)}, u32[]{:S(2)}, u32[]{:S(2)}) collective-permute-start(bf16[96,1792]{1,0:T(8,128)(2,1)S(1)} %copy-done.35), channel_id=1, source_target_pairs={{0,4},{1,101},{2,6},{3,103},{4,32},{5,1},{6,34},{7,3},{8,12},{9,10... | collective-permute-start | bytes 1032200 | tf_op jit(solution)/shard_map/ppermute | solution.py:489
  30.2 5.4 %collective-permute-done.1.refs_2_ = bf16[96,1792]{1,0:T(8,128)(2,1)S(1)} collective-permute-done((bf16[96,1792]{1,0:T(8,128)(2,1)S(1)}, bf16[96,1792]{1,0:T(8,128)(2,1)S(1)}, u32[]{:S(2)}, u32[]{:S(2)}) %collective-permute-start.1) | collective-permute-done | bytes 344096 | tf_op jit(solution)/shard_map/ppermute | solution.py:489
  54.2 6.2 %collective-permute-start.4 = (bf16[96,1792]{1,0:T(8,128)(2,1)}, bf16[96,1792]{1,0:T(8,128)(2,1)S(1)}, u32[]{:S(2)}, u32[]{:S(2)}) collective-permute-start(bf16[96,1792]{1,0:T(8,128)(2,1)} %get-tuple-element.64), channel_id=1, source_target_pairs={{0,4},{1,101},{2,6},{3,103},{4,32},{5,1},{6,34},{7,3},{8,12},{9,10... | collective-permute-start | bytes 1032200 | tf_op jit(solution)/shard_map/ppermute | solution.py:489
  62.3 5.7 %all-to-all-done.1 = bf16[8,48,1792]{2,1,0:T(8,128)(2,1)S(1)} async-done(((bf16[8,48,1792]{2,1,0:T(8,128)(2,1)}), bf16[8,48,1792]{2,1,0:T(8,128)(2,1)S(1)}, u32[]{:S(2)}, u32[]{:S(2)}) %all-to-all-start.1) | async-done | bytes 1376288 | tf_op jit(solution)/shard_map/all_to_all | solution.py:499
  69.1 6.1 %encode_decode.2 = (bf16[384,1792]{1,0:T(8,128)(2,1)}, f32[384,128]{1,0:T(8,128)}) custom-call(bf16[384,1792]{1,0:T(8,128)(2,1)} %bitcast.16, bf16[3584,128]{1,0:T(8,128)(2,1)} %refs_4_.1, f32[1,128]{1,0:T(1,128)} %bitcast.31, bf16[128,3584]{1,0:T(8,128)(2,1)} %dec_ref.1), custom_call_target="tpu_custom_call" | custom-call | tf_op jit(solution)/shard_map/encode_decode/pallas_call | solution.py:255
  81.2 6.0 %encode_decode.3 = (bf16[96,1792]{1,0:T(8,128)(2,1)}, bf16[96,1792]{1,0:T(8,128)(2,1)}, bf16[96,1792]{1,0:T(8,128)(2,1)}, bf16[96,1792]{1,0:T(8,128)(2,1)}, f32[384,128]{1,0:T(8,128)}) custom-call(bf16[96,1792]{1,0:T(8,128)(2,1)} %get-tuple-element.67.refs_0_, bf16[96,1792]{1,0:T(8,128)(2,1)} %copy-done.6, bf16[96,1792]{1,0:T(8,128)(2,1)} %copy-done.7, ...), custom_call_target="tpu_custom_call" | custom-call | tf_op jit(solution)/shard_map/encode_decode/pallas_call | solution.py:255
  87.2 4.9 %collective-permute-start.6 = (bf16[96,1792]{1,0:T(8,128)(2,1)}, bf16[96,1792]{1,0:T(8,128)(2,1)S(1)}, u32[]{:S(2)}, u32[]{:S(2)}) collective-permute-start(bf16[96,1792]{1,0:T(8,128)(2,1)} %get-tuple-element.74), channel_id=1, source_target_pairs={{0,102},{1,103},{2,0},{3,1},{4,2},{5,3},{6,4},{7,5},{8,110},{9,111... | collective-permute-start | bytes 1032200 | tf_op jit(solution)/shard_map/ppermute | solution.py:489
  96.0 6.1 %collective-permute-done.6.refs_1_ = bf16[96,1792]{1,0:T(8,128)(2,1)S(1)} collective-permute-done((bf16[96,1792]{1,0:T(8,128)(2,1)}, bf16[96,1792]{1,0:T(8,128)(2,1)S(1)}, u32[]{:S(2)}, u32[]{:S(2)}) %collective-permute-start.6) | collective-permute-done | bytes 344096 | tf_op jit(solution)/shard_map/ppermute | solution.py:489
  102.1 5.8 %collective-permute-done.7.refs_2_ = bf16[96,1792]{1,0:T(8,128)(2,1)S(1)} collective-permute-done((bf16[96,1792]{1,0:T(8,128)(2,1)}, bf16[96,1792]{1,0:T(8,128)(2,1)S(1)}, u32[]{:S(2)}, u32[]{:S(2)}) %collective-permute-start.7) | collective-permute-done | bytes 344096 | tf_op jit(solution)/shard_map/ppermute | solution.py:489
  115.7 5.0 %all-to-all-start.3 = ((bf16[8,48,1792]{2,1,0:T(8,128)(2,1)}), bf16[8,48,1792]{2,1,0:T(8,128)(2,1)S(1)}, u32[]{:S(2)}, u32[]{:S(2)}) async-start(bf16[8,48,1792]{2,1,0:T(8,128)(2,1)} %bitcast.23), calls=%async_computation.3 | async-start | bytes 2752512 | tf_op jit(solution)/shard_map/all_to_all | solution.py:499
  135.4 6.7 %collective-permute-done.10.refs_2_ = bf16[96,1792]{1,0:T(8,128)(2,1)S(1)} collective-permute-done((bf16[96,1792]{1,0:T(8,128)(2,1)}, bf16[96,1792]{1,0:T(8,128)(2,1)S(1)}, u32[]{:S(2)}, u32[]{:S(2)}) %collective-permute-start.10) | collective-permute-done | bytes 344096 | tf_op jit(solution)/shard_map/ppermute | solution.py:489
  142.1 5.0 %collective-permute-done.11.refs_3_ = bf16[96,1792]{1,0:T(8,128)(2,1)S(1)} collective-permute-done((bf16[96,1792]{1,0:T(8,128)(2,1)}, bf16[96,1792]{1,0:T(8,128)(2,1)S(1)}, u32[]{:S(2)}, u32[]{:S(2)}) %collective-permute-start.11) | collective-permute-done | bytes 344096 | tf_op jit(solution)/shard_map/ppermute | solution.py:489
  148.4 5.8 %error_rows.1 = (bf16[96,1792]{1,0:T(8,128)(2,1)}, bf16[96,1792]{1,0:T(8,128)(2,1)}, bf16[96,1792]{1,0:T(8,128)(2,1)}, bf16[96,1792]{1,0:T(8,128)(2,1)}, bf16[384,1792]{1,0:T(8,128)(2,1)}) custom-call(s32[2,128]{1,0:T(2,128)} %bitcast.30, f32[1,3584]{1,0:T(1,128)} %broadcast_in_dim.7.bias_ref, bf16[128,3584]{1,0:T(8,128)(2,1)} %act_ref.3, ...), custom_call_target="tpu_custom_call" | custom-call | tf_op jit(solution)/shard_map/error_rows/pallas_call | solution.py:309
  172.4 8.9 %collective-permute-done.14.refs_3_ = bf16[96,1792]{1,0:T(8,128)(2,1)S(1)} collective-permute-done((bf16[96,1792]{1,0:T(8,128)(2,1)S(1)}, bf16[96,1792]{1,0:T(8,128)(2,1)S(1)}, u32[]{:S(2)}, u32[]{:S(2)}) %collective-permute-start.14) | collective-permute-done | bytes 344096 | tf_op jit(solution)/shard_map/ppermute | solution.py:489
  195.5 5.1 %collective-permute-start.16 = (bf16[96,1792]{1,0:T(8,128)(2,1)}, bf16[96,1792]{1,0:T(8,128)(2,1)S(1)}, u32[]{:S(2)}, u32[]{:S(2)}) collective-permute-start(bf16[96,1792]{1,0:T(8,128)(2,1)} %get-tuple-element.91), channel_id=1, source_target_pairs={{0,4},{1,101},{2,6},{3,103},{4,32},{5,1},{6,34},{7,3},{8,12},{9,10... | collective-permute-start | bytes 1032200 | tf_op jit(solution)/shard_map/ppermute | solution.py:489
  210.5 6.6 %collective-permute-done.17.refs_8_ = bf16[96,1792]{1,0:T(8,128)(2,1)S(1)} collective-permute-done((bf16[96,1792]{1,0:T(8,128)(2,1)}, bf16[96,1792]{1,0:T(8,128)(2,1)S(1)}, u32[]{:S(2)}, u32[]{:S(2)}) %collective-permute-start.17) | collective-permute-done | bytes 344096 | tf_op jit(solution)/shard_map/ppermute | solution.py:489
  218.3 9.3 %gradients.1 = (bf16[272,896]{1,0:T(8,128)(2,1)}, bf16[272,896]{1,0:T(8,128)(2,1)}, bf16[272,896]{1,0:T(8,128)(2,1)}, bf16[272,896]{1,0:T(8,128)(2,1)}) custom-call(f32[384,128]{1,0:T(8,128)} %get-tuple-element.60.pre_a, f32[384,128]{1,0:T(8,128)} %get-tuple-element.71.pre_b, bf16[128,3584]{1,0:T(8,128)(2,1)} %dec_ref.1, ...), custom_call_target="tpu_custom_call" | custom-call | tf_op jit(solution)/shard_map/gradients/pallas_call | solution.py:383
  237.5 5.5 %collective-permute-done.18.refs_1_ = bf16[272,896]{1,0:T(8,128)(2,1)S(1)} collective-permute-done((bf16[272,896]{1,0:T(8,128)(2,1)}, bf16[272,896]{1,0:T(8,128)(2,1)S(1)}, u32[]{:S(2)}, u32[]{:S(2)}) %collective-permute-start.18) | collective-permute-done | bytes 487456 | tf_op jit(solution)/shard_map/ppermute | solution.py:472
  243.0 12.0 %collective-permute-done.19.refs_2_ = bf16[272,896]{1,0:T(8,128)(2,1)S(1)} collective-permute-done((bf16[272,896]{1,0:T(8,128)(2,1)}, bf16[272,896]{1,0:T(8,128)(2,1)S(1)}, u32[]{:S(2)}, u32[]{:S(2)}) %collective-permute-start.19) | collective-permute-done | bytes 487456 | tf_op jit(solution)/shard_map/ppermute | solution.py:472
  261.5 6.3 %collective-permute-start.22 = (bf16[240,256]{1,0:T(8,128)(2,1)}, bf16[240,256]{1,0:T(8,128)(2,1)S(1)}, u32[]{:S(2)}, u32[]{:S(2)}) collective-permute-start(bf16[240,256]{1,0:T(8,128)(2,1)} %get-tuple-element.100), channel_id=1, source_target_pairs={{0,96},{32,0},{64,32},{96,64},{128,224},{160,128},{192,160},{224,1... | collective-permute-start | bytes 368648 | tf_op jit(solution)/shard_map/ppermute | solution.py:472
  267.9 7.7 %collective-permute-start.23 = (bf16[240,256]{1,0:T(8,128)(2,1)}, bf16[240,256]{1,0:T(8,128)(2,1)S(1)}, u32[]{:S(2)}, u32[]{:S(2)}) collective-permute-start(bf16[240,256]{1,0:T(8,128)(2,1)} %get-tuple-element.101), channel_id=1, source_target_pairs={{0,64},{32,96},{64,0},{96,32},{128,192},{160,224},{192,128},{224,1... | collective-permute-start | bytes 368648 | tf_op jit(solution)/shard_map/ppermute | solution.py:472
  277.0 5.4 %collective-permute-done.22.refs_2_ = bf16[240,256]{1,0:T(8,128)(2,1)S(1)} collective-permute-done((bf16[240,256]{1,0:T(8,128)(2,1)}, bf16[240,256]{1,0:T(8,128)(2,1)S(1)}, u32[]{:S(2)}, u32[]{:S(2)}) %collective-permute-start.22) | collective-permute-done | bytes 122912 | tf_op jit(solution)/shard_map/ppermute | solution.py:472
  282.4 9.0 %collective-permute-done.23.refs_3_ = bf16[240,256]{1,0:T(8,128)(2,1)S(1)} collective-permute-done((bf16[240,256]{1,0:T(8,128)(2,1)}, bf16[240,256]{1,0:T(8,128)(2,1)S(1)}, u32[]{:S(2)}, u32[]{:S(2)}) %collective-permute-start.23) | collective-permute-done | bytes 122912 | tf_op jit(solution)/shard_map/ppermute | solution.py:472
  (124 shorter events, 130.0 us)
Async XLA Ops:
  4.7 39.0 %all-to-all-start = ((bf16[8,48,1792]{2,1,0:T(8,128)(2,1)}), bf16[8,48,1792]{2,1,0:T(8,128)(2,1)S(1)}, u32[]{:S(2)}, u32[]{:S(2)}) async-start(bf16[8,48,1792]{2,1,0:T(8,128)(2,1)} %bitcast.28), calls=%async_computation | async-start | bytes 2752512 | tf_op jit(solution)/shard_map/all_to_all | solution.py:499
  17.1 18.5 %collective-permute-start.1 = (bf16[96,1792]{1,0:T(8,128)(2,1)S(1)}, bf16[96,1792]{1,0:T(8,128)(2,1)S(1)}, u32[]{:S(2)}, u32[]{:S(2)}) collective-permute-start(bf16[96,1792]{1,0:T(8,128)(2,1)S(1)} %copy-done.35), channel_id=1, source_target_pairs={{0,4},{1,101},{2,6},{3,103},{4,32},{5,1},{6,34},{7,3},{8,12},{9,10... | collective-permute-start | bytes 1032200 | tf_op jit(solution)/shard_map/ppermute | solution.py:489
  24.9 15.2 %collective-permute-start.2 = (bf16[96,1792]{1,0:T(8,128)(2,1)S(1)}, bf16[96,1792]{1,0:T(8,128)(2,1)S(1)}, u32[]{:S(2)}, u32[]{:S(2)}) collective-permute-start(bf16[96,1792]{1,0:T(8,128)(2,1)S(1)} %copy-done.33), channel_id=1, source_target_pairs={{0,102},{1,103},{2,0},{3,1},{4,2},{5,3},{6,4},{7,5},{8,110},{9,111... | collective-permute-start | bytes 1032200 | tf_op jit(solution)/shard_map/ppermute | solution.py:489
  44.9 23.2 %all-to-all-start.1 = ((bf16[8,48,1792]{2,1,0:T(8,128)(2,1)}), bf16[8,48,1792]{2,1,0:T(8,128)(2,1)S(1)}, u32[]{:S(2)}, u32[]{:S(2)}) async-start(bf16[8,48,1792]{2,1,0:T(8,128)(2,1)} %bitcast.25), calls=%async_computation.1 | async-start | bytes 2752512 | tf_op jit(solution)/shard_map/all_to_all | solution.py:499
  52.3 22.9 %collective-permute-start.3 = (bf16[96,1792]{1,0:T(8,128)(2,1)}, bf16[96,1792]{1,0:T(8,128)(2,1)S(1)}, u32[]{:S(2)}, u32[]{:S(2)}) collective-permute-start(bf16[96,1792]{1,0:T(8,128)(2,1)} %get-tuple-element.63), channel_id=1, source_target_pairs={{0,2},{1,3},{2,4},{3,5},{4,6},{5,7},{6,32},{7,33},{8,10},{9,11},{1... | collective-permute-start | bytes 1032200 | tf_op jit(solution)/shard_map/ppermute | solution.py:489
  54.2 21.0 %collective-permute-start.4 = (bf16[96,1792]{1,0:T(8,128)(2,1)}, bf16[96,1792]{1,0:T(8,128)(2,1)S(1)}, u32[]{:S(2)}, u32[]{:S(2)}) collective-permute-start(bf16[96,1792]{1,0:T(8,128)(2,1)} %get-tuple-element.64), channel_id=1, source_target_pairs={{0,4},{1,101},{2,6},{3,103},{4,32},{5,1},{6,34},{7,3},{8,12},{9,10... | collective-permute-start | bytes 1032200 | tf_op jit(solution)/shard_map/ppermute | solution.py:489
  60.4 15.5 %collective-permute-start.5 = (bf16[96,1792]{1,0:T(8,128)(2,1)}, bf16[96,1792]{1,0:T(8,128)(2,1)S(1)}, u32[]{:S(2)}, u32[]{:S(2)}) collective-permute-start(bf16[96,1792]{1,0:T(8,128)(2,1)} %get-tuple-element.65), channel_id=1, source_target_pairs={{0,102},{1,103},{2,0},{3,1},{4,2},{5,3},{6,4},{7,5},{8,110},{9,111... | collective-permute-start | bytes 1032200 | tf_op jit(solution)/shard_map/ppermute | solution.py:489
  76.7 37.9 %all-to-all-start.2 = ((bf16[8,48,1792]{2,1,0:T(8,128)(2,1)}), bf16[8,48,1792]{2,1,0:T(8,128)(2,1)S(1)}, u32[]{:S(2)}, u32[]{:S(2)}) async-start(bf16[8,48,1792]{2,1,0:T(8,128)(2,1)} %bitcast.26), calls=%async_computation.2 | async-start | bytes 2752512 | tf_op jit(solution)/shard_map/all_to_all | solution.py:499
  92.1 15.7 %collective-permute-start.7 = (bf16[96,1792]{1,0:T(8,128)(2,1)}, bf16[96,1792]{1,0:T(8,128)(2,1)S(1)}, u32[]{:S(2)}, u32[]{:S(2)}) collective-permute-start(bf16[96,1792]{1,0:T(8,128)(2,1)} %get-tuple-element.75), channel_id=1, source_target_pairs={{0,100},{1,5},{2,102},{3,7},{4,0},{5,33},{6,2},{7,35},{8,108},{9,1... | collective-permute-start | bytes 1032200 | tf_op jit(solution)/shard_map/ppermute | solution.py:489
  94.1 16.8 %collective-permute-start.8 = (bf16[96,1792]{1,0:T(8,128)(2,1)}, bf16[96,1792]{1,0:T(8,128)(2,1)S(1)}, u32[]{:S(2)}, u32[]{:S(2)}) collective-permute-start(bf16[96,1792]{1,0:T(8,128)(2,1)} %get-tuple-element.76), channel_id=1, source_target_pairs={{0,2},{1,3},{2,4},{3,5},{4,6},{5,7},{6,32},{7,33},{8,10},{9,11},{1... | collective-permute-start | bytes 1032200 | tf_op jit(solution)/shard_map/ppermute | solution.py:489
  115.7 31.5 %all-to-all-start.3 = ((bf16[8,48,1792]{2,1,0:T(8,128)(2,1)}), bf16[8,48,1792]{2,1,0:T(8,128)(2,1)S(1)}, u32[]{:S(2)}, u32[]{:S(2)}) async-start(bf16[8,48,1792]{2,1,0:T(8,128)(2,1)} %bitcast.23), calls=%async_computation.3 | async-start | bytes 2752512 | tf_op jit(solution)/shard_map/all_to_all | solution.py:499
  126.7 15.5 %collective-permute-start.10 = (bf16[96,1792]{1,0:T(8,128)(2,1)}, bf16[96,1792]{1,0:T(8,128)(2,1)S(1)}, u32[]{:S(2)}, u32[]{:S(2)}) collective-permute-start(bf16[96,1792]{1,0:T(8,128)(2,1)} %get-tuple-element.80), channel_id=1, source_target_pairs={{0,100},{1,5},{2,102},{3,7},{4,0},{5,33},{6,2},{7,35},{8,108},{9,1... | collective-permute-start | bytes 1032200 | tf_op jit(solution)/shard_map/ppermute | solution.py:489
  128.6 18.5 %collective-permute-start.11 = (bf16[96,1792]{1,0:T(8,128)(2,1)}, bf16[96,1792]{1,0:T(8,128)(2,1)S(1)}, u32[]{:S(2)}, u32[]{:S(2)}) collective-permute-start(bf16[96,1792]{1,0:T(8,128)(2,1)} %get-tuple-element.81), channel_id=1, source_target_pairs={{0,2},{1,3},{2,4},{3,5},{4,6},{5,7},{6,32},{7,33},{8,10},{9,11},{1... | collective-permute-start | bytes 1032200 | tf_op jit(solution)/shard_map/ppermute | solution.py:489
  154.2 30.7 %all-to-all-start.4 = ((bf16[8,48,1792]{2,1,0:T(8,128)(2,1)}), bf16[8,48,1792]{2,1,0:T(8,128)(2,1)S(1)}, u32[]{:S(2)}, u32[]{:S(2)}) async-start(bf16[8,48,1792]{2,1,0:T(8,128)(2,1)} %bitcast.27), calls=%async_computation.4 | async-start | bytes 2752512 | tf_op jit(solution)/shard_map/all_to_all | solution.py:499
  164.4 16.9 %collective-permute-start.14 = (bf16[96,1792]{1,0:T(8,128)(2,1)S(1)}, bf16[96,1792]{1,0:T(8,128)(2,1)S(1)}, u32[]{:S(2)}, u32[]{:S(2)}) collective-permute-start(bf16[96,1792]{1,0:T(8,128)(2,1)S(1)} %copy-done.31), channel_id=1, source_target_pairs={{0,102},{1,103},{2,0},{3,1},{4,2},{5,3},{6,4},{7,5},{8,110},{9,111... | collective-permute-start | bytes 1032200 | tf_op jit(solution)/shard_map/ppermute | solution.py:489
  186.1 30.9 %all-to-all-start.5 = ((bf16[8,48,1792]{2,1,0:T(8,128)(2,1)}), bf16[8,48,1792]{2,1,0:T(8,128)(2,1)S(1)}, u32[]{:S(2)}, u32[]{:S(2)}) async-start(bf16[8,48,1792]{2,1,0:T(8,128)(2,1)} %bitcast.24), calls=%async_computation.5 | async-start | bytes 2752512 | tf_op jit(solution)/shard_map/all_to_all | solution.py:499
  195.5 15.0 %collective-permute-start.16 = (bf16[96,1792]{1,0:T(8,128)(2,1)}, bf16[96,1792]{1,0:T(8,128)(2,1)S(1)}, u32[]{:S(2)}, u32[]{:S(2)}) collective-permute-start(bf16[96,1792]{1,0:T(8,128)(2,1)} %get-tuple-element.91), channel_id=1, source_target_pairs={{0,4},{1,101},{2,6},{3,103},{4,32},{5,1},{6,34},{7,3},{8,12},{9,10... | collective-permute-start | bytes 1032200 | tf_op jit(solution)/shard_map/ppermute | solution.py:489
  200.6 16.4 %collective-permute-start.17 = (bf16[96,1792]{1,0:T(8,128)(2,1)}, bf16[96,1792]{1,0:T(8,128)(2,1)S(1)}, u32[]{:S(2)}, u32[]{:S(2)}) collective-permute-start(bf16[96,1792]{1,0:T(8,128)(2,1)} %get-tuple-element.92), channel_id=1, source_target_pairs={{0,102},{1,103},{2,0},{3,1},{4,2},{5,3},{6,4},{7,5},{8,110},{9,111... | collective-permute-start | bytes 1032200 | tf_op jit(solution)/shard_map/ppermute | solution.py:489
  227.6 15.4 %collective-permute-start.18 = (bf16[272,896]{1,0:T(8,128)(2,1)}, bf16[272,896]{1,0:T(8,128)(2,1)S(1)}, u32[]{:S(2)}, u32[]{:S(2)}) collective-permute-start(bf16[272,896]{1,0:T(8,128)(2,1)} %get-tuple-element.95), channel_id=1, source_target_pairs={{0,128},{32,160},{64,192},{96,224},{128,256},{160,288},{192,320},{... | collective-permute-start | bytes 1462280 | tf_op jit(solution)/shard_map/ppermute | solution.py:472
  230.6 24.4 %collective-permute-start.19 = (bf16[272,896]{1,0:T(8,128)(2,1)}, bf16[272,896]{1,0:T(8,128)(2,1)S(1)}, u32[]{:S(2)}, u32[]{:S(2)}) collective-permute-start(bf16[272,896]{1,0:T(8,128)(2,1)} %get-tuple-element.96), channel_id=1, source_target_pairs={{0,384},{32,416},{64,448},{96,480},{128,0},{160,32},{192,64},{224,... | collective-permute-start | bytes 1462280 | tf_op jit(solution)/shard_map/ppermute | solution.py:472
  234.1 20.9 %collective-permute-start.20 = (bf16[272,896]{1,0:T(8,128)(2,1)}, bf16[272,896]{1,0:T(8,128)(2,1)S(1)}, u32[]{:S(2)}, u32[]{:S(2)}) collective-permute-start(bf16[272,896]{1,0:T(8,128)(2,1)} %get-tuple-element.97), channel_id=1, source_target_pairs={{0,256},{32,288},{64,320},{96,352},{128,384},{160,416},{192,448},{... | collective-permute-start | bytes 1462280 | tf_op jit(solution)/shard_map/ppermute | solution.py:472
  258.6 18.4 %collective-permute-start.21 = (bf16[240,256]{1,0:T(8,128)(2,1)}, bf16[240,256]{1,0:T(8,128)(2,1)S(1)}, u32[]{:S(2)}, u32[]{:S(2)}) collective-permute-start(bf16[240,256]{1,0:T(8,128)(2,1)} %get-tuple-element.99), channel_id=1, source_target_pairs={{0,32},{32,64},{64,96},{96,0},{128,160},{160,192},{192,224},{224,1... | collective-permute-start | bytes 368648 | tf_op jit(solution)/shard_map/ppermute | solution.py:472
  261.5 20.9 %collective-permute-start.22 = (bf16[240,256]{1,0:T(8,128)(2,1)}, bf16[240,256]{1,0:T(8,128)(2,1)S(1)}, u32[]{:S(2)}, u32[]{:S(2)}) collective-permute-start(bf16[240,256]{1,0:T(8,128)(2,1)} %get-tuple-element.100), channel_id=1, source_target_pairs={{0,96},{32,0},{64,32},{96,64},{128,224},{160,128},{192,160},{224,1... | collective-permute-start | bytes 368648 | tf_op jit(solution)/shard_map/ppermute | solution.py:472
  267.9 23.6 %collective-permute-start.23 = (bf16[240,256]{1,0:T(8,128)(2,1)}, bf16[240,256]{1,0:T(8,128)(2,1)S(1)}, u32[]{:S(2)}, u32[]{:S(2)}) collective-permute-start(bf16[240,256]{1,0:T(8,128)(2,1)} %get-tuple-element.101), channel_id=1, source_target_pairs={{0,64},{32,96},{64,0},{96,32},{128,192},{160,224},{192,128},{224,1... | collective-permute-start | bytes 368648 | tf_op jit(solution)/shard_map/ppermute | solution.py:472
  (43 other events, 284.6 us)

commit v5 on v4

--- a/solution.py
+++ b/solution.py
@@ -267,7 +267,7 @@
             pltpu.SemaphoreType.DMA((SIDE,)),
             pltpu.SemaphoreType.DMA((SIDE,)),
         ],
-        compiler_params=PARAMS,
+        compiler_params=pltpu.CompilerParams(vmem_limit_bytes=16 * 1024 * 1024),
         name="encode_decode",
     )(*x, enc, bias, dec)
 
@@ -338,37 +338,50 @@
     rows, half = x.shape
     n = pre_a.shape[1]
     groups, _, quarter = pieces.shape
+    e_copies = start(slot_moves(e_refs, e), e_sems)
     dec_copies = start(
         [(dec_ref.at[:, s * half : (s + 1) * half], dec2.at[s * n : (s + 1) * n]) for s in range(2)],
         w_sems,
     )
-    e_copies = start(slot_moves(e_refs, e), e_sems)
     x_copies = start(slot_moves(x_refs, x), x_sems)
     me = lax.axis_index("rows") // SIDE
     left = left_rows(rows)
     pre = jnp.concatenate([pre_b[...], pre_a[...]], axis=0)
     sig = jax.nn.sigmoid(pre)
     codes = split_halves(pre * sig, left).astype(BF)
+
+    def fill(terms, slots, first):
+        for g in range(groups // 2):
+            both = dot_t(terms, slots[:, g * quarter : (g + 1) * quarter]).astype(BF)
+            for s in range(2):
+                pieces[g + s * (groups // 2), first : first + n, :] = both[s * n : (s + 1) * n]
+
+    def give(first, last, turn):
+        return start(
+            [
+                (pieces.at[lax.rem(me + k, SIDE), first:last], out.at[first:last])
+                for k, out in enumerate(outs)
+            ],
+            sems,
+            turn * SIDE,
+        )
+
+    wait(e_copies)
+    fill(codes, e, 0)
+    given = give(0, n, 0)
     wait(dec_copies)
-    wait(e_copies)
     code_grad = join_halves(dot_nt(e[...], dec2[...]), left)
     grad = (code_grad * sig * (1.0 + pre * (1.0 - sig))).astype(BF).astype(F32)
     grads = split_halves(grad, left)
     bias = jnp.sum(grads[:, :n], axis=0, keepdims=True)
-    grads = grads.astype(BF)
     wait(x_copies)
-    for g in range(0, groups // 2):
-        cols = pl.ds(g * quarter, quarter)
-        enc = dot_t(grads, x[:, cols]).astype(BF)
-        dec = dot_t(codes, e[:, cols]).astype(BF)
-        for s in range(2):
-            pieces[g + s * (groups // 2), :n, :] = enc[s * n : s * n + n]
-            pieces[g + s * (groups // 2), n : 2 * n, :] = dec[s * n : s * n + n]
+    fill(grads.astype(BF), x, n)
     for g in range(groups):
         shifted = pltpu.roll(bias, (n - g * (n // groups)) % n, 1)
         pieces[g, 2 * n :, :] = jnp.zeros((16, quarter), BF)
         pieces[g, 2 * n :, :n] = hi_lo(shifted)
-    hand_out(pieces, outs, me, sems)
+    given += give(n, 2 * n + 16, 1)
+    wait(given)
 
 
 def hand_out(pieces, outs, me, sems):
@@ -393,7 +406,7 @@
             pltpu.SemaphoreType.DMA((2,)),
             pltpu.SemaphoreType.DMA((SIDE + 1,)),
             pltpu.SemaphoreType.DMA((SIDE + 1,)),
-            pltpu.SemaphoreType.DMA((SIDE,)),
+            pltpu.SemaphoreType.DMA((2 * SIDE,)),
         ],
         compiler_params=PARAMS,
         name="gradients",
@@ -440,8 +453,8 @@
     total = ins[0][...].astype(F32)
     for part in ins[1:]:
         total = total + part[...].astype(F32)
-    enc_ref[...] = total[:piece, :n]
-    dec_ref[...] = total[:piece, n:]
+    dec_ref[...] = total[:piece, :n]
+    enc_ref[...] = total[:piece, n:]
     bias = jnp.sum(total[piece:, :n], axis=0, keepdims=True)
     bias_ref[...] = bias[:, : bias_ref.shape[1]]
 
@@ -463,7 +476,7 @@
 
 def share_pieces(pieces, along_y):
     got = [pieces[0]]
-    for k in (1, 3, 2):
+    for k in (2, 1, 3):
         pairs = []
         for i in range(SIDE * SIDE):
             y, z = divmod(i, SIDE)
@@ -473,9 +486,12 @@
     return got
 
 
-def along_z(x, steps, back=False):
-    if steps[0] == 0:
-        return x
+def along_z(arrays, back=False):
+    moved = {k: shift_z(arrays[k], STEPS[k], back) for k in (2, 1, 3)}
+    return [arrays[0], moved[1], moved[2], moved[3]]
+
+
+def shift_z(x, steps, back):
     pairs = []
     for i in range(512):
         rows, lat = divmod(i, 32)
@@ -508,18 +524,18 @@
 
 
 def to_owners(slots):
-    moved = [along_z(a, steps) for a, steps in zip(slots[:SIDE], STEPS)]
+    moved = along_z(slots[:SIDE])
     crossed, merged = lax.optimization_barrier((over_x(slots[SIDE]), swap_pieces(moved, True)))
     stream_a = over_x(merged)
-    stream_b = [along_z(a, steps) for a, steps in zip(swap_pieces([crossed], False), STEPS)]
+    stream_b = along_z(swap_pieces([crossed], False))
     return stream_a, stream_b
 
 
 def to_homes(stream_a, stream_b):
-    moved = [along_z(a, steps, True) for a, steps in zip(stream_b, STEPS)]
+    moved = along_z(stream_b, True)
     crossed, merged = lax.optimization_barrier((over_x(stream_a), swap_pieces(moved, True)))
     home_b = over_x(merged)
-    home_a = [along_z(a, steps, True) for a, steps in zip(swap_pieces([crossed], False), STEPS)]
+    home_a = along_z(swap_pieces([crossed], False), True)
     return [*home_a, home_b]
 
 

time: 299 us -> 290 us (0.970); the launches traced: 294 us -> 288 us
  Pallas kernels: 52.8 us -> 46.9 us
  starting transfers between devices: 117 us -> 120 us
  waiting for transfers between devices: 111 us -> 108 us
    pallas_call x2, Pallas kernels: 12 us -> 6.3 us  [encode_decode(): pl.pallas_call(functools.partial(code_kernel, parts), in_specs=[ANY] * (p...]
    ppermute x6, waiting for transfers between devices: 33.3 us -> 28.2 us  [share_pieces(): got.append(lax.ppermute(pieces[k], 'rows', pairs))]
    unnamed x74 -> x86, local copies, waits for them, and re-layouts: 11.6 us -> 12.3 us
  transfers between devices with their start and end apart: 30 -> 30, of which waited for: 21 -> 21; matrix products, arithmetic and copies ran while one was open for 0% -> 0% of each run, Pallas kernels for 10% -> 8%
where the time goes in v5:
time: 290 us; the launch traced here: 288 us
  starting transfers between devices  120 us (41%)
  waiting for transfers between devices  108 us (37%)
  Pallas kernels  46.9 us (16%)
  local copies, waits for them, and re-layouts  12.9 us (4%)
    ppermute x18, waiting for transfers between devices, shift_z(): return lax.ppermute(x, ('rows', 'lat'), pairs)  73.8 us
    ppermute x18, starting transfers between devices, shift_z(): return lax.ppermute(x, ('rows', 'lat'), pairs)  55.9 us
    all_to_all x6, starting transfers between devices, over_x(): lax.all_to_all(x.reshape(members, shape[0] // members, shape[1]), 'lat',...  34.4 us
    ppermute x6, starting transfers between devices, share_pieces(): got.append(lax.ppermute(pieces[k], 'rows', pairs))  29.4 us
    ppermute x6, waiting for transfers between devices, share_pieces(): got.append(lax.ppermute(pieces[k], 'rows', pairs))  28.2 us
    pallas_call x6, Pallas kernels, swap_pieces(): pl.pallas_call(functools.partial(swap_kernel, merge), in_specs=[ANY] * le...  17.3 us
    unnamed x86, local copies, waits for them, and re-layouts  12.3 us
    pallas_call x1, Pallas kernels, gradients(): pl.pallas_call(grad_kernel, in_specs=[in_vmem, in_vmem] + [ANY] * (2 * SI...  9.02 us
  transfers between devices with their start and end apart: 30, of which 21 were waited for; matrix products, arithmetic and copies ran while one was open for 0% of the time, Pallas kernels for 8%

profile of v5, /device:TPU:1, one launch (start us, length us, event | category | flops | bytes accessed | tf_op | source)
XLA Modules:
  0.0 288.3 jit_solution(8522117799578358068)
XLA Ops:
  4.7 10.5 %all-to-all-start = ((bf16[8,48,1792]{2,1,0:T(8,128)(2,1)}), bf16[8,48,1792]{2,1,0:T(8,128)(2,1)S(1)}, u32[]{:S(2)}, u32[]{:S(2)}) async-start(bf16[8,48,1792]{2,1,0:T(8,128)(2,1)} %bitcast.29), calls=%async_computation | async-start | bytes 2752512 | tf_op jit(solution)/shard_map/all_to_all | solution.py:515
  17.1 7.7 %collective-permute-start.1 = (bf16[96,1792]{1,0:T(8,128)(2,1)S(1)}, bf16[96,1792]{1,0:T(8,128)(2,1)S(1)}, u32[]{:S(2)}, u32[]{:S(2)}) collective-permute-start(bf16[96,1792]{1,0:T(8,128)(2,1)S(1)} %copy-done.41), channel_id=1, source_target_pairs={{0,4},{1,101},{2,6},{3,103},{4,32},{5,1},{6,34},{7,3},{8,12},{9,10... | collective-permute-start | bytes 1032200 | tf_op jit(solution)/shard_map/ppermute | solution.py:505
  30.1 5.4 %collective-permute-done.1.refs_2_ = bf16[96,1792]{1,0:T(8,128)(2,1)S(1)} collective-permute-done((bf16[96,1792]{1,0:T(8,128)(2,1)S(1)}, bf16[96,1792]{1,0:T(8,128)(2,1)S(1)}, u32[]{:S(2)}, u32[]{:S(2)}) %collective-permute-start.1) | collective-permute-done | bytes 344096 | tf_op jit(solution)/shard_map/ppermute | solution.py:505
  44.8 4.7 %all-to-all-start.1 = ((bf16[8,48,1792]{2,1,0:T(8,128)(2,1)}), bf16[8,48,1792]{2,1,0:T(8,128)(2,1)S(1)}, u32[]{:S(2)}, u32[]{:S(2)}) async-start(bf16[8,48,1792]{2,1,0:T(8,128)(2,1)} %bitcast.27), calls=%async_computation.1 | async-start | bytes 2752512 | tf_op jit(solution)/shard_map/all_to_all | solution.py:515
  54.3 6.2 %collective-permute-start.4 = (bf16[96,1792]{1,0:T(8,128)(2,1)}, bf16[96,1792]{1,0:T(8,128)(2,1)}, u32[]{:S(2)}, u32[]{:S(2)}) collective-permute-start(bf16[96,1792]{1,0:T(8,128)(2,1)} %get-tuple-element.64), channel_id=1, source_target_pairs={{0,4},{1,101},{2,6},{3,103},{4,32},{5,1},{6,34},{7,3},{8,12},{9,10... | collective-permute-start | bytes 1032200 | tf_op jit(solution)/shard_map/ppermute | solution.py:505
  62.5 5.7 %all-to-all-done.1 = bf16[8,48,1792]{2,1,0:T(8,128)(2,1)S(1)} async-done(((bf16[8,48,1792]{2,1,0:T(8,128)(2,1)}), bf16[8,48,1792]{2,1,0:T(8,128)(2,1)S(1)}, u32[]{:S(2)}, u32[]{:S(2)}) %all-to-all-start.1) | async-done | bytes 1376288 | tf_op jit(solution)/shard_map/all_to_all | solution.py:515
  86.1 5.0 %collective-permute-start.6 = (bf16[96,1792]{1,0:T(8,128)(2,1)S(1)}, bf16[96,1792]{1,0:T(8,128)(2,1)S(1)}, u32[]{:S(2)}, u32[]{:S(2)}) collective-permute-start(bf16[96,1792]{1,0:T(8,128)(2,1)S(1)} %get-tuple-element.74), channel_id=1, source_target_pairs={{0,102},{1,103},{2,0},{3,1},{4,2},{5,3},{6,4},{7,5},{8,110},{9,111... | collective-permute-start | bytes 1032200 | tf_op jit(solution)/shard_map/ppermute | solution.py:505
  94.9 5.8 %collective-permute-done.6.refs_1_ = bf16[96,1792]{1,0:T(8,128)(2,1)S(1)} collective-permute-done((bf16[96,1792]{1,0:T(8,128)(2,1)S(1)}, bf16[96,1792]{1,0:T(8,128)(2,1)S(1)}, u32[]{:S(2)}, u32[]{:S(2)}) %collective-permute-start.6) | collective-permute-done | bytes 344096 | tf_op jit(solution)/shard_map/ppermute | solution.py:505
  100.8 5.8 %collective-permute-done.7.refs_2_ = bf16[96,1792]{1,0:T(8,128)(2,1)S(1)} collective-permute-done((bf16[96,1792]{1,0:T(8,128)(2,1)S(1)}, bf16[96,1792]{1,0:T(8,128)(2,1)S(1)}, u32[]{:S(2)}, u32[]{:S(2)}) %collective-permute-start.7) | collective-permute-done | bytes 344096 | tf_op jit(solution)/shard_map/ppermute | solution.py:505
  113.1 5.2 %all-to-all-start.3 = ((bf16[8,48,1792]{2,1,0:T(8,128)(2,1)}), bf16[8,48,1792]{2,1,0:T(8,128)(2,1)S(1)}, u32[]{:S(2)}, u32[]{:S(2)}) async-start(bf16[8,48,1792]{2,1,0:T(8,128)(2,1)} %bitcast.25), calls=%async_computation.3 | async-start | bytes 2752512 | tf_op jit(solution)/shard_map/all_to_all | solution.py:515
  133.0 6.8 %collective-permute-done.10.refs_2_ = bf16[96,1792]{1,0:T(8,128)(2,1)S(1)} collective-permute-done((bf16[96,1792]{1,0:T(8,128)(2,1)}, bf16[96,1792]{1,0:T(8,128)(2,1)S(1)}, u32[]{:S(2)}, u32[]{:S(2)}) %collective-permute-start.10) | collective-permute-done | bytes 344096 | tf_op jit(solution)/shard_map/ppermute | solution.py:505
  139.8 5.0 %collective-permute-done.11.refs_3_ = bf16[96,1792]{1,0:T(8,128)(2,1)S(1)} collective-permute-done((bf16[96,1792]{1,0:T(8,128)(2,1)}, bf16[96,1792]{1,0:T(8,128)(2,1)S(1)}, u32[]{:S(2)}, u32[]{:S(2)}) %collective-permute-start.11) | collective-permute-done | bytes 344096 | tf_op jit(solution)/shard_map/ppermute | solution.py:505
  145.9 5.8 %error_rows.1 = (bf16[96,1792]{1,0:T(8,128)(2,1)}, bf16[96,1792]{1,0:T(8,128)(2,1)}, bf16[96,1792]{1,0:T(8,128)(2,1)}, bf16[96,1792]{1,0:T(8,128)(2,1)}, bf16[384,1792]{1,0:T(8,128)(2,1)}) custom-call(s32[2,128]{1,0:T(2,128)} %bitcast.31, f32[1,3584]{1,0:T(1,128)} %broadcast_in_dim.7.bias_ref, bf16[128,3584]{1,0:T(8,128)(2,1)} %act_ref.3, ...), custom_call_target="tpu_custom_call" | custom-call | tf_op jit(solution)/shard_map/error_rows/pallas_call | solution.py:309
  151.8 4.8 %all-to-all-start.4 = ((bf16[8,48,1792]{2,1,0:T(8,128)(2,1)}), bf16[8,48,1792]{2,1,0:T(8,128)(2,1)S(1)}, u32[]{:S(2)}, u32[]{:S(2)}) async-start(bf16[8,48,1792]{2,1,0:T(8,128)(2,1)} %bitcast.28), calls=%async_computation.4 | async-start | bytes 2752512 | tf_op jit(solution)/shard_map/all_to_all | solution.py:515
  165.0 5.0 %collective-permute-done.12.refs_1_ = bf16[96,1792]{1,0:T(8,128)(2,1)S(1)} collective-permute-done((bf16[96,1792]{1,0:T(8,128)(2,1)S(1)}, bf16[96,1792]{1,0:T(8,128)(2,1)S(1)}, u32[]{:S(2)}, u32[]{:S(2)}) %collective-permute-start.12) | collective-permute-done | bytes 344096 | tf_op jit(solution)/shard_map/ppermute | solution.py:505
  170.0 8.8 %collective-permute-done.14.refs_3_ = bf16[96,1792]{1,0:T(8,128)(2,1)S(1)} collective-permute-done((bf16[96,1792]{1,0:T(8,128)(2,1)S(1)}, bf16[96,1792]{1,0:T(8,128)(2,1)S(1)}, u32[]{:S(2)}, u32[]{:S(2)}) %collective-permute-start.14) | collective-permute-done | bytes 344096 | tf_op jit(solution)/shard_map/ppermute | solution.py:505
  192.9 5.3 %collective-permute-start.16 = (bf16[96,1792]{1,0:T(8,128)(2,1)}, bf16[96,1792]{1,0:T(8,128)(2,1)S(1)}, u32[]{:S(2)}, u32[]{:S(2)}) collective-permute-start(bf16[96,1792]{1,0:T(8,128)(2,1)} %get-tuple-element.91), channel_id=1, source_target_pairs={{0,4},{1,101},{2,6},{3,103},{4,32},{5,1},{6,34},{7,3},{8,12},{9,10... | collective-permute-start | bytes 1032200 | tf_op jit(solution)/shard_map/ppermute | solution.py:505
  207.9 6.5 %collective-permute-done.17.refs_8_ = bf16[96,1792]{1,0:T(8,128)(2,1)S(1)} collective-permute-done((bf16[96,1792]{1,0:T(8,128)(2,1)}, bf16[96,1792]{1,0:T(8,128)(2,1)S(1)}, u32[]{:S(2)}, u32[]{:S(2)}) %collective-permute-start.17) | collective-permute-done | bytes 344096 | tf_op jit(solution)/shard_map/ppermute | solution.py:505
  215.7 9.0 %gradients.1 = (bf16[272,896]{1,0:T(8,128)(2,1)}, bf16[272,896]{1,0:T(8,128)(2,1)}, bf16[272,896]{1,0:T(8,128)(2,1)}, bf16[272,896]{1,0:T(8,128)(2,1)}) custom-call(f32[384,128]{1,0:T(8,128)} %copy-done.7, f32[384,128]{1,0:T(8,128)} %copy-done.8, bf16[128,3584]{1,0:T(8,128)(2,1)} %dec_ref.1, bf16[96,1792]{1,0:T(8,128)(2,1)} %get-tuple-element.67.refs_0_, ...), custom_call_target="tpu_custom_call" | custom-call | tf_op jit(solution)/shard_map/gradients/pallas_call | solution.py:396
  235.8 5.4 %collective-permute-done.18.refs_1_ = bf16[272,896]{1,0:T(8,128)(2,1)S(1)} collective-permute-done((bf16[272,896]{1,0:T(8,128)(2,1)}, bf16[272,896]{1,0:T(8,128)(2,1)S(1)}, u32[]{:S(2)}, u32[]{:S(2)}) %collective-permute-start.18) | collective-permute-done | bytes 487456 | tf_op jit(solution)/shard_map/ppermute | solution.py:485
  241.2 9.7 %collective-permute-done.19.refs_2_ = bf16[272,896]{1,0:T(8,128)(2,1)S(1)} collective-permute-done((bf16[272,896]{1,0:T(8,128)(2,1)}, bf16[272,896]{1,0:T(8,128)(2,1)S(1)}, u32[]{:S(2)}, u32[]{:S(2)}) %collective-permute-start.19) | collective-permute-done | bytes 487456 | tf_op jit(solution)/shard_map/ppermute | solution.py:485
  254.4 9.0 %collective-permute-start.21 = (bf16[240,256]{1,0:T(8,128)(2,1)}, bf16[240,256]{1,0:T(8,128)(2,1)S(1)}, u32[]{:S(2)}, u32[]{:S(2)}) collective-permute-start(bf16[240,256]{1,0:T(8,128)(2,1)} %get-tuple-element.99), channel_id=1, source_target_pairs={{0,64},{32,96},{64,0},{96,32},{128,192},{160,224},{192,128},{224,1... | collective-permute-start | bytes 368648 | tf_op jit(solution)/shard_map/ppermute | solution.py:485
  267.8 4.9 %collective-permute-start.23 = (bf16[240,256]{1,0:T(8,128)(2,1)}, bf16[240,256]{1,0:T(8,128)(2,1)S(1)}, u32[]{:S(2)}, u32[]{:S(2)}) collective-permute-start(bf16[240,256]{1,0:T(8,128)(2,1)} %get-tuple-element.101), channel_id=1, source_target_pairs={{0,96},{32,0},{64,32},{96,64},{128,224},{160,128},{192,160},{224,1... | collective-permute-start | bytes 368648 | tf_op jit(solution)/shard_map/ppermute | solution.py:485
  272.7 5.8 %collective-permute-done.21.refs_1_ = bf16[240,256]{1,0:T(8,128)(2,1)S(1)} collective-permute-done((bf16[240,256]{1,0:T(8,128)(2,1)}, bf16[240,256]{1,0:T(8,128)(2,1)S(1)}, u32[]{:S(2)}, u32[]{:S(2)}) %collective-permute-start.21) | collective-permute-done | bytes 122912 | tf_op jit(solution)/shard_map/ppermute | solution.py:485
  (136 shorter events, 133.2 us)
Async XLA Ops:
  4.7 39.0 %all-to-all-start = ((bf16[8,48,1792]{2,1,0:T(8,128)(2,1)}), bf16[8,48,1792]{2,1,0:T(8,128)(2,1)S(1)}, u32[]{:S(2)}, u32[]{:S(2)}) async-start(bf16[8,48,1792]{2,1,0:T(8,128)(2,1)} %bitcast.29), calls=%async_computation | async-start | bytes 2752512 | tf_op jit(solution)/shard_map/all_to_all | solution.py:515
  17.1 18.5 %collective-permute-start.1 = (bf16[96,1792]{1,0:T(8,128)(2,1)S(1)}, bf16[96,1792]{1,0:T(8,128)(2,1)S(1)}, u32[]{:S(2)}, u32[]{:S(2)}) collective-permute-start(bf16[96,1792]{1,0:T(8,128)(2,1)S(1)} %copy-done.41), channel_id=1, source_target_pairs={{0,4},{1,101},{2,6},{3,103},{4,32},{5,1},{6,34},{7,3},{8,12},{9,10... | collective-permute-start | bytes 1032200 | tf_op jit(solution)/shard_map/ppermute | solution.py:505
  24.8 15.2 %collective-permute-start.2 = (bf16[96,1792]{1,0:T(8,128)(2,1)S(1)}, bf16[96,1792]{1,0:T(8,128)(2,1)S(1)}, u32[]{:S(2)}, u32[]{:S(2)}) collective-permute-start(bf16[96,1792]{1,0:T(8,128)(2,1)S(1)} %copy-done.39), channel_id=1, source_target_pairs={{0,102},{1,103},{2,0},{3,1},{4,2},{5,3},{6,4},{7,5},{8,110},{9,111... | collective-permute-start | bytes 1032200 | tf_op jit(solution)/shard_map/ppermute | solution.py:505
  44.8 23.4 %all-to-all-start.1 = ((bf16[8,48,1792]{2,1,0:T(8,128)(2,1)}), bf16[8,48,1792]{2,1,0:T(8,128)(2,1)S(1)}, u32[]{:S(2)}, u32[]{:S(2)}) async-start(bf16[8,48,1792]{2,1,0:T(8,128)(2,1)} %bitcast.27), calls=%async_computation.1 | async-start | bytes 2752512 | tf_op jit(solution)/shard_map/all_to_all | solution.py:515
  52.4 20.7 %collective-permute-start.3 = (bf16[96,1792]{1,0:T(8,128)(2,1)}, bf16[96,1792]{1,0:T(8,128)(2,1)S(1)}, u32[]{:S(2)}, u32[]{:S(2)}) collective-permute-start(bf16[96,1792]{1,0:T(8,128)(2,1)} %get-tuple-element.63), channel_id=1, source_target_pairs={{0,2},{1,3},{2,4},{3,5},{4,6},{5,7},{6,32},{7,33},{8,10},{9,11},{1... | collective-permute-start | bytes 1032200 | tf_op jit(solution)/shard_map/ppermute | solution.py:505
  54.3 18.8 %collective-permute-start.4 = (bf16[96,1792]{1,0:T(8,128)(2,1)}, bf16[96,1792]{1,0:T(8,128)(2,1)}, u32[]{:S(2)}, u32[]{:S(2)}) collective-permute-start(bf16[96,1792]{1,0:T(8,128)(2,1)} %get-tuple-element.64), channel_id=1, source_target_pairs={{0,4},{1,101},{2,6},{3,103},{4,32},{5,1},{6,34},{7,3},{8,12},{9,10... | collective-permute-start | bytes 1032200 | tf_op jit(solution)/shard_map/ppermute | solution.py:505
  60.5 15.5 %collective-permute-start.5 = (bf16[96,1792]{1,0:T(8,128)(2,1)}, bf16[96,1792]{1,0:T(8,128)(2,1)}, u32[]{:S(2)}, u32[]{:S(2)}) collective-permute-start(bf16[96,1792]{1,0:T(8,128)(2,1)} %get-tuple-element.65), channel_id=1, source_target_pairs={{0,102},{1,103},{2,0},{3,1},{4,2},{5,3},{6,4},{7,5},{8,110},{9,111... | collective-permute-start | bytes 1032200 | tf_op jit(solution)/shard_map/ppermute | solution.py:505
  76.1 37.0 %all-to-all-start.2 = ((bf16[8,48,1792]{2,1,0:T(8,128)(2,1)}), bf16[8,48,1792]{2,1,0:T(8,128)(2,1)}, u32[]{:S(2)}, u32[]{:S(2)}) async-start(bf16[8,48,1792]{2,1,0:T(8,128)(2,1)} %bitcast.18), calls=%async_computation.2 | async-start | bytes 2752512 | tf_op jit(solution)/shard_map/all_to_all | solution.py:515
  91.1 15.5 %collective-permute-start.7 = (bf16[96,1792]{1,0:T(8,128)(2,1)S(1)}, bf16[96,1792]{1,0:T(8,128)(2,1)S(1)}, u32[]{:S(2)}, u32[]{:S(2)}) collective-permute-start(bf16[96,1792]{1,0:T(8,128)(2,1)S(1)} %get-tuple-element.75), channel_id=1, source_target_pairs={{0,100},{1,5},{2,102},{3,7},{4,0},{5,33},{6,2},{7,35},{8,108},{9,1... | collective-permute-start | bytes 1032200 | tf_op jit(solution)/shard_map/ppermute | solution.py:505
  93.0 16.4 %collective-permute-start.8 = (bf16[96,1792]{1,0:T(8,128)(2,1)S(1)}, bf16[96,1792]{1,0:T(8,128)(2,1)S(1)}, u32[]{:S(2)}, u32[]{:S(2)}) collective-permute-start(bf16[96,1792]{1,0:T(8,128)(2,1)S(1)} %get-tuple-element.76), channel_id=1, source_target_pairs={{0,2},{1,3},{2,4},{3,5},{4,6},{5,7},{6,32},{7,33},{8,10},{9,11},{1... | collective-permute-start | bytes 1032200 | tf_op jit(solution)/shard_map/ppermute | solution.py:505
  113.1 31.6 %all-to-all-start.3 = ((bf16[8,48,1792]{2,1,0:T(8,128)(2,1)}), bf16[8,48,1792]{2,1,0:T(8,128)(2,1)S(1)}, u32[]{:S(2)}, u32[]{:S(2)}) async-start(bf16[8,48,1792]{2,1,0:T(8,128)(2,1)} %bitcast.25), calls=%async_computation.3 | async-start | bytes 2752512 | tf_op jit(solution)/shard_map/all_to_all | solution.py:515
  124.3 15.5 %collective-permute-start.10 = (bf16[96,1792]{1,0:T(8,128)(2,1)}, bf16[96,1792]{1,0:T(8,128)(2,1)S(1)}, u32[]{:S(2)}, u32[]{:S(2)}) collective-permute-start(bf16[96,1792]{1,0:T(8,128)(2,1)} %get-tuple-element.80), channel_id=1, source_target_pairs={{0,100},{1,5},{2,102},{3,7},{4,0},{5,33},{6,2},{7,35},{8,108},{9,1... | collective-permute-start | bytes 1032200 | tf_op jit(solution)/shard_map/ppermute | solution.py:505
  126.3 18.4 %collective-permute-start.11 = (bf16[96,1792]{1,0:T(8,128)(2,1)}, bf16[96,1792]{1,0:T(8,128)(2,1)S(1)}, u32[]{:S(2)}, u32[]{:S(2)}) collective-permute-start(bf16[96,1792]{1,0:T(8,128)(2,1)} %get-tuple-element.81), channel_id=1, source_target_pairs={{0,2},{1,3},{2,4},{3,5},{4,6},{5,7},{6,32},{7,33},{8,10},{9,11},{1... | collective-permute-start | bytes 1032200 | tf_op jit(solution)/shard_map/ppermute | solution.py:505
  151.8 30.7 %all-to-all-start.4 = ((bf16[8,48,1792]{2,1,0:T(8,128)(2,1)}), bf16[8,48,1792]{2,1,0:T(8,128)(2,1)S(1)}, u32[]{:S(2)}, u32[]{:S(2)}) async-start(bf16[8,48,1792]{2,1,0:T(8,128)(2,1)} %bitcast.28), calls=%async_computation.4 | async-start | bytes 2752512 | tf_op jit(solution)/shard_map/all_to_all | solution.py:515
  162.1 16.7 %collective-permute-start.14 = (bf16[96,1792]{1,0:T(8,128)(2,1)S(1)}, bf16[96,1792]{1,0:T(8,128)(2,1)S(1)}, u32[]{:S(2)}, u32[]{:S(2)}) collective-permute-start(bf16[96,1792]{1,0:T(8,128)(2,1)S(1)} %copy-done.37), channel_id=1, source_target_pairs={{0,102},{1,103},{2,0},{3,1},{4,2},{5,3},{6,4},{7,5},{8,110},{9,111... | collective-permute-start | bytes 1032200 | tf_op jit(solution)/shard_map/ppermute | solution.py:505
  183.6 30.9 %all-to-all-start.5 = ((bf16[8,48,1792]{2,1,0:T(8,128)(2,1)}), bf16[8,48,1792]{2,1,0:T(8,128)(2,1)S(1)}, u32[]{:S(2)}, u32[]{:S(2)}) async-start(bf16[8,48,1792]{2,1,0:T(8,128)(2,1)} %bitcast.26), calls=%async_computation.5 | async-start | bytes 2752512 | tf_op jit(solution)/shard_map/all_to_all | solution.py:515
  192.9 15.0 %collective-permute-start.16 = (bf16[96,1792]{1,0:T(8,128)(2,1)}, bf16[96,1792]{1,0:T(8,128)(2,1)S(1)}, u32[]{:S(2)}, u32[]{:S(2)}) collective-permute-start(bf16[96,1792]{1,0:T(8,128)(2,1)} %get-tuple-element.91), channel_id=1, source_target_pairs={{0,4},{1,101},{2,6},{3,103},{4,32},{5,1},{6,34},{7,3},{8,12},{9,10... | collective-permute-start | bytes 1032200 | tf_op jit(solution)/shard_map/ppermute | solution.py:505
  198.2 16.3 %collective-permute-start.17 = (bf16[96,1792]{1,0:T(8,128)(2,1)}, bf16[96,1792]{1,0:T(8,128)(2,1)S(1)}, u32[]{:S(2)}, u32[]{:S(2)}) collective-permute-start(bf16[96,1792]{1,0:T(8,128)(2,1)} %get-tuple-element.92), channel_id=1, source_target_pairs={{0,102},{1,103},{2,0},{3,1},{4,2},{5,3},{6,4},{7,5},{8,110},{9,111... | collective-permute-start | bytes 1032200 | tf_op jit(solution)/shard_map/ppermute | solution.py:505
  224.7 16.5 %collective-permute-start.18 = (bf16[272,896]{1,0:T(8,128)(2,1)}, bf16[272,896]{1,0:T(8,128)(2,1)S(1)}, u32[]{:S(2)}, u32[]{:S(2)}) collective-permute-start(bf16[272,896]{1,0:T(8,128)(2,1)} %get-tuple-element.95), channel_id=1, source_target_pairs={{0,256},{32,288},{64,320},{96,352},{128,384},{160,416},{192,448},{... | collective-permute-start | bytes 1462280 | tf_op jit(solution)/shard_map/ppermute | solution.py:485
  229.3 21.5 %collective-permute-start.19 = (bf16[272,896]{1,0:T(8,128)(2,1)}, bf16[272,896]{1,0:T(8,128)(2,1)S(1)}, u32[]{:S(2)}, u32[]{:S(2)}) collective-permute-start(bf16[272,896]{1,0:T(8,128)(2,1)} %get-tuple-element.96), channel_id=1, source_target_pairs={{0,128},{32,160},{64,192},{96,224},{128,256},{160,288},{192,320},{... | collective-permute-start | bytes 1462280 | tf_op jit(solution)/shard_map/ppermute | solution.py:485
  231.6 19.3 %collective-permute-start.20 = (bf16[272,896]{1,0:T(8,128)(2,1)}, bf16[272,896]{1,0:T(8,128)(2,1)S(1)}, u32[]{:S(2)}, u32[]{:S(2)}) collective-permute-start(bf16[272,896]{1,0:T(8,128)(2,1)} %get-tuple-element.97), channel_id=1, source_target_pairs={{0,384},{32,416},{64,448},{96,480},{128,0},{160,32},{192,64},{224,... | collective-permute-start | bytes 1462280 | tf_op jit(solution)/shard_map/ppermute | solution.py:485
  254.4 24.1 %collective-permute-start.21 = (bf16[240,256]{1,0:T(8,128)(2,1)}, bf16[240,256]{1,0:T(8,128)(2,1)S(1)}, u32[]{:S(2)}, u32[]{:S(2)}) collective-permute-start(bf16[240,256]{1,0:T(8,128)(2,1)} %get-tuple-element.99), channel_id=1, source_target_pairs={{0,64},{32,96},{64,0},{96,32},{128,192},{160,224},{192,128},{224,1... | collective-permute-start | bytes 368648 | tf_op jit(solution)/shard_map/ppermute | solution.py:485
  263.5 19.0 %collective-permute-start.22 = (bf16[240,256]{1,0:T(8,128)(2,1)}, bf16[240,256]{1,0:T(8,128)(2,1)S(1)}, u32[]{:S(2)}, u32[]{:S(2)}) collective-permute-start(bf16[240,256]{1,0:T(8,128)(2,1)} %get-tuple-element.100), channel_id=1, source_target_pairs={{0,32},{32,64},{64,96},{96,0},{128,160},{160,192},{192,224},{224,1... | collective-permute-start | bytes 368648 | tf_op jit(solution)/shard_map/ppermute | solution.py:485
  267.8 18.0 %collective-permute-start.23 = (bf16[240,256]{1,0:T(8,128)(2,1)}, bf16[240,256]{1,0:T(8,128)(2,1)S(1)}, u32[]{:S(2)}, u32[]{:S(2)}) collective-permute-start(bf16[240,256]{1,0:T(8,128)(2,1)} %get-tuple-element.101), channel_id=1, source_target_pairs={{0,96},{32,0},{64,32},{96,64},{128,224},{160,128},{192,160},{224,1... | collective-permute-start | bytes 368648 | tf_op jit(solution)/shard_map/ppermute | solution.py:485
  (49 other events, 329.1 us)

commit v6 on v5

--- a/solution.py
+++ b/solution.py
@@ -25,10 +25,6 @@
 
 def dot(a, b):
     return lax.dot_general(a, b, (((1,), (0,)), ((), ())), preferred_element_type=F32)
-
-
-def dot_t(a, b):
-    return lax.dot_general(a, b, (((0,), (0,)), ((), ())), preferred_element_type=F32)
 
 
 def dot_nt(a, b):
@@ -77,7 +73,7 @@
     expand = lax.broadcasted_iota(jnp.int32, (rows, blocks), 1) == block
     spread = dot(expand.astype(F32).astype(BF), code)
     hit = (spread == slot.astype(F32)).astype(F32)
-    return split_halves(hit, left).astype(BF)
+    return split_halves(hit, left)
 
 
 def start(pairs, sems, first=0):
@@ -126,7 +122,7 @@
         [(act_ref.at[:, s * half : (s + 1) * half], act2.at[s * n : (s + 1) * n]) for s in range(2)],
         in_sems,
     )
-    sel[...] = one_hot_slots(ids_ref[...], blocks)
+    sel[...] = one_hot_slots(ids_ref[...], blocks).astype(BF)
     wait(copies)
     send_slots(sel, act2, pieces, outs, sems)
 
@@ -288,11 +284,13 @@
         [(act_ref.at[:, s * half : (s + 1) * half], act2.at[s * n : (s + 1) * n]) for s in range(2)],
         act_sems,
     )
-    sel[...] = one_hot_slots(ids_ref[...], blocks)
+    hits = one_hot_slots(ids_ref[...], blocks)
+    sel[...] = hits.astype(BF)
+    turned = hits.T.astype(BF)
     wait(copies)
     step = COLS
     for c in range(0, half, step):
-        sums = dot_t(sel[...], back[:, c : c + step])
+        sums = dot(turned, back[:, c : c + step])
         for s in range(2):
             rows = slice(s * n, (s + 1) * n)
             bias = bias_ref[:, s * half + c : s * half + c + step]
@@ -348,11 +346,12 @@
     left = left_rows(rows)
     pre = jnp.concatenate([pre_b[...], pre_a[...]], axis=0)
     sig = jax.nn.sigmoid(pre)
-    codes = split_halves(pre * sig, left).astype(BF)
+    codes = split_halves((pre * sig).astype(BF).astype(F32), left)
 
     def fill(terms, slots, first):
+        turned = terms.T.astype(BF)
         for g in range(groups // 2):
-            both = dot_t(terms, slots[:, g * quarter : (g + 1) * quarter]).astype(BF)
+            both = dot(turned, slots[:, g * quarter : (g + 1) * quarter]).astype(BF)
             for s in range(2):
                 pieces[g + s * (groups // 2), first : first + n, :] = both[s * n : (s + 1) * n]
 
@@ -375,7 +374,7 @@
     grads = split_halves(grad, left)
     bias = jnp.sum(grads[:, :n], axis=0, keepdims=True)
     wait(x_copies)
-    fill(grads.astype(BF), x, n)
+    fill(grads, x, n)
     for g in range(groups):
         shifted = pltpu.roll(bias, (n - g * (n // groups)) % n, 1)
         pieces[g, 2 * n :, :] = jnp.zeros((16, quarter), BF)
@@ -525,17 +524,19 @@
 
 def to_owners(slots):
     moved = along_z(slots[:SIDE])
-    crossed, merged = lax.optimization_barrier((over_x(slots[SIDE]), swap_pieces(moved, True)))
-    stream_a = over_x(merged)
-    stream_b = along_z(swap_pieces([crossed], False))
+    pieces = swap_pieces([over_x(slots[SIDE])], False)
+    pieces, moved = lax.optimization_barrier((pieces, moved))
+    stream_a = over_x(swap_pieces(moved, True))
+    stream_b = along_z(pieces)
     return stream_a, stream_b
 
 
 def to_homes(stream_a, stream_b):
     moved = along_z(stream_b, True)
-    crossed, merged = lax.optimization_barrier((over_x(stream_a), swap_pieces(moved, True)))
-    home_b = over_x(merged)
-    home_a = along_z(swap_pieces([crossed], False), True)
+    pieces = swap_pieces([over_x(stream_a)], False)
+    pieces, moved = lax.optimization_barrier((pieces, moved))
+    home_b = over_x(swap_pieces(moved, True))
+    home_a = along_z(pieces, True)
     return [*home_a, home_b]
 
 

time: 290 us -> 283 us (0.976)
  waiting for transfers between devices: 108 us -> 99.3 us
    ppermute x18, waiting for transfers between devices: 73.8 us -> 39 us  [shift_z(): return lax.ppermute(x, ('rows', 'lat'), pairs)]
    all_to_all x6, waiting for transfers between devices: 5.74 us -> 29.2 us  [over_x(): lax.all_to_all(x.reshape(members, shape[0] // members, shape[1]), 'lat',...]
    ppermute x6, waiting for transfers between devices: 28.2 us -> 31.1 us  [share_pieces(): got.append(lax.ppermute(pieces[k], 'rows', pairs))]
    unnamed x86 -> x98, local copies, waits for them, and re-layouts: 12.3 us -> 12.6 us
  transfers between devices with their start and end apart: 30 -> 30, of which waited for: 21 -> 19; matrix products, arithmetic and copies ran while one was open for 0% -> 0% of each run, Pallas kernels for 8% -> 5%
where the time goes in v6:
time: 283 us; the launch traced here: 281 us
  starting transfers between devices  120 us (42%)
  waiting for transfers between devices  99.3 us (35%)
  Pallas kernels  47.1 us (17%)
  local copies, waits for them, and re-layouts  13.2 us (5%)
    ppermute x18, starting transfers between devices, shift_z(): return lax.ppermute(x, ('rows', 'lat'), pairs)  56 us
    ppermute x18, waiting for transfers between devices, shift_z(): return lax.ppermute(x, ('rows', 'lat'), pairs)  39 us
    all_to_all x6, starting transfers between devices, over_x(): lax.all_to_all(x.reshape(members, shape[0] // members, shape[1]), 'lat',...  35.2 us
    ppermute x6, waiting for transfers between devices, share_pieces(): got.append(lax.ppermute(pieces[k], 'rows', pairs))  31.1 us
    all_to_all x6, waiting for transfers between devices, over_x(): lax.all_to_all(x.reshape(members, shape[0] // members, shape[1]), 'lat',...  29.2 us
    ppermute x6, starting transfers between devices, share_pieces(): got.append(lax.ppermute(pieces[k], 'rows', pairs))  28.9 us
    pallas_call x6, Pallas kernels, swap_pieces(): pl.pallas_call(functools.partial(swap_kernel, merge), in_specs=[ANY] * le...  17.2 us
    unnamed x98, local copies, waits for them, and re-layouts  12.6 us
  transfers between devices with their start and end apart: 30, of which 19 were waited for; matrix products, arithmetic and copies ran while one was open for 0% of the time, Pallas kernels for 5%

profile of v6, /device:TPU:1, one launch (start us, length us, event | category | flops | bytes accessed | tf_op | source)
XLA Modules:
  0.0 281.0 jit_solution(14008982180997107251)
XLA Ops:
  4.7 10.5 %all-to-all-start = ((bf16[8,48,1792]{2,1,0:T(8,128)(2,1)}), bf16[8,48,1792]{2,1,0:T(8,128)(2,1)S(1)}, u32[]{:S(2)}, u32[]{:S(2)}) async-start(bf16[8,48,1792]{2,1,0:T(8,128)(2,1)} %bitcast.29), calls=%async_computation | async-start | bytes 2752512 | tf_op jit(solution)/shard_map/all_to_all | solution.py:514
  17.1 7.7 %collective-permute-start.1 = (bf16[96,1792]{1,0:T(8,128)(2,1)S(1)}, bf16[96,1792]{1,0:T(8,128)(2,1)S(1)}, u32[]{:S(2)}, u32[]{:S(2)}) collective-permute-start(bf16[96,1792]{1,0:T(8,128)(2,1)S(1)} %copy-done.47), channel_id=1, source_target_pairs={{0,4},{1,101},{2,6},{3,103},{4,32},{5,1},{6,34},{7,3},{8,12},{9,10... | collective-permute-start | bytes 1032200 | tf_op jit(solution)/shard_map/ppermute | solution.py:504
  27.5 6.3 %all-to-all-done = bf16[8,48,1792]{2,1,0:T(8,128)(2,1)S(1)} async-done(((bf16[8,48,1792]{2,1,0:T(8,128)(2,1)}), bf16[8,48,1792]{2,1,0:T(8,128)(2,1)S(1)}, u32[]{:S(2)}, u32[]{:S(2)}) %all-to-all-start) | async-done | bytes 1376288 | tf_op jit(solution)/shard_map/all_to_all | solution.py:514
  43.7 4.7 %all-to-all-start.1 = ((bf16[8,48,1792]{2,1,0:T(8,128)(2,1)}), bf16[8,48,1792]{2,1,0:T(8,128)(2,1)S(1)}, u32[]{:S(2)}, u32[]{:S(2)}) async-start(bf16[8,48,1792]{2,1,0:T(8,128)(2,1)} %bitcast.27), calls=%async_computation.1 | async-start | bytes 2752512 | tf_op jit(solution)/shard_map/all_to_all | solution.py:514
  50.3 6.2 %collective-permute-start.4 = (bf16[96,1792]{1,0:T(8,128)(2,1)}, bf16[96,1792]{1,0:T(8,128)(2,1)}, u32[]{:S(2)}, u32[]{:S(2)}) collective-permute-start(bf16[96,1792]{1,0:T(8,128)(2,1)} %get-tuple-element.88), channel_id=1, source_target_pairs={{0,4},{1,101},{2,6},{3,103},{4,32},{5,1},{6,34},{7,3},{8,12},{9,10... | collective-permute-start | bytes 1032200 | tf_op jit(solution)/shard_map/ppermute | solution.py:504
  58.5 8.7 %all-to-all-done.1 = bf16[8,48,1792]{2,1,0:T(8,128)(2,1)S(1)} async-done(((bf16[8,48,1792]{2,1,0:T(8,128)(2,1)}), bf16[8,48,1792]{2,1,0:T(8,128)(2,1)S(1)}, u32[]{:S(2)}, u32[]{:S(2)}) %all-to-all-start.1) | async-done | bytes 1376288 | tf_op jit(solution)/shard_map/all_to_all | solution.py:514
  72.1 5.0 %all-to-all-start.2 = ((bf16[8,48,1792]{2,1,0:T(8,128)(2,1)}), bf16[8,48,1792]{2,1,0:T(8,128)(2,1)}, u32[]{:S(2)}, u32[]{:S(2)}) async-start(bf16[8,48,1792]{2,1,0:T(8,128)(2,1)} %bitcast.18), calls=%async_computation.2 | async-start | bytes 2752512 | tf_op jit(solution)/shard_map/all_to_all | solution.py:514
  82.8 5.0 %collective-permute-start.6 = (bf16[96,1792]{1,0:T(8,128)(2,1)}, bf16[96,1792]{1,0:T(8,128)(2,1)S(1)}, u32[]{:S(2)}, u32[]{:S(2)}) collective-permute-start(bf16[96,1792]{1,0:T(8,128)(2,1)} %get-tuple-element.102), channel_id=1, source_target_pairs={{0,102},{1,103},{2,0},{3,1},{4,2},{5,3},{6,4},{7,5},{8,110},{9,111... | collective-permute-start | bytes 1032200 | tf_op jit(solution)/shard_map/ppermute | solution.py:504
  109.5 5.7 %all-to-all-start.3 = ((bf16[8,48,1792]{2,1,0:T(8,128)(2,1)}), bf16[8,48,1792]{2,1,0:T(8,128)(2,1)S(1)}, u32[]{:S(2)}, u32[]{:S(2)}) async-start(bf16[8,48,1792]{2,1,0:T(8,128)(2,1)} %bitcast.23), calls=%async_computation.3 | async-start | bytes 2752512 | tf_op jit(solution)/shard_map/all_to_all | solution.py:514
  126.8 6.5 %collective-permute-done.10.refs_2_ = bf16[96,1792]{1,0:T(8,128)(2,1)S(1)} collective-permute-done((bf16[96,1792]{1,0:T(8,128)(2,1)S(1)}, bf16[96,1792]{1,0:T(8,128)(2,1)S(1)}, u32[]{:S(2)}, u32[]{:S(2)}) %collective-permute-start.10) | collective-permute-done | bytes 344096 | tf_op jit(solution)/shard_map/ppermute | solution.py:504
  133.2 5.3 %collective-permute-done.11.refs_3_ = bf16[96,1792]{1,0:T(8,128)(2,1)S(1)} collective-permute-done((bf16[96,1792]{1,0:T(8,128)(2,1)S(1)}, bf16[96,1792]{1,0:T(8,128)(2,1)S(1)}, u32[]{:S(2)}, u32[]{:S(2)}) %collective-permute-start.11) | collective-permute-done | bytes 344096 | tf_op jit(solution)/shard_map/ppermute | solution.py:504
  139.8 5.8 %error_rows.1 = (bf16[96,1792]{1,0:T(8,128)(2,1)}, bf16[96,1792]{1,0:T(8,128)(2,1)}, bf16[96,1792]{1,0:T(8,128)(2,1)}, bf16[96,1792]{1,0:T(8,128)(2,1)}, bf16[384,1792]{1,0:T(8,128)(2,1)}) custom-call(s32[2,128]{1,0:T(2,128)} %bitcast.31, f32[1,3584]{1,0:T(1,128)} %broadcast_in_dim.7.bias_ref, bf16[128,3584]{1,0:T(8,128)(2,1)} %act_ref.3, ...), custom_call_target="tpu_custom_call" | custom-call | tf_op jit(solution)/shard_map/error_rows/pallas_call | solution.py:307
  145.6 4.7 %all-to-all-start.4 = ((bf16[8,48,1792]{2,1,0:T(8,128)(2,1)}), bf16[8,48,1792]{2,1,0:T(8,128)(2,1)S(1)}, u32[]{:S(2)}, u32[]{:S(2)}) async-start(bf16[8,48,1792]{2,1,0:T(8,128)(2,1)} %bitcast.28), calls=%async_computation.4 | async-start | bytes 2752512 | tf_op jit(solution)/shard_map/all_to_all | solution.py:514
  158.9 10.0 %all-to-all-done.4 = bf16[8,48,1792]{2,1,0:T(8,128)(2,1)S(1)} async-done(((bf16[8,48,1792]{2,1,0:T(8,128)(2,1)}), bf16[8,48,1792]{2,1,0:T(8,128)(2,1)S(1)}, u32[]{:S(2)}, u32[]{:S(2)}) %all-to-all-start.4) | async-done | bytes 1376288 | tf_op jit(solution)/shard_map/all_to_all | solution.py:514
  183.3 5.3 %collective-permute-start.16 = (bf16[96,1792]{1,0:T(8,128)(2,1)S(1)}, bf16[96,1792]{1,0:T(8,128)(2,1)S(1)}, u32[]{:S(2)}, u32[]{:S(2)}) collective-permute-start(bf16[96,1792]{1,0:T(8,128)(2,1)S(1)} %copy-done.41), channel_id=1, source_target_pairs={{0,4},{1,101},{2,6},{3,103},{4,32},{5,1},{6,34},{7,3},{8,12},{9,10... | collective-permute-start | bytes 1032200 | tf_op jit(solution)/shard_map/ppermute | solution.py:504
  197.3 7.3 %collective-permute-done.17.refs_8_ = bf16[96,1792]{1,0:T(8,128)(2,1)S(1)} collective-permute-done((bf16[96,1792]{1,0:T(8,128)(2,1)S(1)}, bf16[96,1792]{1,0:T(8,128)(2,1)S(1)}, u32[]{:S(2)}, u32[]{:S(2)}) %collective-permute-start.17) | collective-permute-done | bytes 344096 | tf_op jit(solution)/shard_map/ppermute | solution.py:504
  205.9 9.1 %gradients.1 = (bf16[272,896]{1,0:T(8,128)(2,1)}, bf16[272,896]{1,0:T(8,128)(2,1)}, bf16[272,896]{1,0:T(8,128)(2,1)}, bf16[272,896]{1,0:T(8,128)(2,1)}) custom-call(f32[384,128]{1,0:T(8,128)} %copy-done.7, f32[384,128]{1,0:T(8,128)} %copy-done.8, bf16[128,3584]{1,0:T(8,128)(2,1)} %dec_ref.1, bf16[96,1792]{1,0:T(8,128)(2,1)} %get-tuple-element.91.refs_0_, ...), custom_call_target="tpu_custom_call" | custom-call | tf_op jit(solution)/shard_map/gradients/pallas_call | solution.py:395
  214.9 4.6 %collective-permute-start.18 = (bf16[272,896]{1,0:T(8,128)(2,1)}, bf16[272,896]{1,0:T(8,128)(2,1)S(1)}, u32[]{:S(2)}, u32[]{:S(2)}) collective-permute-start(bf16[272,896]{1,0:T(8,128)(2,1)} %get-tuple-element.131), channel_id=1, source_target_pairs={{0,256},{32,288},{64,320},{96,352},{128,384},{160,416},{192,448},{... | collective-permute-start | bytes 1462280 | tf_op jit(solution)/shard_map/ppermute | solution.py:484
  226.1 5.3 %collective-permute-done.18.refs_1_ = bf16[272,896]{1,0:T(8,128)(2,1)S(1)} collective-permute-done((bf16[272,896]{1,0:T(8,128)(2,1)}, bf16[272,896]{1,0:T(8,128)(2,1)S(1)}, u32[]{:S(2)}, u32[]{:S(2)}) %collective-permute-start.18) | collective-permute-done | bytes 487456 | tf_op jit(solution)/shard_map/ppermute | solution.py:484
  231.5 9.6 %collective-permute-done.19.refs_2_ = bf16[272,896]{1,0:T(8,128)(2,1)S(1)} collective-permute-done((bf16[272,896]{1,0:T(8,128)(2,1)}, bf16[272,896]{1,0:T(8,128)(2,1)S(1)}, u32[]{:S(2)}, u32[]{:S(2)}) %collective-permute-start.19) | collective-permute-done | bytes 487456 | tf_op jit(solution)/shard_map/ppermute | solution.py:484
  244.6 8.6 %collective-permute-start.21 = (bf16[240,256]{1,0:T(8,128)(2,1)}, bf16[240,256]{1,0:T(8,128)(2,1)S(1)}, u32[]{:S(2)}, u32[]{:S(2)}) collective-permute-start(bf16[240,256]{1,0:T(8,128)(2,1)} %get-tuple-element.135), channel_id=1, source_target_pairs={{0,64},{32,96},{64,0},{96,32},{128,192},{160,224},{192,128},{224,1... | collective-permute-start | bytes 368648 | tf_op jit(solution)/shard_map/ppermute | solution.py:484
  257.7 4.8 %collective-permute-start.23 = (bf16[240,256]{1,0:T(8,128)(2,1)}, bf16[240,256]{1,0:T(8,128)(2,1)S(1)}, u32[]{:S(2)}, u32[]{:S(2)}) collective-permute-start(bf16[240,256]{1,0:T(8,128)(2,1)} %get-tuple-element.137), channel_id=1, source_target_pairs={{0,96},{32,0},{64,32},{96,64},{128,224},{160,128},{192,160},{224,1... | collective-permute-start | bytes 368648 | tf_op jit(solution)/shard_map/ppermute | solution.py:484
  262.5 5.8 %collective-permute-done.21.refs_1_ = bf16[240,256]{1,0:T(8,128)(2,1)S(1)} collective-permute-done((bf16[240,256]{1,0:T(8,128)(2,1)}, bf16[240,256]{1,0:T(8,128)(2,1)S(1)}, u32[]{:S(2)}, u32[]{:S(2)}) %collective-permute-start.21) | collective-permute-done | bytes 122912 | tf_op jit(solution)/shard_map/ppermute | solution.py:484
  268.3 5.6 %collective-permute-done.22.refs_2_ = bf16[240,256]{1,0:T(8,128)(2,1)S(1)} collective-permute-done((bf16[240,256]{1,0:T(8,128)(2,1)}, bf16[240,256]{1,0:T(8,128)(2,1)S(1)}, u32[]{:S(2)}, u32[]{:S(2)}) %collective-permute-start.22) | collective-permute-done | bytes 122912 | tf_op jit(solution)/shard_map/ppermute | solution.py:484
  (148 shorter events, 121.5 us)
Async XLA Ops:
  4.7 29.1 %all-to-all-start = ((bf16[8,48,1792]{2,1,0:T(8,128)(2,1)}), bf16[8,48,1792]{2,1,0:T(8,128)(2,1)S(1)}, u32[]{:S(2)}, u32[]{:S(2)}) async-start(bf16[8,48,1792]{2,1,0:T(8,128)(2,1)} %bitcast.29), calls=%async_computation | async-start | bytes 2752512 | tf_op jit(solution)/shard_map/all_to_all | solution.py:514
  15.2 22.6 %collective-permute-start = (bf16[96,1792]{1,0:T(8,128)(2,1)S(1)}, bf16[96,1792]{1,0:T(8,128)(2,1)S(1)}, u32[]{:S(2)}, u32[]{:S(2)}) collective-permute-start(bf16[96,1792]{1,0:T(8,128)(2,1)S(1)} %copy-done.48), channel_id=1, source_target_pairs={{0,2},{1,3},{2,4},{3,5},{4,6},{5,7},{6,32},{7,33},{8,10},{9,11},{1... | collective-permute-start | bytes 1032200 | tf_op jit(solution)/shard_map/ppermute | solution.py:504
  17.1 20.7 %collective-permute-start.1 = (bf16[96,1792]{1,0:T(8,128)(2,1)S(1)}, bf16[96,1792]{1,0:T(8,128)(2,1)S(1)}, u32[]{:S(2)}, u32[]{:S(2)}) collective-permute-start(bf16[96,1792]{1,0:T(8,128)(2,1)S(1)} %copy-done.47), channel_id=1, source_target_pairs={{0,4},{1,101},{2,6},{3,103},{4,32},{5,1},{6,34},{7,3},{8,12},{9,10... | collective-permute-start | bytes 1032200 | tf_op jit(solution)/shard_map/ppermute | solution.py:504
  43.7 23.4 %all-to-all-start.1 = ((bf16[8,48,1792]{2,1,0:T(8,128)(2,1)}), bf16[8,48,1792]{2,1,0:T(8,128)(2,1)S(1)}, u32[]{:S(2)}, u32[]{:S(2)}) async-start(bf16[8,48,1792]{2,1,0:T(8,128)(2,1)} %bitcast.27), calls=%async_computation.1 | async-start | bytes 2752512 | tf_op jit(solution)/shard_map/all_to_all | solution.py:514
  48.4 23.7 %collective-permute-start.3 = (bf16[96,1792]{1,0:T(8,128)(2,1)}, bf16[96,1792]{1,0:T(8,128)(2,1)S(1)}, u32[]{:S(2)}, u32[]{:S(2)}) collective-permute-start(bf16[96,1792]{1,0:T(8,128)(2,1)} %get-tuple-element.87), channel_id=1, source_target_pairs={{0,2},{1,3},{2,4},{3,5},{4,6},{5,7},{6,32},{7,33},{8,10},{9,11},{1... | collective-permute-start | bytes 1032200 | tf_op jit(solution)/shard_map/ppermute | solution.py:504
  50.3 21.8 %collective-permute-start.4 = (bf16[96,1792]{1,0:T(8,128)(2,1)}, bf16[96,1792]{1,0:T(8,128)(2,1)}, u32[]{:S(2)}, u32[]{:S(2)}) collective-permute-start(bf16[96,1792]{1,0:T(8,128)(2,1)} %get-tuple-element.88), channel_id=1, source_target_pairs={{0,4},{1,101},{2,6},{3,103},{4,32},{5,1},{6,34},{7,3},{8,12},{9,10... | collective-permute-start | bytes 1032200 | tf_op jit(solution)/shard_map/ppermute | solution.py:504
  56.5 15.6 %collective-permute-start.5 = (bf16[96,1792]{1,0:T(8,128)(2,1)}, bf16[96,1792]{1,0:T(8,128)(2,1)}, u32[]{:S(2)}, u32[]{:S(2)}) collective-permute-start(bf16[96,1792]{1,0:T(8,128)(2,1)} %get-tuple-element.89), channel_id=1, source_target_pairs={{0,102},{1,103},{2,0},{3,1},{4,2},{5,3},{6,4},{7,5},{8,110},{9,111... | collective-permute-start | bytes 1032200 | tf_op jit(solution)/shard_map/ppermute | solution.py:504
  72.1 23.8 %all-to-all-start.2 = ((bf16[8,48,1792]{2,1,0:T(8,128)(2,1)}), bf16[8,48,1792]{2,1,0:T(8,128)(2,1)}, u32[]{:S(2)}, u32[]{:S(2)}) async-start(bf16[8,48,1792]{2,1,0:T(8,128)(2,1)} %bitcast.18), calls=%async_computation.2 | async-start | bytes 2752512 | tf_op jit(solution)/shard_map/all_to_all | solution.py:514
  82.8 15.9 %collective-permute-start.6 = (bf16[96,1792]{1,0:T(8,128)(2,1)}, bf16[96,1792]{1,0:T(8,128)(2,1)S(1)}, u32[]{:S(2)}, u32[]{:S(2)}) collective-permute-start(bf16[96,1792]{1,0:T(8,128)(2,1)} %get-tuple-element.102), channel_id=1, source_target_pairs={{0,102},{1,103},{2,0},{3,1},{4,2},{5,3},{6,4},{7,5},{8,110},{9,111... | collective-permute-start | bytes 1032200 | tf_op jit(solution)/shard_map/ppermute | solution.py:504
  89.8 16.0 %collective-permute-start.8 = (bf16[96,1792]{1,0:T(8,128)(2,1)S(1)}, bf16[96,1792]{1,0:T(8,128)(2,1)S(1)}, u32[]{:S(2)}, u32[]{:S(2)}) collective-permute-start(bf16[96,1792]{1,0:T(8,128)(2,1)S(1)} %get-tuple-element.104), channel_id=1, source_target_pairs={{0,2},{1,3},{2,4},{3,5},{4,6},{5,7},{6,32},{7,33},{8,10},{9,11},{1... | collective-permute-start | bytes 1032200 | tf_op jit(solution)/shard_map/ppermute | solution.py:504
  109.5 29.1 %all-to-all-start.3 = ((bf16[8,48,1792]{2,1,0:T(8,128)(2,1)}), bf16[8,48,1792]{2,1,0:T(8,128)(2,1)S(1)}, u32[]{:S(2)}, u32[]{:S(2)}) async-start(bf16[8,48,1792]{2,1,0:T(8,128)(2,1)} %bitcast.23), calls=%async_computation.3 | async-start | bytes 2752512 | tf_op jit(solution)/shard_map/all_to_all | solution.py:514
  120.4 18.2 %collective-permute-start.11 = (bf16[96,1792]{1,0:T(8,128)(2,1)S(1)}, bf16[96,1792]{1,0:T(8,128)(2,1)S(1)}, u32[]{:S(2)}, u32[]{:S(2)}) collective-permute-start(bf16[96,1792]{1,0:T(8,128)(2,1)S(1)} %copy-done.37), channel_id=1, source_target_pairs={{0,2},{1,3},{2,4},{3,5},{4,6},{5,7},{6,32},{7,33},{8,10},{9,11},{1... | collective-permute-start | bytes 1032200 | tf_op jit(solution)/shard_map/ppermute | solution.py:504
  145.6 23.3 %all-to-all-start.4 = ((bf16[8,48,1792]{2,1,0:T(8,128)(2,1)}), bf16[8,48,1792]{2,1,0:T(8,128)(2,1)S(1)}, u32[]{:S(2)}, u32[]{:S(2)}) async-start(bf16[8,48,1792]{2,1,0:T(8,128)(2,1)} %bitcast.28), calls=%async_computation.4 | async-start | bytes 2752512 | tf_op jit(solution)/shard_map/all_to_all | solution.py:514
  150.3 22.6 %collective-permute-start.12 = (bf16[96,1792]{1,0:T(8,128)(2,1)S(1)}, bf16[96,1792]{1,0:T(8,128)(2,1)S(1)}, u32[]{:S(2)}, u32[]{:S(2)}) collective-permute-start(bf16[96,1792]{1,0:T(8,128)(2,1)S(1)} %copy-done.46), channel_id=1, source_target_pairs={{0,2},{1,3},{2,4},{3,5},{4,6},{5,7},{6,32},{7,33},{8,10},{9,11},{1... | collective-permute-start | bytes 1032200 | tf_op jit(solution)/shard_map/ppermute | solution.py:504
  152.4 20.5 %collective-permute-start.13 = (bf16[96,1792]{1,0:T(8,128)(2,1)S(1)}, bf16[96,1792]{1,0:T(8,128)(2,1)S(1)}, u32[]{:S(2)}, u32[]{:S(2)}) collective-permute-start(bf16[96,1792]{1,0:T(8,128)(2,1)S(1)} %copy-done.42), channel_id=1, source_target_pairs={{0,4},{1,101},{2,6},{3,103},{4,32},{5,1},{6,34},{7,3},{8,12},{9,10... | collective-permute-start | bytes 1032200 | tf_op jit(solution)/shard_map/ppermute | solution.py:504
  156.2 16.7 %collective-permute-start.14 = (bf16[96,1792]{1,0:T(8,128)(2,1)S(1)}, bf16[96,1792]{1,0:T(8,128)(2,1)S(1)}, u32[]{:S(2)}, u32[]{:S(2)}) collective-permute-start(bf16[96,1792]{1,0:T(8,128)(2,1)S(1)} %copy-done.39), channel_id=1, source_target_pairs={{0,102},{1,103},{2,0},{3,1},{4,2},{5,3},{6,4},{7,5},{8,110},{9,111... | collective-permute-start | bytes 1032200 | tf_op jit(solution)/shard_map/ppermute | solution.py:504
  176.8 27.8 %all-to-all-start.5 = ((bf16[8,48,1792]{2,1,0:T(8,128)(2,1)}), bf16[8,48,1792]{2,1,0:T(8,128)(2,1)S(1)}, u32[]{:S(2)}, u32[]{:S(2)}) async-start(bf16[8,48,1792]{2,1,0:T(8,128)(2,1)} %bitcast.24), calls=%async_computation.5 | async-start | bytes 2752512 | tf_op jit(solution)/shard_map/all_to_all | solution.py:514
  188.5 16.1 %collective-permute-start.17 = (bf16[96,1792]{1,0:T(8,128)(2,1)S(1)}, bf16[96,1792]{1,0:T(8,128)(2,1)S(1)}, u32[]{:S(2)}, u32[]{:S(2)}) collective-permute-start(bf16[96,1792]{1,0:T(8,128)(2,1)S(1)} %copy-done.38), channel_id=1, source_target_pairs={{0,102},{1,103},{2,0},{3,1},{4,2},{5,3},{6,4},{7,5},{8,110},{9,111... | collective-permute-start | bytes 1032200 | tf_op jit(solution)/shard_map/ppermute | solution.py:504
  214.9 16.5 %collective-permute-start.18 = (bf16[272,896]{1,0:T(8,128)(2,1)}, bf16[272,896]{1,0:T(8,128)(2,1)S(1)}, u32[]{:S(2)}, u32[]{:S(2)}) collective-permute-start(bf16[272,896]{1,0:T(8,128)(2,1)} %get-tuple-element.131), channel_id=1, source_target_pairs={{0,256},{32,288},{64,320},{96,352},{128,384},{160,416},{192,448},{... | collective-permute-start | bytes 1462280 | tf_op jit(solution)/shard_map/ppermute | solution.py:484
  219.6 21.5 %collective-permute-start.19 = (bf16[272,896]{1,0:T(8,128)(2,1)}, bf16[272,896]{1,0:T(8,128)(2,1)S(1)}, u32[]{:S(2)}, u32[]{:S(2)}) collective-permute-start(bf16[272,896]{1,0:T(8,128)(2,1)} %get-tuple-element.132), channel_id=1, source_target_pairs={{0,128},{32,160},{64,192},{96,224},{128,256},{160,288},{192,320},{... | collective-permute-start | bytes 1462280 | tf_op jit(solution)/shard_map/ppermute | solution.py:484
  221.9 19.3 %collective-permute-start.20 = (bf16[272,896]{1,0:T(8,128)(2,1)}, bf16[272,896]{1,0:T(8,128)(2,1)S(1)}, u32[]{:S(2)}, u32[]{:S(2)}) collective-permute-start(bf16[272,896]{1,0:T(8,128)(2,1)} %get-tuple-element.133), channel_id=1, source_target_pairs={{0,384},{32,416},{64,448},{96,480},{128,0},{160,32},{192,64},{224,... | collective-permute-start | bytes 1462280 | tf_op jit(solution)/shard_map/ppermute | solution.py:484
  244.6 23.7 %collective-permute-start.21 = (bf16[240,256]{1,0:T(8,128)(2,1)}, bf16[240,256]{1,0:T(8,128)(2,1)S(1)}, u32[]{:S(2)}, u32[]{:S(2)}) collective-permute-start(bf16[240,256]{1,0:T(8,128)(2,1)} %get-tuple-element.135), channel_id=1, source_target_pairs={{0,64},{32,96},{64,0},{96,32},{128,192},{160,224},{192,128},{224,1... | collective-permute-start | bytes 368648 | tf_op jit(solution)/shard_map/ppermute | solution.py:484
  253.3 20.7 %collective-permute-start.22 = (bf16[240,256]{1,0:T(8,128)(2,1)}, bf16[240,256]{1,0:T(8,128)(2,1)S(1)}, u32[]{:S(2)}, u32[]{:S(2)}) collective-permute-start(bf16[240,256]{1,0:T(8,128)(2,1)} %get-tuple-element.136), channel_id=1, source_target_pairs={{0,32},{32,64},{64,96},{96,0},{128,160},{160,192},{192,224},{224,1... | collective-permute-start | bytes 368648 | tf_op jit(solution)/shard_map/ppermute | solution.py:484
  257.7 20.8 %collective-permute-start.23 = (bf16[240,256]{1,0:T(8,128)(2,1)}, bf16[240,256]{1,0:T(8,128)(2,1)S(1)}, u32[]{:S(2)}, u32[]{:S(2)}) collective-permute-start(bf16[240,256]{1,0:T(8,128)(2,1)} %get-tuple-element.137), channel_id=1, source_target_pairs={{0,96},{32,0},{64,32},{96,64},{128,224},{160,128},{192,160},{224,1... | collective-permute-start | bytes 368648 | tf_op jit(solution)/shard_map/ppermute | solution.py:484
  (55 other events, 365.7 us)

commit v7 on v6

--- a/solution.py
+++ b/solution.py
@@ -148,66 +148,58 @@
     )(ids, act)
 
 
-def swap_kernel(merge, *refs):
-    if merge:
-        ins, out_ref, (pieces, done, in_sems, sems) = refs[:SIDE], refs[SIDE], refs[SIDE + 1 :]
-    else:
-        in_ref, outs, (pieces, done, in_sems, sems) = refs[0], refs[1 : SIDE + 1], refs[SIDE + 1 :]
+def turn_kernel(*refs):
+    moved, crossed, merged, split = refs[:SIDE], refs[SIDE], refs[SIDE + 1], refs[SIDE + 2 : -4]
+    pieces, done, in_sems, sems = refs[-4:]
     rows = pieces.shape[1]
     part = rows // SIDE
-    halves = range(2)
-    if merge:
-        moves = [
-            [
-                (ins[k].at[h * part : (h + 1) * part], pieces.at[h, k * part : (k + 1) * part])
-                for k in range(SIDE)
-            ]
-            for h in halves
+
+    def by_step(arrays, buffer, h):
+        return [
+            (arrays[k].at[h * part : (h + 1) * part], buffer.at[h, k * part : (k + 1) * part])
+            for k in range(SIDE)
         ]
-    else:
-        moves = [[(in_ref.at[h * rows : (h + 1) * rows], pieces.at[h])] for h in halves]
-    copies = [start(moves[h], in_sems, h * SIDE) for h in halves]
+
+    copies = [start(by_step(moved, pieces, h), in_sems, h * SIDE) for h in range(2)]
+    copies += [
+        start([(crossed.at[h * rows : (h + 1) * rows], pieces.at[2 + h])], in_sems, 2 * SIDE + h)
+        for h in range(2)
+    ]
     row = lax.broadcasted_iota(jnp.int32, (rows, 1), 0)
     piece = by_twelve(row)
     source = (piece & 3) * part + lax.shift_right_logical(piece, 2) * PAIR + row - piece * PAIR
     turn = (lax.broadcasted_iota(jnp.int32, (rows, rows), 1) == source).astype(F32).astype(BF)
     sent = []
-    for h in halves:
-        wait(copies[h])
-        done[h] = dot(turn, pieces[h]).astype(BF)
-        if merge:
-            sent += start([(done.at[h], out_ref.at[h * rows : (h + 1) * rows])], sems, h * SIDE)
+    for i in range(4):
+        wait(copies[i])
+        done[i] = dot(turn, pieces[i]).astype(BF)
+        if i < 2:
+            pairs = [(done.at[i], merged.at[i * rows : (i + 1) * rows])]
         else:
-            sent += start(
-                [
-                    (done.at[h, k * part : (k + 1) * part], outs[k].at[h * part : (h + 1) * part])
-                    for k in range(SIDE)
-                ],
-                sems,
-                h * SIDE,
-            )
+            pairs = [(b, a) for a, b in by_step(split, done.at[2:], i - 2)]
+        sent += start(pairs, sems, i * SIDE)
     wait(sent)
 
 
-def swap_pieces(arrays, merge):
-    total = arrays[0].shape[0] * (SIDE if merge else 1)
-    half = arrays[0].shape[1]
+def turn_pieces(moved, crossed):
+    total, half = crossed.shape
     shape = jax.ShapeDtypeStruct((total, half), BF)
     shapes = [jax.ShapeDtypeStruct((total // SIDE, half), BF)] * SIDE
-    return pl.pallas_call(
-        functools.partial(swap_kernel, merge),
-        in_specs=[ANY] * len(arrays),
-        out_specs=ANY if merge else [ANY] * SIDE,
-        out_shape=shape if merge else shapes,
+    merged, *split = pl.pallas_call(
+        turn_kernel,
+        in_specs=[ANY] * (SIDE + 1),
+        out_specs=[ANY] * (SIDE + 1),
+        out_shape=[shape] + shapes,
         scratch_shapes=[
-            pltpu.VMEM((2, total // 2, half), BF),
-            pltpu.VMEM((2, total // 2, half), BF),
-            pltpu.SemaphoreType.DMA((2 * SIDE,)),
-            pltpu.SemaphoreType.DMA((2 * SIDE,)),
+            pltpu.VMEM((4, total // 2, half), BF),
+            pltpu.VMEM((4, total // 2, half), BF),
+            pltpu.SemaphoreType.DMA((2 * SIDE + 2,)),
+            pltpu.SemaphoreType.DMA((4 * SIDE,)),
         ],
         compiler_params=PARAMS,
-        name="merge_pieces" if merge else "split_pieces",
-    )(*arrays)
+        name="turn_pieces",
+    )(*moved, crossed)
+    return merged, split
 
 
 def code_kernel(parts, *refs):
@@ -524,18 +516,16 @@
 
 def to_owners(slots):
     moved = along_z(slots[:SIDE])
-    pieces = swap_pieces([over_x(slots[SIDE])], False)
-    pieces, moved = lax.optimization_barrier((pieces, moved))
-    stream_a = over_x(swap_pieces(moved, True))
+    merged, pieces = turn_pieces(moved, over_x(slots[SIDE]))
+    stream_a = over_x(merged)
     stream_b = along_z(pieces)
     return stream_a, stream_b
 
 
 def to_homes(stream_a, stream_b):
     moved = along_z(stream_b, True)
-    pieces = swap_pieces([over_x(stream_a)], False)
-    pieces, moved = lax.optimization_barrier((pieces, moved))
-    home_b = over_x(swap_pieces(moved, True))
+    merged, pieces = turn_pieces(moved, over_x(stream_a))
+    home_b = over_x(merged)
     home_a = along_z(pieces, True)
     return [*home_a, home_b]
 

time: 283 us -> 284 us (level)
  waiting for transfers between devices: 99.3 us -> 108 us
  Pallas kernels: 47.1 us -> 40.6 us
    ppermute x18, waiting for transfers between devices: 39 us -> 70.6 us  [shift_z(): return lax.ppermute(x, ('rows', 'lat'), pairs)]
    all_to_all x6, waiting for transfers between devices: 29.2 us -> 8.68 us  [over_x(): lax.all_to_all(x.reshape(members, shape[0] // members, shape[1]), 'lat',...]
    pallas_call x6 -> x3, Pallas kernels: 17.2 us -> 11.1 us  [turn_pieces(): pl.pallas_call(turn_kernel, in_specs=[ANY] * (SIDE + 1), out_specs=[ANY]...]
  transfers between devices with their start and end apart: 30 -> 30, of which waited for: 19 -> 21; matrix products, arithmetic and copies ran while one was open for 0% -> 0% of each run, Pallas kernels for 5% -> 2%
where the time goes in v7:
time: 284 us; the launch traced here: 283 us
  starting transfers between devices  121 us (43%)
  waiting for transfers between devices  108 us (38%)
  Pallas kernels  40.6 us (14%)
  local copies, waits for them, and re-layouts  11.6 us (4%)
    ppermute x18, waiting for transfers between devices, shift_z(): return lax.ppermute(x, ('rows', 'lat'), pairs)  70.6 us
    ppermute x18, starting transfers between devices, shift_z(): return lax.ppermute(x, ('rows', 'lat'), pairs)  56 us
    all_to_all x6, starting transfers between devices, over_x(): lax.all_to_all(x.reshape(members, shape[0] // members, shape[1]), 'lat',...  34.9 us
    ppermute x6, starting transfers between devices, share_pieces(): got.append(lax.ppermute(pieces[k], 'rows', pairs))  29.9 us
    ppermute x6, waiting for transfers between devices, share_pieces(): got.append(lax.ppermute(pieces[k], 'rows', pairs))  29.2 us
    pallas_call x3, Pallas kernels, turn_pieces(): pl.pallas_call(turn_kernel, in_specs=[ANY] * (SIDE + 1), out_specs=[ANY]...  11.1 us
    unnamed x98, local copies, waits for them, and re-layouts  11 us
    pallas_call x1, Pallas kernels, gradients(): pl.pallas_call(grad_kernel, in_specs=[in_vmem, in_vmem] + [ANY] * (2 * SI...  9.06 us
  transfers between devices with their start and end apart: 30, of which 21 were waited for; matrix products, arithmetic and copies ran while one was open for 0% of the time, Pallas kernels for 2%

profile of v7, /device:TPU:1, one launch (start us, length us, event | category | flops | bytes accessed | tf_op | source)
XLA Modules:
  0.0 282.8 jit_solution(1521973435492998550)
XLA Ops:
  4.7 10.5 %all-to-all-start = ((bf16[8,48,1792]{2,1,0:T(8,128)(2,1)}), bf16[8,48,1792]{2,1,0:T(8,128)(2,1)S(1)}, u32[]{:S(2)}, u32[]{:S(2)}) async-start(bf16[8,48,1792]{2,1,0:T(8,128)(2,1)} %bitcast.28), calls=%async_computation | async-start | bytes 2752512 | tf_op jit(solution)/shard_map/all_to_all | solution.py:506
  17.1 7.7 %collective-permute-start.1 = (bf16[96,1792]{1,0:T(8,128)(2,1)S(1)}, bf16[96,1792]{1,0:T(8,128)(2,1)S(1)}, u32[]{:S(2)}, u32[]{:S(2)}) collective-permute-start(bf16[96,1792]{1,0:T(8,128)(2,1)S(1)} %copy-done.47), channel_id=1, source_target_pairs={{0,4},{1,101},{2,6},{3,103},{4,32},{5,1},{6,34},{7,3},{8,12},{9,10... | collective-permute-start | bytes 1032200 | tf_op jit(solution)/shard_map/ppermute | solution.py:496
  30.1 5.4 %collective-permute-done.1.refs_2_ = bf16[96,1792]{1,0:T(8,128)(2,1)S(1)} collective-permute-done((bf16[96,1792]{1,0:T(8,128)(2,1)S(1)}, bf16[96,1792]{1,0:T(8,128)(2,1)S(1)}, u32[]{:S(2)}, u32[]{:S(2)}) %collective-permute-start.1) | collective-permute-done | bytes 344096 | tf_op jit(solution)/shard_map/ppermute | solution.py:496
  45.0 4.7 %all-to-all-start.1 = ((bf16[8,48,1792]{2,1,0:T(8,128)(2,1)}), bf16[8,48,1792]{2,1,0:T(8,128)(2,1)S(1)}, u32[]{:S(2)}, u32[]{:S(2)}) async-start(bf16[8,48,1792]{2,1,0:T(8,128)(2,1)} %bitcast.29), calls=%async_computation.1 | async-start | bytes 2752512 | tf_op jit(solution)/shard_map/all_to_all | solution.py:506
  51.6 6.2 %collective-permute-start.4 = (bf16[96,1792]{1,0:T(8,128)(2,1)}, bf16[96,1792]{1,0:T(8,128)(2,1)}, u32[]{:S(2)}, u32[]{:S(2)}) collective-permute-start(bf16[96,1792]{1,0:T(8,128)(2,1)} %get-tuple-element.60), channel_id=1, source_target_pairs={{0,4},{1,101},{2,6},{3,103},{4,32},{5,1},{6,34},{7,3},{8,12},{9,10... | collective-permute-start | bytes 1032200 | tf_op jit(solution)/shard_map/ppermute | solution.py:496
  59.7 8.7 %all-to-all-done.1 = bf16[8,48,1792]{2,1,0:T(8,128)(2,1)S(1)} async-done(((bf16[8,48,1792]{2,1,0:T(8,128)(2,1)}), bf16[8,48,1792]{2,1,0:T(8,128)(2,1)S(1)}, u32[]{:S(2)}, u32[]{:S(2)}) %all-to-all-start.1) | async-done | bytes 1376288 | tf_op jit(solution)/shard_map/all_to_all | solution.py:506
  73.4 5.1 %all-to-all-start.2 = ((bf16[8,48,1792]{2,1,0:T(8,128)(2,1)}), bf16[8,48,1792]{2,1,0:T(8,128)(2,1)}, u32[]{:S(2)}, u32[]{:S(2)}) async-start(bf16[8,48,1792]{2,1,0:T(8,128)(2,1)} %bitcast.18), calls=%async_computation.2 | async-start | bytes 2752512 | tf_op jit(solution)/shard_map/all_to_all | solution.py:506
  83.7 5.0 %collective-permute-start.6 = (bf16[96,1792]{1,0:T(8,128)(2,1)S(1)}, bf16[96,1792]{1,0:T(8,128)(2,1)S(1)}, u32[]{:S(2)}, u32[]{:S(2)}) collective-permute-start(bf16[96,1792]{1,0:T(8,128)(2,1)S(1)} %get-tuple-element.69), channel_id=1, source_target_pairs={{0,102},{1,103},{2,0},{3,1},{4,2},{5,3},{6,4},{7,5},{8,110},{9,111... | collective-permute-start | bytes 1032200 | tf_op jit(solution)/shard_map/ppermute | solution.py:496
  92.6 6.0 %collective-permute-done.6.refs_1_ = bf16[96,1792]{1,0:T(8,128)(2,1)S(1)} collective-permute-done((bf16[96,1792]{1,0:T(8,128)(2,1)S(1)}, bf16[96,1792]{1,0:T(8,128)(2,1)S(1)}, u32[]{:S(2)}, u32[]{:S(2)}) %collective-permute-start.6) | collective-permute-done | bytes 344096 | tf_op jit(solution)/shard_map/ppermute | solution.py:496
  98.6 5.2 %collective-permute-done.7.refs_2_ = bf16[96,1792]{1,0:T(8,128)(2,1)S(1)} collective-permute-done((bf16[96,1792]{1,0:T(8,128)(2,1)S(1)}, bf16[96,1792]{1,0:T(8,128)(2,1)S(1)}, u32[]{:S(2)}, u32[]{:S(2)}) %collective-permute-start.7) | collective-permute-done | bytes 344096 | tf_op jit(solution)/shard_map/ppermute | solution.py:496
  111.7 5.3 %all-to-all-start.3 = ((bf16[8,48,1792]{2,1,0:T(8,128)(2,1)}), bf16[8,48,1792]{2,1,0:T(8,128)(2,1)S(1)}, u32[]{:S(2)}, u32[]{:S(2)}) async-start(bf16[8,48,1792]{2,1,0:T(8,128)(2,1)} %bitcast.25), calls=%async_computation.3 | async-start | bytes 2752512 | tf_op jit(solution)/shard_map/all_to_all | solution.py:506
  128.5 6.8 %collective-permute-done.10.refs_2_ = bf16[96,1792]{1,0:T(8,128)(2,1)S(1)} collective-permute-done((bf16[96,1792]{1,0:T(8,128)(2,1)S(1)}, bf16[96,1792]{1,0:T(8,128)(2,1)S(1)}, u32[]{:S(2)}, u32[]{:S(2)}) %collective-permute-start.10) | collective-permute-done | bytes 344096 | tf_op jit(solution)/shard_map/ppermute | solution.py:496
  135.3 5.0 %collective-permute-done.11.refs_3_ = bf16[96,1792]{1,0:T(8,128)(2,1)S(1)} collective-permute-done((bf16[96,1792]{1,0:T(8,128)(2,1)S(1)}, bf16[96,1792]{1,0:T(8,128)(2,1)S(1)}, u32[]{:S(2)}, u32[]{:S(2)}) %collective-permute-start.11) | collective-permute-done | bytes 344096 | tf_op jit(solution)/shard_map/ppermute | solution.py:496
  141.6 5.7 %error_rows.1 = (bf16[96,1792]{1,0:T(8,128)(2,1)}, bf16[96,1792]{1,0:T(8,128)(2,1)}, bf16[96,1792]{1,0:T(8,128)(2,1)}, bf16[96,1792]{1,0:T(8,128)(2,1)}, bf16[384,1792]{1,0:T(8,128)(2,1)}) custom-call(s32[2,128]{1,0:T(2,128)} %bitcast.31, f32[1,3584]{1,0:T(1,128)} %broadcast_in_dim.7.bias_ref, bf16[128,3584]{1,0:T(8,128)(2,1)} %act_ref.3, ...), custom_call_target="tpu_custom_call" | custom-call | tf_op jit(solution)/shard_map/error_rows/pallas_call | solution.py:299
  160.7 4.8 %collective-permute-done.12.refs_1_ = bf16[96,1792]{1,0:T(8,128)(2,1)S(1)} collective-permute-done((bf16[96,1792]{1,0:T(8,128)(2,1)S(1)}, bf16[96,1792]{1,0:T(8,128)(2,1)S(1)}, u32[]{:S(2)}, u32[]{:S(2)}) %collective-permute-start.12) | collective-permute-done | bytes 344096 | tf_op jit(solution)/shard_map/ppermute | solution.py:496
  165.5 9.0 %collective-permute-done.14.refs_3_ = bf16[96,1792]{1,0:T(8,128)(2,1)S(1)} collective-permute-done((bf16[96,1792]{1,0:T(8,128)(2,1)S(1)}, bf16[96,1792]{1,0:T(8,128)(2,1)S(1)}, u32[]{:S(2)}, u32[]{:S(2)}) %collective-permute-start.14) | collective-permute-done | bytes 344096 | tf_op jit(solution)/shard_map/ppermute | solution.py:496
  186.1 5.2 %collective-permute-start.16 = (bf16[96,1792]{1,0:T(8,128)(2,1)S(1)}, bf16[96,1792]{1,0:T(8,128)(2,1)S(1)}, u32[]{:S(2)}, u32[]{:S(2)}) collective-permute-start(bf16[96,1792]{1,0:T(8,128)(2,1)S(1)} %copy-done.42), channel_id=1, source_target_pairs={{0,4},{1,101},{2,6},{3,103},{4,32},{5,1},{6,34},{7,3},{8,12},{9,10... | collective-permute-start | bytes 1032200 | tf_op jit(solution)/shard_map/ppermute | solution.py:496
  200.4 7.1 %collective-permute-done.17.refs_8_ = bf16[96,1792]{1,0:T(8,128)(2,1)S(1)} collective-permute-done((bf16[96,1792]{1,0:T(8,128)(2,1)S(1)}, bf16[96,1792]{1,0:T(8,128)(2,1)S(1)}, u32[]{:S(2)}, u32[]{:S(2)}) %collective-permute-start.17) | collective-permute-done | bytes 344096 | tf_op jit(solution)/shard_map/ppermute | solution.py:496
  208.7 9.1 %gradients.1 = (bf16[272,896]{1,0:T(8,128)(2,1)}, bf16[272,896]{1,0:T(8,128)(2,1)}, bf16[272,896]{1,0:T(8,128)(2,1)}, bf16[272,896]{1,0:T(8,128)(2,1)}) custom-call(f32[384,128]{1,0:T(8,128)} %copy-done.7, f32[384,128]{1,0:T(8,128)} %copy-done.8, bf16[128,3584]{1,0:T(8,128)(2,1)} %dec_ref.1, bf16[96,1792]{1,0:T(8,128)(2,1)} %get-tuple-element.63.refs_0_, ...), custom_call_target="tpu_custom_call" | custom-call | tf_op jit(solution)/shard_map/gradients/pallas_call | solution.py:387
  228.9 5.4 %collective-permute-done.18.refs_1_ = bf16[272,896]{1,0:T(8,128)(2,1)S(1)} collective-permute-done((bf16[272,896]{1,0:T(8,128)(2,1)}, bf16[272,896]{1,0:T(8,128)(2,1)S(1)}, u32[]{:S(2)}, u32[]{:S(2)}) %collective-permute-start.18) | collective-permute-done | bytes 487456 | tf_op jit(solution)/shard_map/ppermute | solution.py:476
  234.3 9.6 %collective-permute-done.19.refs_2_ = bf16[272,896]{1,0:T(8,128)(2,1)S(1)} collective-permute-done((bf16[272,896]{1,0:T(8,128)(2,1)}, bf16[272,896]{1,0:T(8,128)(2,1)S(1)}, u32[]{:S(2)}, u32[]{:S(2)}) %collective-permute-start.19) | collective-permute-done | bytes 487456 | tf_op jit(solution)/shard_map/ppermute | solution.py:476
  247.5 9.6 %collective-permute-start.21 = (bf16[240,256]{1,0:T(8,128)(2,1)}, bf16[240,256]{1,0:T(8,128)(2,1)S(1)}, u32[]{:S(2)}, u32[]{:S(2)}) collective-permute-start(bf16[240,256]{1,0:T(8,128)(2,1)} %get-tuple-element.93), channel_id=1, source_target_pairs={{0,64},{32,96},{64,0},{96,32},{128,192},{160,224},{192,128},{224,1... | collective-permute-start | bytes 368648 | tf_op jit(solution)/shard_map/ppermute | solution.py:476
  260.9 5.3 %collective-permute-start.23 = (bf16[240,256]{1,0:T(8,128)(2,1)}, bf16[240,256]{1,0:T(8,128)(2,1)S(1)}, u32[]{:S(2)}, u32[]{:S(2)}) collective-permute-start(bf16[240,256]{1,0:T(8,128)(2,1)} %get-tuple-element.95), channel_id=1, source_target_pairs={{0,96},{32,0},{64,32},{96,64},{128,224},{160,128},{192,160},{224,1... | collective-permute-start | bytes 368648 | tf_op jit(solution)/shard_map/ppermute | solution.py:476
  266.2 5.3 %collective-permute-done.21.refs_1_ = bf16[240,256]{1,0:T(8,128)(2,1)S(1)} collective-permute-done((bf16[240,256]{1,0:T(8,128)(2,1)}, bf16[240,256]{1,0:T(8,128)(2,1)S(1)}, u32[]{:S(2)}, u32[]{:S(2)}) %collective-permute-start.21) | collective-permute-done | bytes 122912 | tf_op jit(solution)/shard_map/ppermute | solution.py:476
  (145 shorter events, 123.9 us)
Async XLA Ops:
  4.7 35.4 %all-to-all-start = ((bf16[8,48,1792]{2,1,0:T(8,128)(2,1)}), bf16[8,48,1792]{2,1,0:T(8,128)(2,1)S(1)}, u32[]{:S(2)}, u32[]{:S(2)}) async-start(bf16[8,48,1792]{2,1,0:T(8,128)(2,1)} %bitcast.28), calls=%async_computation | async-start | bytes 2752512 | tf_op jit(solution)/shard_map/all_to_all | solution.py:506
  15.1 15.0 %collective-permute-start = (bf16[96,1792]{1,0:T(8,128)(2,1)S(1)}, bf16[96,1792]{1,0:T(8,128)(2,1)S(1)}, u32[]{:S(2)}, u32[]{:S(2)}) collective-permute-start(bf16[96,1792]{1,0:T(8,128)(2,1)S(1)} %copy-done.48), channel_id=1, source_target_pairs={{0,2},{1,3},{2,4},{3,5},{4,6},{5,7},{6,32},{7,33},{8,10},{9,11},{1... | collective-permute-start | bytes 1032200 | tf_op jit(solution)/shard_map/ppermute | solution.py:496
  17.1 18.5 %collective-permute-start.1 = (bf16[96,1792]{1,0:T(8,128)(2,1)S(1)}, bf16[96,1792]{1,0:T(8,128)(2,1)S(1)}, u32[]{:S(2)}, u32[]{:S(2)}) collective-permute-start(bf16[96,1792]{1,0:T(8,128)(2,1)S(1)} %copy-done.47), channel_id=1, source_target_pairs={{0,4},{1,101},{2,6},{3,103},{4,32},{5,1},{6,34},{7,3},{8,12},{9,10... | collective-permute-start | bytes 1032200 | tf_op jit(solution)/shard_map/ppermute | solution.py:496
  24.8 15.2 %collective-permute-start.2 = (bf16[96,1792]{1,0:T(8,128)(2,1)S(1)}, bf16[96,1792]{1,0:T(8,128)(2,1)S(1)}, u32[]{:S(2)}, u32[]{:S(2)}) collective-permute-start(bf16[96,1792]{1,0:T(8,128)(2,1)S(1)} %copy-done.43), channel_id=1, source_target_pairs={{0,102},{1,103},{2,0},{3,1},{4,2},{5,3},{6,4},{7,5},{8,110},{9,111... | collective-permute-start | bytes 1032200 | tf_op jit(solution)/shard_map/ppermute | solution.py:496
  45.0 23.4 %all-to-all-start.1 = ((bf16[8,48,1792]{2,1,0:T(8,128)(2,1)}), bf16[8,48,1792]{2,1,0:T(8,128)(2,1)S(1)}, u32[]{:S(2)}, u32[]{:S(2)}) async-start(bf16[8,48,1792]{2,1,0:T(8,128)(2,1)} %bitcast.29), calls=%async_computation.1 | async-start | bytes 2752512 | tf_op jit(solution)/shard_map/all_to_all | solution.py:506
  49.7 23.7 %collective-permute-start.3 = (bf16[96,1792]{1,0:T(8,128)(2,1)}, bf16[96,1792]{1,0:T(8,128)(2,1)S(1)}, u32[]{:S(2)}, u32[]{:S(2)}) collective-permute-start(bf16[96,1792]{1,0:T(8,128)(2,1)} %get-tuple-element.59), channel_id=1, source_target_pairs={{0,2},{1,3},{2,4},{3,5},{4,6},{5,7},{6,32},{7,33},{8,10},{9,11},{1... | collective-permute-start | bytes 1032200 | tf_op jit(solution)/shard_map/ppermute | solution.py:496
  51.6 21.8 %collective-permute-start.4 = (bf16[96,1792]{1,0:T(8,128)(2,1)}, bf16[96,1792]{1,0:T(8,128)(2,1)}, u32[]{:S(2)}, u32[]{:S(2)}) collective-permute-start(bf16[96,1792]{1,0:T(8,128)(2,1)} %get-tuple-element.60), channel_id=1, source_target_pairs={{0,4},{1,101},{2,6},{3,103},{4,32},{5,1},{6,34},{7,3},{8,12},{9,10... | collective-permute-start | bytes 1032200 | tf_op jit(solution)/shard_map/ppermute | solution.py:496
  57.8 15.6 %collective-permute-start.5 = (bf16[96,1792]{1,0:T(8,128)(2,1)}, bf16[96,1792]{1,0:T(8,128)(2,1)}, u32[]{:S(2)}, u32[]{:S(2)}) collective-permute-start(bf16[96,1792]{1,0:T(8,128)(2,1)} %get-tuple-element.61), channel_id=1, source_target_pairs={{0,102},{1,103},{2,0},{3,1},{4,2},{5,3},{6,4},{7,5},{8,110},{9,111... | collective-permute-start | bytes 1032200 | tf_op jit(solution)/shard_map/ppermute | solution.py:496
  73.4 33.7 %all-to-all-start.2 = ((bf16[8,48,1792]{2,1,0:T(8,128)(2,1)}), bf16[8,48,1792]{2,1,0:T(8,128)(2,1)}, u32[]{:S(2)}, u32[]{:S(2)}) async-start(bf16[8,48,1792]{2,1,0:T(8,128)(2,1)} %bitcast.18), calls=%async_computation.2 | async-start | bytes 2752512 | tf_op jit(solution)/shard_map/all_to_all | solution.py:506
  88.8 15.1 %collective-permute-start.7 = (bf16[96,1792]{1,0:T(8,128)(2,1)S(1)}, bf16[96,1792]{1,0:T(8,128)(2,1)S(1)}, u32[]{:S(2)}, u32[]{:S(2)}) collective-permute-start(bf16[96,1792]{1,0:T(8,128)(2,1)S(1)} %get-tuple-element.70), channel_id=1, source_target_pairs={{0,100},{1,5},{2,102},{3,7},{4,0},{5,33},{6,2},{7,35},{8,108},{9,1... | collective-permute-start | bytes 1032200 | tf_op jit(solution)/shard_map/ppermute | solution.py:496
  90.7 16.5 %collective-permute-start.8 = (bf16[96,1792]{1,0:T(8,128)(2,1)S(1)}, bf16[96,1792]{1,0:T(8,128)(2,1)S(1)}, u32[]{:S(2)}, u32[]{:S(2)}) collective-permute-start(bf16[96,1792]{1,0:T(8,128)(2,1)S(1)} %get-tuple-element.71), channel_id=1, source_target_pairs={{0,2},{1,3},{2,4},{3,5},{4,6},{5,7},{6,32},{7,33},{8,10},{9,11},{1... | collective-permute-start | bytes 1032200 | tf_op jit(solution)/shard_map/ppermute | solution.py:496
  111.7 28.6 %all-to-all-start.3 = ((bf16[8,48,1792]{2,1,0:T(8,128)(2,1)}), bf16[8,48,1792]{2,1,0:T(8,128)(2,1)S(1)}, u32[]{:S(2)}, u32[]{:S(2)}) async-start(bf16[8,48,1792]{2,1,0:T(8,128)(2,1)} %bitcast.25), calls=%async_computation.3 | async-start | bytes 2752512 | tf_op jit(solution)/shard_map/all_to_all | solution.py:506
  120.1 15.3 %collective-permute-start.10 = (bf16[96,1792]{1,0:T(8,128)(2,1)S(1)}, bf16[96,1792]{1,0:T(8,128)(2,1)S(1)}, u32[]{:S(2)}, u32[]{:S(2)}) collective-permute-start(bf16[96,1792]{1,0:T(8,128)(2,1)S(1)} %copy-done.40), channel_id=1, source_target_pairs={{0,100},{1,5},{2,102},{3,7},{4,0},{5,33},{6,2},{7,35},{8,108},{9,1... | collective-permute-start | bytes 1032200 | tf_op jit(solution)/shard_map/ppermute | solution.py:496
  122.1 18.2 %collective-permute-start.11 = (bf16[96,1792]{1,0:T(8,128)(2,1)S(1)}, bf16[96,1792]{1,0:T(8,128)(2,1)S(1)}, u32[]{:S(2)}, u32[]{:S(2)}) collective-permute-start(bf16[96,1792]{1,0:T(8,128)(2,1)S(1)} %copy-done.37), channel_id=1, source_target_pairs={{0,2},{1,3},{2,4},{3,5},{4,6},{5,7},{6,32},{7,33},{8,10},{9,11},{1... | collective-permute-start | bytes 1032200 | tf_op jit(solution)/shard_map/ppermute | solution.py:496
  147.3 27.2 %all-to-all-start.4 = ((bf16[8,48,1792]{2,1,0:T(8,128)(2,1)}), bf16[8,48,1792]{2,1,0:T(8,128)(2,1)S(1)}, u32[]{:S(2)}, u32[]{:S(2)}) async-start(bf16[8,48,1792]{2,1,0:T(8,128)(2,1)} %bitcast.26), calls=%async_computation.4 | async-start | bytes 2752512 | tf_op jit(solution)/shard_map/all_to_all | solution.py:506
  157.7 16.8 %collective-permute-start.14 = (bf16[96,1792]{1,0:T(8,128)(2,1)S(1)}, bf16[96,1792]{1,0:T(8,128)(2,1)S(1)}, u32[]{:S(2)}, u32[]{:S(2)}) collective-permute-start(bf16[96,1792]{1,0:T(8,128)(2,1)S(1)} %copy-done.38), channel_id=1, source_target_pairs={{0,102},{1,103},{2,0},{3,1},{4,2},{5,3},{6,4},{7,5},{8,110},{9,111... | collective-permute-start | bytes 1032200 | tf_op jit(solution)/shard_map/ppermute | solution.py:496
  179.5 28.0 %all-to-all-start.5 = ((bf16[8,48,1792]{2,1,0:T(8,128)(2,1)}), bf16[8,48,1792]{2,1,0:T(8,128)(2,1)S(1)}, u32[]{:S(2)}, u32[]{:S(2)}) async-start(bf16[8,48,1792]{2,1,0:T(8,128)(2,1)} %bitcast.27), calls=%async_computation.5 | async-start | bytes 2752512 | tf_op jit(solution)/shard_map/all_to_all | solution.py:506
  191.4 16.1 %collective-permute-start.17 = (bf16[96,1792]{1,0:T(8,128)(2,1)S(1)}, bf16[96,1792]{1,0:T(8,128)(2,1)S(1)}, u32[]{:S(2)}, u32[]{:S(2)}) collective-permute-start(bf16[96,1792]{1,0:T(8,128)(2,1)S(1)} %copy-done.39), channel_id=1, source_target_pairs={{0,102},{1,103},{2,0},{3,1},{4,2},{5,3},{6,4},{7,5},{8,110},{9,111... | collective-permute-start | bytes 1032200 | tf_op jit(solution)/shard_map/ppermute | solution.py:496
  217.8 16.5 %collective-permute-start.18 = (bf16[272,896]{1,0:T(8,128)(2,1)}, bf16[272,896]{1,0:T(8,128)(2,1)S(1)}, u32[]{:S(2)}, u32[]{:S(2)}) collective-permute-start(bf16[272,896]{1,0:T(8,128)(2,1)} %get-tuple-element.89), channel_id=1, source_target_pairs={{0,256},{32,288},{64,320},{96,352},{128,384},{160,416},{192,448},{... | collective-permute-start | bytes 1462280 | tf_op jit(solution)/shard_map/ppermute | solution.py:476
  222.4 21.5 %collective-permute-start.19 = (bf16[272,896]{1,0:T(8,128)(2,1)}, bf16[272,896]{1,0:T(8,128)(2,1)S(1)}, u32[]{:S(2)}, u32[]{:S(2)}) collective-permute-start(bf16[272,896]{1,0:T(8,128)(2,1)} %get-tuple-element.90), channel_id=1, source_target_pairs={{0,128},{32,160},{64,192},{96,224},{128,256},{160,288},{192,320},{... | collective-permute-start | bytes 1462280 | tf_op jit(solution)/shard_map/ppermute | solution.py:476
  224.7 19.3 %collective-permute-start.20 = (bf16[272,896]{1,0:T(8,128)(2,1)}, bf16[272,896]{1,0:T(8,128)(2,1)S(1)}, u32[]{:S(2)}, u32[]{:S(2)}) collective-permute-start(bf16[272,896]{1,0:T(8,128)(2,1)} %get-tuple-element.91), channel_id=1, source_target_pairs={{0,384},{32,416},{64,448},{96,480},{128,0},{160,32},{192,64},{224,... | collective-permute-start | bytes 1462280 | tf_op jit(solution)/shard_map/ppermute | solution.py:476
  247.5 24.1 %collective-permute-start.21 = (bf16[240,256]{1,0:T(8,128)(2,1)}, bf16[240,256]{1,0:T(8,128)(2,1)S(1)}, u32[]{:S(2)}, u32[]{:S(2)}) collective-permute-start(bf16[240,256]{1,0:T(8,128)(2,1)} %get-tuple-element.93), channel_id=1, source_target_pairs={{0,64},{32,96},{64,0},{96,32},{128,192},{160,224},{192,128},{224,1... | collective-permute-start | bytes 368648 | tf_op jit(solution)/shard_map/ppermute | solution.py:476
  257.0 19.2 %collective-permute-start.22 = (bf16[240,256]{1,0:T(8,128)(2,1)}, bf16[240,256]{1,0:T(8,128)(2,1)S(1)}, u32[]{:S(2)}, u32[]{:S(2)}) collective-permute-start(bf16[240,256]{1,0:T(8,128)(2,1)} %get-tuple-element.94), channel_id=1, source_target_pairs={{0,32},{32,64},{64,96},{96,0},{128,160},{160,192},{192,224},{224,1... | collective-permute-start | bytes 368648 | tf_op jit(solution)/shard_map/ppermute | solution.py:476
  260.9 19.4 %collective-permute-start.23 = (bf16[240,256]{1,0:T(8,128)(2,1)}, bf16[240,256]{1,0:T(8,128)(2,1)S(1)}, u32[]{:S(2)}, u32[]{:S(2)}) collective-permute-start(bf16[240,256]{1,0:T(8,128)(2,1)} %get-tuple-element.95), channel_id=1, source_target_pairs={{0,96},{32,0},{64,32},{96,64},{128,224},{160,128},{192,160},{224,1... | collective-permute-start | bytes 368648 | tf_op jit(solution)/shard_map/ppermute | solution.py:476
  (55 other events, 384.9 us)

commit v8 on v6

--- a/solution.py
+++ b/solution.py
@@ -10,7 +10,7 @@
 SLOTS = 6
 PAIR = 2 * SLOTS
 SIDE = 4
-STEPS = ((0, 0), (1, 1), (2, -2), (-1, -1))
+STEPS = ((0, 0), (2, -2), (1, 1), (-1, -1))
 BF = jnp.bfloat16
 F32 = jnp.float32
 VMEM = 56 * 1024 * 1024
@@ -67,7 +67,8 @@
     in_a, in_b = piece, piece - blocks
     xc = jnp.where(first, in_a & 7, lax.shift_right_logical(in_b, 2))
     k = jnp.where(first, lax.shift_right_logical(in_a, 3), in_b & 3)
-    block = lax.shift_right_logical(xc, 1) * (2 * SIDE) + ((zl + k) & 3) * 2 + (xc & 1)
+    up = jnp.where((k == 1) | (k == 2), 3 - k, k)
+    block = lax.shift_right_logical(xc, 1) * (2 * SIDE) + ((zl + up) & 3) * 2 + (xc & 1)
     left = place < SLOTS
     slot = place - jnp.where(left, 0, SLOTS) + jnp.where(first, 0, SLOTS)
     expand = lax.broadcasted_iota(jnp.int32, (rows, blocks), 1) == block
@@ -486,8 +487,7 @@
 
 
 def along_z(arrays, back=False):
-    moved = {k: shift_z(arrays[k], STEPS[k], back) for k in (2, 1, 3)}
-    return [arrays[0], moved[1], moved[2], moved[3]]
+    return [arrays[0]] + [shift_z(arrays[k], STEPS[k], back) for k in range(1, SIDE)]
 
 
 def shift_z(x, steps, back):

time: 283 us -> 275 us (0.972)
  waiting for transfers between devices: 99.3 us -> 79 us
  starting transfers between devices: 120 us -> 130 us
    ppermute x18, waiting for transfers between devices: 39 us -> 25.8 us  [shift_z(): return lax.ppermute(x, ('rows', 'lat'), pairs)]
    ppermute x18, starting transfers between devices: 56 us -> 65.4 us  [shift_z(): return lax.ppermute(x, ('rows', 'lat'), pairs)]
    all_to_all x6, waiting for transfers between devices: 29.2 us -> 22.9 us  [over_x(): lax.all_to_all(x.reshape(members, shape[0] // members, shape[1]), 'lat',...]
  transfers between devices with their start and end apart: 30 -> 30, of which waited for: 19 -> 16; matrix products, arithmetic and copies ran while one was open for 0% -> 0% of each run, Pallas kernels for 5% -> 6%
where the time goes in v8:
time: 275 us; the launch traced here: 271 us
  starting transfers between devices  130 us (47%)
  waiting for transfers between devices  79 us (29%)
  Pallas kernels  47.1 us (17%)
  local copies, waits for them, and re-layouts  13.4 us (5%)
    ppermute x18, starting transfers between devices, shift_z(): return lax.ppermute(x, ('rows', 'lat'), pairs)  65.4 us
    all_to_all x6, starting transfers between devices, over_x(): lax.all_to_all(x.reshape(members, shape[0] // members, shape[1]), 'lat',...  37.8 us
    ppermute x6, waiting for transfers between devices, share_pieces(): got.append(lax.ppermute(pieces[k], 'rows', pairs))  30.3 us
    ppermute x6, starting transfers between devices, share_pieces(): got.append(lax.ppermute(pieces[k], 'rows', pairs))  26.9 us
    ppermute x18, waiting for transfers between devices, shift_z(): return lax.ppermute(x, ('rows', 'lat'), pairs)  25.8 us
    all_to_all x6, waiting for transfers between devices, over_x(): lax.all_to_all(x.reshape(members, shape[0] // members, shape[1]), 'lat',...  22.9 us
    pallas_call x6, Pallas kernels, swap_pieces(): pl.pallas_call(functools.partial(swap_kernel, merge), in_specs=[ANY] * le...  17.2 us
    unnamed x98, local copies, waits for them, and re-layouts  12.8 us
  transfers between devices with their start and end apart: 30, of which 16 were waited for; matrix products, arithmetic and copies ran while one was open for 0% of the time, Pallas kernels for 6%

profile of v8, /device:TPU:1, one launch (start us, length us, event | category | flops | bytes accessed | tf_op | source)
XLA Modules:
  0.0 271.0 jit_solution(15410884367643170918)
XLA Ops:
  4.7 10.5 %all-to-all-start = ((bf16[8,48,1792]{2,1,0:T(8,128)(2,1)}), bf16[8,48,1792]{2,1,0:T(8,128)(2,1)S(1)}, u32[]{:S(2)}, u32[]{:S(2)}) async-start(bf16[8,48,1792]{2,1,0:T(8,128)(2,1)} %bitcast.29), calls=%async_computation | async-start | bytes 2752512 | tf_op jit(solution)/shard_map/all_to_all | solution.py:514
  15.2 7.0 %collective-permute-start = (bf16[96,1792]{1,0:T(8,128)(2,1)S(1)}, bf16[96,1792]{1,0:T(8,128)(2,1)S(1)}, u32[]{:S(2)}, u32[]{:S(2)}) collective-permute-start(bf16[96,1792]{1,0:T(8,128)(2,1)S(1)} %copy-done.48), channel_id=1, source_target_pairs={{0,4},{1,101},{2,6},{3,103},{4,32},{5,1},{6,34},{7,3},{8,12},{9,10... | collective-permute-start | bytes 1032200 | tf_op jit(solution)/shard_map/ppermute | solution.py:504
  28.7 5.1 %all-to-all-done = bf16[8,48,1792]{2,1,0:T(8,128)(2,1)S(1)} async-done(((bf16[8,48,1792]{2,1,0:T(8,128)(2,1)}), bf16[8,48,1792]{2,1,0:T(8,128)(2,1)S(1)}, u32[]{:S(2)}, u32[]{:S(2)}) %all-to-all-start) | async-done | bytes 1376288 | tf_op jit(solution)/shard_map/all_to_all | solution.py:514
  41.6 5.4 %all-to-all-start.1 = ((bf16[8,48,1792]{2,1,0:T(8,128)(2,1)}), bf16[8,48,1792]{2,1,0:T(8,128)(2,1)S(1)}, u32[]{:S(2)}, u32[]{:S(2)}) async-start(bf16[8,48,1792]{2,1,0:T(8,128)(2,1)} %bitcast.27), calls=%async_computation.1 | async-start | bytes 2752512 | tf_op jit(solution)/shard_map/all_to_all | solution.py:514
  47.0 6.1 %collective-permute-start.3 = (bf16[96,1792]{1,0:T(8,128)(2,1)}, bf16[96,1792]{1,0:T(8,128)(2,1)S(1)}, u32[]{:S(2)}, u32[]{:S(2)}) collective-permute-start(bf16[96,1792]{1,0:T(8,128)(2,1)} %get-tuple-element.87), channel_id=1, source_target_pairs={{0,4},{1,101},{2,6},{3,103},{4,32},{5,1},{6,34},{7,3},{8,12},{9,10... | collective-permute-start | bytes 1032200 | tf_op jit(solution)/shard_map/ppermute | solution.py:504
  59.6 6.0 %all-to-all-done.1 = bf16[8,48,1792]{2,1,0:T(8,128)(2,1)S(1)} async-done(((bf16[8,48,1792]{2,1,0:T(8,128)(2,1)}), bf16[8,48,1792]{2,1,0:T(8,128)(2,1)S(1)}, u32[]{:S(2)}, u32[]{:S(2)}) %all-to-all-start.1) | async-done | bytes 1376288 | tf_op jit(solution)/shard_map/all_to_all | solution.py:514
  70.6 5.2 %all-to-all-start.2 = ((bf16[8,48,1792]{2,1,0:T(8,128)(2,1)}), bf16[8,48,1792]{2,1,0:T(8,128)(2,1)}, u32[]{:S(2)}, u32[]{:S(2)}) async-start(bf16[8,48,1792]{2,1,0:T(8,128)(2,1)} %bitcast.18), calls=%async_computation.2 | async-start | bytes 2752512 | tf_op jit(solution)/shard_map/all_to_all | solution.py:514
  75.8 4.2 %encode_decode.3 = (bf16[96,1792]{1,0:T(8,128)(2,1)S(1)}, bf16[96,1792]{1,0:T(8,128)(2,1)}, bf16[96,1792]{1,0:T(8,128)(2,1)S(1)}, bf16[96,1792]{1,0:T(8,128)(2,1)S(1)}, f32[384,128]{1,0:T(8,128)S(1)}) custom-call(bf16[96,1792]{1,0:T(8,128)(2,1)S(1)} %copy-done.4, bf16[96,1792]{1,0:T(8,128)(2,1)S(1)} %collective-permute-done.3.refs_1_, ...), custom_call_target="tpu_custom_call" | custom-call | tf_op jit(solution)/shard_map/encode_decode/pallas_call | solution.py:252
  83.3 5.7 %collective-permute-start.7 = (bf16[96,1792]{1,0:T(8,128)(2,1)S(1)}, bf16[96,1792]{1,0:T(8,128)(2,1)S(1)}, u32[]{:S(2)}, u32[]{:S(2)}) collective-permute-start(bf16[96,1792]{1,0:T(8,128)(2,1)S(1)} %get-tuple-element.103), channel_id=1, source_target_pairs={{0,102},{1,103},{2,0},{3,1},{4,2},{5,3},{6,4},{7,5},{8,110},{9,111... | collective-permute-start | bytes 1032200 | tf_op jit(solution)/shard_map/ppermute | solution.py:504
  105.6 7.0 %all-to-all-start.3 = ((bf16[8,48,1792]{2,1,0:T(8,128)(2,1)}), bf16[8,48,1792]{2,1,0:T(8,128)(2,1)S(1)}, u32[]{:S(2)}, u32[]{:S(2)}) async-start(bf16[8,48,1792]{2,1,0:T(8,128)(2,1)} %bitcast.23), calls=%async_computation.3 | async-start | bytes 2752512 | tf_op jit(solution)/shard_map/all_to_all | solution.py:514
  114.6 5.3 %collective-permute-start.10 = (bf16[96,1792]{1,0:T(8,128)(2,1)S(1)}, bf16[96,1792]{1,0:T(8,128)(2,1)S(1)}, u32[]{:S(2)}, u32[]{:S(2)}) collective-permute-start(bf16[96,1792]{1,0:T(8,128)(2,1)S(1)} %copy-done.40), channel_id=1, source_target_pairs={{0,102},{1,103},{2,0},{3,1},{4,2},{5,3},{6,4},{7,5},{8,110},{9,111... | collective-permute-start | bytes 1032200 | tf_op jit(solution)/shard_map/ppermute | solution.py:504
  124.1 7.2 %collective-permute-done.10.refs_2_ = bf16[96,1792]{1,0:T(8,128)(2,1)S(1)} collective-permute-done((bf16[96,1792]{1,0:T(8,128)(2,1)S(1)}, bf16[96,1792]{1,0:T(8,128)(2,1)S(1)}, u32[]{:S(2)}, u32[]{:S(2)}) %collective-permute-start.10) | collective-permute-done | bytes 344096 | tf_op jit(solution)/shard_map/ppermute | solution.py:504
  134.9 5.8 %error_rows.1 = (bf16[96,1792]{1,0:T(8,128)(2,1)}, bf16[96,1792]{1,0:T(8,128)(2,1)}, bf16[96,1792]{1,0:T(8,128)(2,1)}, bf16[96,1792]{1,0:T(8,128)(2,1)}, bf16[384,1792]{1,0:T(8,128)(2,1)}) custom-call(s32[2,128]{1,0:T(2,128)} %bitcast.31, f32[1,3584]{1,0:T(1,128)} %broadcast_in_dim.7.bias_ref, bf16[128,3584]{1,0:T(8,128)(2,1)} %act_ref.3, ...), custom_call_target="tpu_custom_call" | custom-call | tf_op jit(solution)/shard_map/error_rows/pallas_call | solution.py:308
  140.7 5.2 %all-to-all-start.4 = ((bf16[8,48,1792]{2,1,0:T(8,128)(2,1)}), bf16[8,48,1792]{2,1,0:T(8,128)(2,1)S(1)}, u32[]{:S(2)}, u32[]{:S(2)}) async-start(bf16[8,48,1792]{2,1,0:T(8,128)(2,1)} %bitcast.28), calls=%async_computation.4 | async-start | bytes 2752512 | tf_op jit(solution)/shard_map/all_to_all | solution.py:514
  156.4 8.2 %all-to-all-done.4 = bf16[8,48,1792]{2,1,0:T(8,128)(2,1)S(1)} async-done(((bf16[8,48,1792]{2,1,0:T(8,128)(2,1)}), bf16[8,48,1792]{2,1,0:T(8,128)(2,1)S(1)}, u32[]{:S(2)}, u32[]{:S(2)}) %all-to-all-start.4) | async-done | bytes 1376288 | tf_op jit(solution)/shard_map/all_to_all | solution.py:514
  172.6 4.5 %all-to-all-start.5 = ((bf16[8,48,1792]{2,1,0:T(8,128)(2,1)}), bf16[8,48,1792]{2,1,0:T(8,128)(2,1)S(1)}, u32[]{:S(2)}, u32[]{:S(2)}) async-start(bf16[8,48,1792]{2,1,0:T(8,128)(2,1)} %bitcast.24), calls=%async_computation.5 | async-start | bytes 2752512 | tf_op jit(solution)/shard_map/all_to_all | solution.py:514
  190.7 4.9 %collective-permute-done.16.refs_7_ = bf16[96,1792]{1,0:T(8,128)(2,1)S(1)} collective-permute-done((bf16[96,1792]{1,0:T(8,128)(2,1)S(1)}, bf16[96,1792]{1,0:T(8,128)(2,1)S(1)}, u32[]{:S(2)}, u32[]{:S(2)}) %collective-permute-start.16) | collective-permute-done | bytes 344096 | tf_op jit(solution)/shard_map/ppermute | solution.py:504
  198.7 9.1 %gradients.1 = (bf16[272,896]{1,0:T(8,128)(2,1)}, bf16[272,896]{1,0:T(8,128)(2,1)}, bf16[272,896]{1,0:T(8,128)(2,1)}, bf16[272,896]{1,0:T(8,128)(2,1)}) custom-call(f32[384,128]{1,0:T(8,128)} %copy-done.7, f32[384,128]{1,0:T(8,128)} %copy-done.8, bf16[128,3584]{1,0:T(8,128)(2,1)} %dec_ref.1, bf16[96,1792]{1,0:T(8,128)(2,1)} %get-tuple-element.91.refs_0_, ...), custom_call_target="tpu_custom_call" | custom-call | tf_op jit(solution)/shard_map/gradients/pallas_call | solution.py:396
  207.8 4.8 %collective-permute-start.18 = (bf16[272,896]{1,0:T(8,128)(2,1)}, bf16[272,896]{1,0:T(8,128)(2,1)S(1)}, u32[]{:S(2)}, u32[]{:S(2)}) collective-permute-start(bf16[272,896]{1,0:T(8,128)(2,1)} %get-tuple-element.131), channel_id=1, source_target_pairs={{0,256},{32,288},{64,320},{96,352},{128,384},{160,416},{192,448},{... | collective-permute-start | bytes 1462280 | tf_op jit(solution)/shard_map/ppermute | solution.py:485
  222.7 12.2 %collective-permute-done.19.refs_2_ = bf16[272,896]{1,0:T(8,128)(2,1)S(1)} collective-permute-done((bf16[272,896]{1,0:T(8,128)(2,1)}, bf16[272,896]{1,0:T(8,128)(2,1)S(1)}, u32[]{:S(2)}, u32[]{:S(2)}) %collective-permute-start.19) | collective-permute-done | bytes 487456 | tf_op jit(solution)/shard_map/ppermute | solution.py:485
  238.5 5.1 %collective-permute-start.21 = (bf16[240,256]{1,0:T(8,128)(2,1)}, bf16[240,256]{1,0:T(8,128)(2,1)S(1)}, u32[]{:S(2)}, u32[]{:S(2)}) collective-permute-start(bf16[240,256]{1,0:T(8,128)(2,1)} %get-tuple-element.135), channel_id=1, source_target_pairs={{0,64},{32,96},{64,0},{96,32},{128,192},{160,224},{192,128},{224,1... | collective-permute-start | bytes 368648 | tf_op jit(solution)/shard_map/ppermute | solution.py:485
  243.6 8.5 %collective-permute-start.22 = (bf16[240,256]{1,0:T(8,128)(2,1)}, bf16[240,256]{1,0:T(8,128)(2,1)S(1)}, u32[]{:S(2)}, u32[]{:S(2)}) collective-permute-start(bf16[240,256]{1,0:T(8,128)(2,1)} %get-tuple-element.136), channel_id=1, source_target_pairs={{0,32},{32,64},{64,96},{96,0},{128,160},{160,192},{192,224},{224,1... | collective-permute-start | bytes 368648 | tf_op jit(solution)/shard_map/ppermute | solution.py:485
  254.1 5.1 %collective-permute-done.22.refs_2_ = bf16[240,256]{1,0:T(8,128)(2,1)S(1)} collective-permute-done((bf16[240,256]{1,0:T(8,128)(2,1)}, bf16[240,256]{1,0:T(8,128)(2,1)S(1)}, u32[]{:S(2)}, u32[]{:S(2)}) %collective-permute-start.22) | collective-permute-done | bytes 122912 | tf_op jit(solution)/shard_map/ppermute | solution.py:485
  259.1 9.4 %collective-permute-done.23.refs_3_ = bf16[240,256]{1,0:T(8,128)(2,1)S(1)} collective-permute-done((bf16[240,256]{1,0:T(8,128)(2,1)}, bf16[240,256]{1,0:T(8,128)(2,1)S(1)}, u32[]{:S(2)}, u32[]{:S(2)}) %collective-permute-start.23) | collective-permute-done | bytes 122912 | tf_op jit(solution)/shard_map/ppermute | solution.py:485
  (148 shorter events, 112.2 us)
Async XLA Ops:
  4.7 29.1 %all-to-all-start = ((bf16[8,48,1792]{2,1,0:T(8,128)(2,1)}), bf16[8,48,1792]{2,1,0:T(8,128)(2,1)S(1)}, u32[]{:S(2)}, u32[]{:S(2)}) async-start(bf16[8,48,1792]{2,1,0:T(8,128)(2,1)} %bitcast.29), calls=%async_computation | async-start | bytes 2752512 | tf_op jit(solution)/shard_map/all_to_all | solution.py:514
  15.2 22.6 %collective-permute-start = (bf16[96,1792]{1,0:T(8,128)(2,1)S(1)}, bf16[96,1792]{1,0:T(8,128)(2,1)S(1)}, u32[]{:S(2)}, u32[]{:S(2)}) collective-permute-start(bf16[96,1792]{1,0:T(8,128)(2,1)S(1)} %copy-done.48), channel_id=1, source_target_pairs={{0,4},{1,101},{2,6},{3,103},{4,32},{5,1},{6,34},{7,3},{8,12},{9,10... | collective-permute-start | bytes 1032200 | tf_op jit(solution)/shard_map/ppermute | solution.py:504
  22.2 15.6 %collective-permute-start.1 = (bf16[96,1792]{1,0:T(8,128)(2,1)S(1)}, bf16[96,1792]{1,0:T(8,128)(2,1)S(1)}, u32[]{:S(2)}, u32[]{:S(2)}) collective-permute-start(bf16[96,1792]{1,0:T(8,128)(2,1)S(1)} %copy-done.47), channel_id=1, source_target_pairs={{0,2},{1,3},{2,4},{3,5},{4,6},{5,7},{6,32},{7,33},{8,10},{9,11},{1... | collective-permute-start | bytes 1032200 | tf_op jit(solution)/shard_map/ppermute | solution.py:504
  41.6 24.0 %all-to-all-start.1 = ((bf16[8,48,1792]{2,1,0:T(8,128)(2,1)}), bf16[8,48,1792]{2,1,0:T(8,128)(2,1)S(1)}, u32[]{:S(2)}, u32[]{:S(2)}) async-start(bf16[8,48,1792]{2,1,0:T(8,128)(2,1)} %bitcast.27), calls=%async_computation.1 | async-start | bytes 2752512 | tf_op jit(solution)/shard_map/all_to_all | solution.py:514
  47.0 23.6 %collective-permute-start.3 = (bf16[96,1792]{1,0:T(8,128)(2,1)}, bf16[96,1792]{1,0:T(8,128)(2,1)S(1)}, u32[]{:S(2)}, u32[]{:S(2)}) collective-permute-start(bf16[96,1792]{1,0:T(8,128)(2,1)} %get-tuple-element.87), channel_id=1, source_target_pairs={{0,4},{1,101},{2,6},{3,103},{4,32},{5,1},{6,34},{7,3},{8,12},{9,10... | collective-permute-start | bytes 1032200 | tf_op jit(solution)/shard_map/ppermute | solution.py:504
  53.1 17.5 %collective-permute-start.4 = (bf16[96,1792]{1,0:T(8,128)(2,1)}, bf16[96,1792]{1,0:T(8,128)(2,1)}, u32[]{:S(2)}, u32[]{:S(2)}) collective-permute-start(bf16[96,1792]{1,0:T(8,128)(2,1)} %get-tuple-element.88), channel_id=1, source_target_pairs={{0,2},{1,3},{2,4},{3,5},{4,6},{5,7},{6,32},{7,33},{8,10},{9,11},{1... | collective-permute-start | bytes 1032200 | tf_op jit(solution)/shard_map/ppermute | solution.py:504
  55.7 14.8 %collective-permute-start.5 = (bf16[96,1792]{1,0:T(8,128)(2,1)}, bf16[96,1792]{1,0:T(8,128)(2,1)}, u32[]{:S(2)}, u32[]{:S(2)}) collective-permute-start(bf16[96,1792]{1,0:T(8,128)(2,1)} %get-tuple-element.89), channel_id=1, source_target_pairs={{0,102},{1,103},{2,0},{3,1},{4,2},{5,3},{6,4},{7,5},{8,110},{9,111... | collective-permute-start | bytes 1032200 | tf_op jit(solution)/shard_map/ppermute | solution.py:504
  70.6 23.9 %all-to-all-start.2 = ((bf16[8,48,1792]{2,1,0:T(8,128)(2,1)}), bf16[8,48,1792]{2,1,0:T(8,128)(2,1)}, u32[]{:S(2)}, u32[]{:S(2)}) async-start(bf16[8,48,1792]{2,1,0:T(8,128)(2,1)} %bitcast.18), calls=%async_computation.2 | async-start | bytes 2752512 | tf_op jit(solution)/shard_map/all_to_all | solution.py:514
  81.4 15.9 %collective-permute-start.6 = (bf16[96,1792]{1,0:T(8,128)(2,1)}, bf16[96,1792]{1,0:T(8,128)(2,1)S(1)}, u32[]{:S(2)}, u32[]{:S(2)}) collective-permute-start(bf16[96,1792]{1,0:T(8,128)(2,1)} %get-tuple-element.102), channel_id=1, source_target_pairs={{0,100},{1,5},{2,102},{3,7},{4,0},{5,33},{6,2},{7,35},{8,108},{9,1... | collective-permute-start | bytes 1032200 | tf_op jit(solution)/shard_map/ppermute | solution.py:504
  83.3 17.1 %collective-permute-start.7 = (bf16[96,1792]{1,0:T(8,128)(2,1)S(1)}, bf16[96,1792]{1,0:T(8,128)(2,1)S(1)}, u32[]{:S(2)}, u32[]{:S(2)}) collective-permute-start(bf16[96,1792]{1,0:T(8,128)(2,1)S(1)} %get-tuple-element.103), channel_id=1, source_target_pairs={{0,102},{1,103},{2,0},{3,1},{4,2},{5,3},{6,4},{7,5},{8,110},{9,111... | collective-permute-start | bytes 1032200 | tf_op jit(solution)/shard_map/ppermute | solution.py:504
  105.6 28.1 %all-to-all-start.3 = ((bf16[8,48,1792]{2,1,0:T(8,128)(2,1)}), bf16[8,48,1792]{2,1,0:T(8,128)(2,1)S(1)}, u32[]{:S(2)}, u32[]{:S(2)}) async-start(bf16[8,48,1792]{2,1,0:T(8,128)(2,1)} %bitcast.23), calls=%async_computation.3 | async-start | bytes 2752512 | tf_op jit(solution)/shard_map/all_to_all | solution.py:514
  114.6 16.8 %collective-permute-start.10 = (bf16[96,1792]{1,0:T(8,128)(2,1)S(1)}, bf16[96,1792]{1,0:T(8,128)(2,1)S(1)}, u32[]{:S(2)}, u32[]{:S(2)}) collective-permute-start(bf16[96,1792]{1,0:T(8,128)(2,1)S(1)} %copy-done.40), channel_id=1, source_target_pairs={{0,102},{1,103},{2,0},{3,1},{4,2},{5,3},{6,4},{7,5},{8,110},{9,111... | collective-permute-start | bytes 1032200 | tf_op jit(solution)/shard_map/ppermute | solution.py:504
  140.7 23.9 %all-to-all-start.4 = ((bf16[8,48,1792]{2,1,0:T(8,128)(2,1)}), bf16[8,48,1792]{2,1,0:T(8,128)(2,1)S(1)}, u32[]{:S(2)}, u32[]{:S(2)}) async-start(bf16[8,48,1792]{2,1,0:T(8,128)(2,1)} %bitcast.28), calls=%async_computation.4 | async-start | bytes 2752512 | tf_op jit(solution)/shard_map/all_to_all | solution.py:514
  146.0 22.6 %collective-permute-start.12 = (bf16[96,1792]{1,0:T(8,128)(2,1)S(1)}, bf16[96,1792]{1,0:T(8,128)(2,1)S(1)}, u32[]{:S(2)}, u32[]{:S(2)}) collective-permute-start(bf16[96,1792]{1,0:T(8,128)(2,1)S(1)} %copy-done.46), channel_id=1, source_target_pairs={{0,4},{1,101},{2,6},{3,103},{4,32},{5,1},{6,34},{7,3},{8,12},{9,10... | collective-permute-start | bytes 1032200 | tf_op jit(solution)/shard_map/ppermute | solution.py:504
  149.9 18.7 %collective-permute-start.13 = (bf16[96,1792]{1,0:T(8,128)(2,1)S(1)}, bf16[96,1792]{1,0:T(8,128)(2,1)S(1)}, u32[]{:S(2)}, u32[]{:S(2)}) collective-permute-start(bf16[96,1792]{1,0:T(8,128)(2,1)S(1)} %copy-done.42), channel_id=1, source_target_pairs={{0,2},{1,3},{2,4},{3,5},{4,6},{5,7},{6,32},{7,33},{8,10},{9,11},{1... | collective-permute-start | bytes 1032200 | tf_op jit(solution)/shard_map/ppermute | solution.py:504
  153.8 14.8 %collective-permute-start.14 = (bf16[96,1792]{1,0:T(8,128)(2,1)S(1)}, bf16[96,1792]{1,0:T(8,128)(2,1)S(1)}, u32[]{:S(2)}, u32[]{:S(2)}) collective-permute-start(bf16[96,1792]{1,0:T(8,128)(2,1)S(1)} %copy-done.39), channel_id=1, source_target_pairs={{0,102},{1,103},{2,0},{3,1},{4,2},{5,3},{6,4},{7,5},{8,110},{9,111... | collective-permute-start | bytes 1032200 | tf_op jit(solution)/shard_map/ppermute | solution.py:504
  172.6 24.9 %all-to-all-start.5 = ((bf16[8,48,1792]{2,1,0:T(8,128)(2,1)}), bf16[8,48,1792]{2,1,0:T(8,128)(2,1)S(1)}, u32[]{:S(2)}, u32[]{:S(2)}) async-start(bf16[8,48,1792]{2,1,0:T(8,128)(2,1)} %bitcast.24), calls=%async_computation.5 | async-start | bytes 2752512 | tf_op jit(solution)/shard_map/all_to_all | solution.py:514
  180.9 14.7 %collective-permute-start.16 = (bf16[96,1792]{1,0:T(8,128)(2,1)S(1)}, bf16[96,1792]{1,0:T(8,128)(2,1)S(1)}, u32[]{:S(2)}, u32[]{:S(2)}) collective-permute-start(bf16[96,1792]{1,0:T(8,128)(2,1)S(1)} %copy-done.41), channel_id=1, source_target_pairs={{0,2},{1,3},{2,4},{3,5},{4,6},{5,7},{6,32},{7,33},{8,10},{9,11},{1... | collective-permute-start | bytes 1032200 | tf_op jit(solution)/shard_map/ppermute | solution.py:504
  207.8 14.9 %collective-permute-start.18 = (bf16[272,896]{1,0:T(8,128)(2,1)}, bf16[272,896]{1,0:T(8,128)(2,1)S(1)}, u32[]{:S(2)}, u32[]{:S(2)}) collective-permute-start(bf16[272,896]{1,0:T(8,128)(2,1)} %get-tuple-element.131), channel_id=1, source_target_pairs={{0,256},{32,288},{64,320},{96,352},{128,384},{160,416},{192,448},{... | collective-permute-start | bytes 1462280 | tf_op jit(solution)/shard_map/ppermute | solution.py:485
  212.6 22.3 %collective-permute-start.19 = (bf16[272,896]{1,0:T(8,128)(2,1)}, bf16[272,896]{1,0:T(8,128)(2,1)S(1)}, u32[]{:S(2)}, u32[]{:S(2)}) collective-permute-start(bf16[272,896]{1,0:T(8,128)(2,1)} %get-tuple-element.132), channel_id=1, source_target_pairs={{0,128},{32,160},{64,192},{96,224},{128,256},{160,288},{192,320},{... | collective-permute-start | bytes 1462280 | tf_op jit(solution)/shard_map/ppermute | solution.py:485
  214.9 20.0 %collective-permute-start.20 = (bf16[272,896]{1,0:T(8,128)(2,1)}, bf16[272,896]{1,0:T(8,128)(2,1)S(1)}, u32[]{:S(2)}, u32[]{:S(2)}) collective-permute-start(bf16[272,896]{1,0:T(8,128)(2,1)} %get-tuple-element.133), channel_id=1, source_target_pairs={{0,384},{32,416},{64,448},{96,480},{128,0},{160,32},{192,64},{224,... | collective-permute-start | bytes 1462280 | tf_op jit(solution)/shard_map/ppermute | solution.py:485
  238.5 15.6 %collective-permute-start.21 = (bf16[240,256]{1,0:T(8,128)(2,1)}, bf16[240,256]{1,0:T(8,128)(2,1)S(1)}, u32[]{:S(2)}, u32[]{:S(2)}) collective-permute-start(bf16[240,256]{1,0:T(8,128)(2,1)} %get-tuple-element.135), channel_id=1, source_target_pairs={{0,64},{32,96},{64,0},{96,32},{128,192},{160,224},{192,128},{224,1... | collective-permute-start | bytes 368648 | tf_op jit(solution)/shard_map/ppermute | solution.py:485
  243.6 15.6 %collective-permute-start.22 = (bf16[240,256]{1,0:T(8,128)(2,1)}, bf16[240,256]{1,0:T(8,128)(2,1)S(1)}, u32[]{:S(2)}, u32[]{:S(2)}) collective-permute-start(bf16[240,256]{1,0:T(8,128)(2,1)} %get-tuple-element.136), channel_id=1, source_target_pairs={{0,32},{32,64},{64,96},{96,0},{128,160},{160,192},{192,224},{224,1... | collective-permute-start | bytes 368648 | tf_op jit(solution)/shard_map/ppermute | solution.py:485
  252.1 16.4 %collective-permute-start.23 = (bf16[240,256]{1,0:T(8,128)(2,1)}, bf16[240,256]{1,0:T(8,128)(2,1)S(1)}, u32[]{:S(2)}, u32[]{:S(2)}) collective-permute-start(bf16[240,256]{1,0:T(8,128)(2,1)} %get-tuple-element.137), channel_id=1, source_target_pairs={{0,96},{32,0},{64,32},{96,64},{128,224},{160,128},{192,160},{224,1... | collective-permute-start | bytes 368648 | tf_op jit(solution)/shard_map/ppermute | solution.py:485
  (55 other events, 372.6 us)
